TPU v7x, 32 devices: a whole 2x2x4 slice. The times are simulated.
32 devices in a mesh: sec: 2 (over core), grp: 4 (over y, x), tp: 4 (over z).
Axes of the slice: x: 2, y: 2, z: 4, core: 2. Of those that a mesh axis runs over, the one named last changes fastest.
Arguments:
- resid_in: bfloat16 [192, 6144], P(('sec', 'grp'), 'tp'), may hold values from -6 to 6
- queries: bfloat16 [192, 6144], P(('sec', 'grp'), 'tp'), may hold values from -20 to 20
- new_kv: bfloat16 [192, 2, 1024], P(('sec', 'grp'), None, 'tp'), may hold values from -6 to 6
- cache: bfloat16 [192, 2, 256, 1024], P(('sec', 'grp'), None, None, 'tp'), may hold values from -20 to 20
- lengths: int32 [192], P(('sec', 'grp')), may hold values from 16 to 256, as said below
- norm_gain: float32 [6144], replicated, may hold values from 0.25 to 1.75
- router: float32 [6144, 8], replicated, may hold values from -0.078125 to 0.078125
- route_ids: int32 [192, 2], P(('sec', 'grp')), may hold values from 0 to 7, all different within a row; in each aligned block of 6 rows (0 to 5, 6 to 11, ...) at most 3 rows name the same one
- w_gate: bfloat16 [8, 6144, 8192], P('grp', None, ('sec', 'tp')), may hold values from -0.078125 to 0.078125
- w_up: bfloat16 [8, 6144, 8192], P('grp', None, ('sec', 'tp')), may hold values from -0.078125 to 0.078125
- w_down: bfloat16 [8, 8192, 6144], P('grp', ('sec', 'tp')), may hold values from -0.0625 to 0.0625
Outputs:
- resid_out: bfloat16 [192, 6144], P(('sec', 'grp'), 'tp')
Inputs may be any that keep to these rules, and one draw needn't show every extreme that they name: `route_ids`: each row names 2 different experts; in each aligned block of 6 rows, the rows of one micro-batch of one device, no expert is named by more than 3 rows. `lengths`: some sequence has all 256 slots valid.
All inputs are finite; a program needn't handle non-finite values.
Results may differ from a plain program's by a relative error of at most 0.006.
Values may be sent and summed in bfloat16 or wider, within the bound.
No kernel may reach another device: no remote copies, remote signals or barrier semaphores. Data moves between devices by JAX's collectives and lax.ppermute only.
A program may use at most 192 MiB of HBM per device.

v0:
```python
import math

import jax
import jax.numpy as jnp
from jax import lax
from jax.sharding import PartitionSpec as P

HEAD_DIM = 128
MB = 4
CAP = 3


epsilon = 1e-05


def attend(query_rows, cached_keys, cached_values, new_key, new_value, seq_lengths):
    factor = 1.0 / math.sqrt(query_rows.shape[-1])
    scores = (
        jnp.einsum("nkgd,nckd->nkgc", query_rows, cached_keys, preferred_element_type=jnp.float32)
        * factor
    )
    fresh_score = (
        jnp.einsum("nkgd,nkd->nkg", query_rows, new_key, preferred_element_type=jnp.float32)
        * factor
    )
    valid_mask = (jnp.arange(cached_keys.shape[1])[None, :] < seq_lengths[:, None])[
        :, None, None, :
    ]
    masked = jnp.where(valid_mask, scores, -jnp.inf)
    largest = jnp.maximum(jnp.max(masked, axis=-1), fresh_score)
    raw_weights = jnp.where(valid_mask, jnp.exp(masked - largest[..., None]), 0.0)
    fresh_weight = jnp.exp(fresh_score - largest)
    denominator = jnp.sum(raw_weights, axis=-1) + fresh_weight
    probabilities = (raw_weights / denominator[..., None]).astype(jnp.bfloat16)
    fresh_prob = (fresh_weight / denominator).astype(jnp.bfloat16)
    output = jnp.einsum(
        "nkgc,nckd->nkgd", probabilities, cached_values, preferred_element_type=jnp.float32
    )
    output = (
        output
        + fresh_prob.astype(jnp.float32)[..., None] * new_value.astype(jnp.float32)[:, :, None, :]
    )
    return output.astype(jnp.bfloat16).reshape(query_rows.shape[0], -1)


def expert_work(received, w_gate, w_up, w_down):
    gate_value = jnp.einsum(
        "jlmcd,ldf->jlmcf", received, w_gate, preferred_element_type=jnp.float32
    )
    up_value = jnp.einsum("jlmcd,ldf->jlmcf", received, w_up, preferred_element_type=jnp.float32)
    activated = (jax.nn.silu(gate_value) * up_value).astype(jnp.bfloat16)
    partial_out = jnp.einsum(
        "jlmcf,lfd->jlmcd", activated, w_down, preferred_element_type=jnp.float32
    )
    return lax.all_to_all(partial_out, ("sec", "grp"), split_axis=0, concat_axis=0, tiled=True)


def on_device(
    resid_in, queries, new_kv, cache, lengths, norm_gain, router, route_ids, w_gate, w_up, w_down
):
    sequences, part_cols = resid_in.shape
    owners = lax.axis_size("grp")
    peer_count = lax.axis_size("sec") * owners
    held_blocks = w_gate.shape[0]
    expert_count = router.shape[1]
    split_count = max(1, owners // expert_count)
    batch_rows = sequences // MB
    kv_local = new_kv.shape[2] // HEAD_DIM
    group_size = queries.shape[1] // (kv_local * HEAD_DIM)
    cache_len = cache.shape[2]
    slot_ids = jnp.arange(peer_count * held_blocks, dtype=jnp.int32)
    slot_expert = (
        slot_ids // held_blocks % owners * held_blocks + slot_ids % held_blocks
    ) // split_count
    cap_slots = jnp.arange(CAP, dtype=jnp.int32)
    expert_ids = jnp.arange(expert_count, dtype=jnp.int32)
    query_q = queries.reshape(sequences, kv_local, group_size, HEAD_DIM)
    fresh_q = new_kv.reshape(sequences, 2, kv_local, HEAD_DIM)
    cache_q = cache.reshape(sequences, 2, cache_len, kv_local, HEAD_DIM)
    attended = attend(query_q, cache_q[:, 0], cache_q[:, 1], fresh_q[:, 0], fresh_q[:, 1], lengths)
    hidden_part = resid_in.astype(jnp.float32) + attended.astype(jnp.float32)
    attn_all, resid_all = (
        lax.all_gather(attended, "tp", axis=1, tiled=True),
        lax.all_gather(resid_in, "tp", axis=1, tiled=True),
    )
    hidden = resid_all.astype(jnp.float32) + attn_all.astype(jnp.float32)
    row_scaling = lax.rsqrt(jnp.mean(hidden * hidden, axis=1, keepdims=True) + epsilon)
    packed_tokens = (hidden * row_scaling * norm_gain).astype(jnp.bfloat16)
    logits = jnp.dot(packed_tokens.astype(jnp.float32), router, precision=lax.Precision.HIGHEST)
    onehot = (route_ids[:, :, None] == expert_ids[None, None, :]).astype(jnp.float32)
    picked = jnp.sum(onehot * logits[:, None, :], axis=2)
    first_mix = 1.0 / (1.0 + jnp.exp(picked[:, 1] - picked[:, 0]))
    second_mix = 1.0 / (1.0 + jnp.exp(picked[:, 0] - picked[:, 1]))
    mixes = jnp.stack([first_mix, second_mix], axis=1).reshape(MB, batch_rows, 2)
    route_blocks = route_ids.reshape(MB, batch_rows, 2)
    slot_equality = route_blocks[None] == slot_expert[:, None, None, None]
    slot_hits = jnp.sum(slot_equality.astype(jnp.int32), axis=3)
    position = jnp.cumsum(slot_hits, axis=2) - 1
    in_place = position[:, :, None, :] == cap_slots[None, None, :, None]
    expert_position = ((slot_hits[:, :, None, :] == 1) & in_place).astype(jnp.bfloat16)
    token_blocks = packed_tokens.reshape(MB, batch_rows, packed_tokens.shape[1])
    dispatch_buffer = jnp.einsum(
        "smcr,mru->smcu", expert_position, token_blocks, preferred_element_type=jnp.float32
    )
    dispatch_buffer = dispatch_buffer.astype(jnp.bfloat16).reshape(
        peer_count, held_blocks, MB, CAP, packed_tokens.shape[1]
    )
    weight_slot = jnp.sum(mixes[None] * slot_equality.astype(jnp.float32), axis=3)
    slot_gate_weight = weight_slot[:, :, None, :] * in_place.astype(jnp.float32)
    combined_return = expert_work(
        lax.all_to_all(dispatch_buffer, ("sec", "grp"), split_axis=0, concat_axis=0, tiled=True),
        w_gate,
        w_up,
        w_down,
    )
    combined_return = combined_return.reshape(
        peer_count * held_blocks, MB, CAP, combined_return.shape[4]
    )
    combined = jnp.einsum(
        "smcr,smcw->mrw", slot_gate_weight, combined_return, precision=lax.Precision.HIGHEST
    )
    combined = combined.reshape(sequences, combined.shape[2])
    mixed = lax.psum_scatter(combined, "tp", scatter_dimension=1, tiled=True)
    return (hidden_part + mixed).astype(jnp.bfloat16)


def solution(mesh):
    return jax.shard_map(
        on_device,
        mesh=mesh,
        in_specs=(
            P(("sec", "grp"), "tp"),
            P(("sec", "grp"), "tp"),
            P(("sec", "grp"), None, "tp"),
            P(("sec", "grp"), None, None, "tp"),
            P(("sec", "grp")),
            P(),
            P(),
            P(("sec", "grp"), None),
            P("grp", None, ("sec", "tp")),
            P("grp", None, ("sec", "tp")),
            P("grp", ("sec", "tp"), None),
        ),
        out_specs=P(("sec", "grp"), "tp"),
        check_vma=False,
    )
```

profile of v0, /device:TPU:0, one launch (start us, length us, event | category | flops | bytes accessed | tf_op | source)
XLA Modules:
  0.0 234.2 jit_solution(18297986253377737287)
XLA Ops:
  6.5 0.0 copy-start
  6.5 0.8 eq.55
  7.3 0.1 copy.75
  7.4 0.1 fusion.34
  7.6 0.7 iota_compare_fusion.2
  8.3 0.8 reshape.112
  9.1 1.0 reshape.110
  10.1 15.9 %all_gather.6 = bf16[24,6144]{1,0:T(8,128)(2,1)S(1)} all-gather(bf16[24,1536]{1,0:T(8,128)(2,1)} %param.11), channel_id=1, replica_groups=mesh['sec'=2,'grp'=4,'tp'=4] {'tp'}, dimensions={1}, use_global_device_ids=true | all-gather | bytes 368640 | tf_op jit(solution)/shard_map/all_gather | solution.py:84
  26.0 8.7 %copy.71 = bf16[24,2,256,256]{2,3,1,0:T(8,128)(2,1)} copy(bf16[24,2,256,256]{3,2,1,0:T(8,128)(2,1)} %param.14) | data formatting | bytes 12582912 | tf_op args[3]
  34.6 0.2 fusion.40
  34.8 2.5 %fusion.52 = (f32[24,2,6]{2,1,0:T(2,128)S(1)}, f32[24,2,6,256]{3,2,1,0:T(8,128)S(1)}) fusion(bf16[24,2,6,128]{3,2,1,0:T(8,128)(2,1)S(1)} %reshape.110, bf16[24,2,256,2,128]{2,4,3,1,0:T(8,128)(2,1)} %bitcast.88, pred[24,256]{1,0:T(8,128)(4,1)S(1)} %iota_compare_fusion.2), kind=kOutput, calls=%fused_computation.86 | convolution fusion | flops 19095264 | bytes 3521664 | tf_op jit(solution)/shard_map/nkgd,nckd->nkgc/dot_general | solution.py:19
  37.3 0.0 copy-start.2
  37.4 0.2 fusion.26
  37.7 2.9 %fusion.18 = bf16[24,2,6,128]{3,2,1,0:T(8,128)(2,1)S(1)} fusion(bf16[24,2,256,2,128]{2,4,3,1,0:T(8,128)(2,1)} %bitcast.89, f32[24,2,6,256]{3,2,1,0:T(8,128)S(1)} %get-tuple-element.12, f32[24,2,6]{2,1,0:T(2,128)S(1)} %get-tuple-element.8, f32[24,2,6]{2,1,0:T(2,128)S(1)} %multiply_maximum_fusion, pred[24,256]{1,0:T(8,128)(4,1)S(1)} %iota_compare_fusion.2, ...), kind=kOutput, calls=%fused_computation.20 | convolution fusion | flops 19279872 | bytes 3548544 | tf_op jit(solution)/shard_map/nkgc,nckd->nkgd/dot_general | solution.py:36
  40.5 0.1 reshape.113
  40.6 14.9 %all_gather.7 = bf16[24,6144]{1,0:T(8,128)(2,1)S(1)} all-gather(bf16[24,1536]{1,0:T(8,128)(2,1)S(1)} %reshape.113), channel_id=1, replica_groups=mesh['sec'=2,'grp'=4,'tp'=4] {'tp'}, dimensions={1}, use_global_device_ids=true | all-gather | bytes 368640 | tf_op jit(solution)/shard_map/all_gather | solution.py:83
  55.5 0.2 multiply_reduce_fusion
  55.8 0.0 copy-done.2
  55.8 0.1 multiply_convert_fusion
  55.9 0.1 reshape.121
  56.0 0.8 fusion.9
  56.8 1.8 copy.94
  58.7 32.6 %all_to_all.10 = bf16[8,2,4,3,6144]{4,2,3,1,0:T(4,128)(2,1)S(1)} all-to-all(bf16[8,2,4,3,6144]{4,2,3,1,0:T(4,128)(2,1)S(1)} %bitcast.90), channel_id=1, replica_groups=mesh['sec'=2,'grp'=4,'tp'=4] {'sec','grp'}, dimensions={0} | all-to-all | bytes 4718592 | tf_op jit(solution)/shard_map/all_to_all | solution.py:111
  91.2 14.8 %fusion.2 = f32[2,8,4,3,1024]{4,2,3,1,0:T(4,128)S(1)} fusion(bf16[2,6144,1024]{2,1,0:T(8,128)(2,1)} %param.20, bf16[8,2,4,3,6144]{4,2,3,1,0:T(4,128)(2,1)S(1)} %all_to_all.10), kind=kOutput, calls=%fused_computation.2 | convolution fusion | flops 2415919104 | bytes 28311552 | tf_op jit(solution)/shard_map/jlmcd,ldf->jlmcf/dot_general | solution.py:50
  106.0 15.0 %fusion.4 = f32[2,8,4,3,1024]{4,2,3,1,0:T(4,128)S(1)} fusion(bf16[2,6144,1024]{2,1,0:T(8,128)(2,1)} %param.19, bf16[8,2,4,3,6144]{4,2,3,1,0:T(4,128)(2,1)S(1)} %all_to_all.10), kind=kOutput, calls=%fused_computation.4 | convolution fusion | flops 2415919104 | bytes 28311552 | tf_op jit(solution)/shard_map/jlmcd,ldf->jlmcf/dot_general | solution.py:47
  121.0 10.7 %fusion.6 = f32[8,2,4,3,6144]{4,0,3,2,1:T(8,128)S(1)} fusion(bf16[2,1024,6144]{2,1,0:T(8,128)(2,1)} %param.21, f32[2,8,4,3,1024]{4,2,3,1,0:T(4,128)S(1)} %fusion.2, f32[2,8,4,3,1024]{4,2,3,1,0:T(4,128)S(1)} %fusion.4), kind=kOutput, calls=%fused_computation.6 | convolution fusion | flops 2417098752 | bytes 31457280 | tf_op jit(solution)/shard_map/jlmcf,lfd->jlmcd/dot_general | solution.py:52
  131.7 5.2 %copy.85 = f32[8,2,4,3,6144]{4,2,3,1,0:T(4,128)} copy(f32[8,2,4,3,6144]{4,0,3,2,1:T(8,128)S(1)} %fusion.6) | data formatting | bytes 9437184 | tf_op jit(solution)/shard_map/jlmcf,lfd->jlmcd/transpose | solution.py:52
  136.9 0.0 copy-start.3
  136.9 4.7 %all-to-all-start.1 = ((f32[8,2,4,3,6144]{4,2,3,1,0:T(4,128)}), f32[8,2,4,3,6144]{4,2,3,1,0:T(4,128)}, u32[]{:S(2)}, u32[]{:S(2)}) async-start(f32[8,2,4,3,6144]{4,2,3,1,0:T(4,128)} %copy.85), calls=%async_computation.1 | async-start | bytes 9437184 | tf_op jit(solution)/shard_map/all_to_all | solution.py:55
  141.6 0.0 copy-start.1
  141.6 0.0 reduce-scatter.2.cloned.1.call-start
  141.7 0.0 copy-done
  141.7 0.4 fusion.53
  142.1 0.0 copy-done.3
  142.1 0.1 stack.9
  142.2 0.1 stack.10
  142.3 0.1 copy.77
  142.4 0.1 fusion.35
  142.5 53.3 %all-to-all-done.1 = f32[8,2,4,3,6144]{4,2,3,1,0:T(4,128)} async-done(((f32[8,2,4,3,6144]{4,2,3,1,0:T(4,128)}), f32[8,2,4,3,6144]{4,2,3,1,0:T(4,128)}, u32[]{:S(2)}, u32[]{:S(2)}) %all-to-all-start.1) | async-done | bytes 4718624 | tf_op jit(solution)/shard_map/all_to_all | solution.py:55
  195.8 7.5 %convolution_bitcast_fusion = f32[4,6,6144]{2,1,0:T(8,128)S(1)} fusion(f32[16,4,3,6144]{3,1,2,0:T(4,128)} %bitcast.21, f32[16,4,6]{0,2,1:T(8,128)S(1)} %copy.78, s32[16,4,6]{0,2,1:T(8,128)S(1)} %copy.76), kind=kOutput, calls=%fused_computation.9 | convolution fusion | flops 84936960 | bytes 5311488 | tf_op jit(solution)/shard_map/smcr,smcw->mrw/dot_general | solution.py:119
  203.4 0.9 reshape.117
  204.2 0.0 reduce-scatter.2.cloned.1.call-update
  204.3 21.6 %reduce-scatter.2.cloned.1.call-done = f32[24,1536]{1,0:T(8,128)} async-done(((f32[24,6144]{1,0:T(8,128)}), f32[24,1536]{1,0:T(8,128)}) %reduce-scatter.2.cloned.1.call-update) | async-done | bytes 147472 | tf_op jit(solution)/shard_map/reduce_scatter | solution.py:123
  225.8 0.0 copy-done.1
  225.8 1.6 add_convert_fusion
  (13 shorter events, 0.2 us)
Async XLA Ops:
  6.5 135.2 %copy-start = (f32[6144,8]{0,1:T(8,128)S(1)}, f32[6144,8]{0,1:T(8,128)}, u32[]{:S(2)}) copy-start(f32[6144,8]{0,1:T(8,128)} %param.17) | copy-start | bytes 589828
  37.3 18.4 %copy-start.2 = (f32[6144]{0:T(1024)S(1)}, f32[6144]{0:T(1024)}, u32[]{:S(2)}) copy-start(f32[6144]{0:T(1024)} %param.16) | copy-start | bytes 73732
  136.9 5.2 %copy-start.3 = (s32[24,2]{0,1:T(2,128)S(1)}, s32[24,2]{0,1:T(2,128)}, u32[]{:S(2)}) copy-start(s32[24,2]{0,1:T(2,128)} %param.18) | copy-start | bytes 580
  136.9 58.9 %all-to-all-start.1 = ((f32[8,2,4,3,6144]{4,2,3,1,0:T(4,128)}), f32[8,2,4,3,6144]{4,2,3,1,0:T(4,128)}, u32[]{:S(2)}, u32[]{:S(2)}) async-start(f32[8,2,4,3,6144]{4,2,3,1,0:T(4,128)} %copy.85), calls=%async_computation.1 | async-start | bytes 9437184 | tf_op jit(solution)/shard_map/all_to_all | solution.py:55
  141.6 84.2 %copy-start.1 = (bf16[24,1536]{1,0:T(8,128)(2,1)S(1)}, bf16[24,1536]{1,0:T(8,128)(2,1)}, u32[]{:S(2)}) copy-start(bf16[24,1536]{1,0:T(8,128)(2,1)} %param.11) | copy-start | bytes 221188
  141.6 84.2 %reduce-scatter.2.cloned.1.call-start = ((), (), s32[]{:S(2)}) async-start(), calls=%async_computation.3 | async-start | bytes 737280 | tf_op jit(solution)/shard_map/reduce_scatter | solution.py:123
Sparse Core Ops, SparseCore 0:
  204.4 21.3 reduce-scatter.1
where the time goes:
time: 235 us; the launch traced here: 234 us
  waiting for transfers between devices  74.9 us (32%)
  blocking collectives  63.3 us (27%)
  matrix products  54.7 us (23%)
  local copies, waits for them, and re-layouts  19.7 us (8%)
  between operations  13.6 us (6%)
  starting transfers between devices  4.76 us (2%)
  other arithmetic  3.28 us (1%)
    all_to_all x1, waiting for transfers between devices, expert_work(): lax.all_to_all(partial_out, ('sec', 'grp'), split_axis=0, concat_axis=0,...  53.3 us
    all_to_all x1, blocking collectives, on_device(): lax.all_to_all(dispatch_buffer, ('sec', 'grp'), split_axis=0, concat_axis...  32.6 us
    reduce_scatter x1, waiting for transfers between devices, on_device(): mixed = lax.psum_scatter(combined, 'tp', scatter_dimension=1, tiled=True)  21.6 us
    all_gather x1, blocking collectives, on_device(): lax.all_gather(resid_in, 'tp', axis=1, tiled=True)  15.9 us
    dot_general x1, matrix products, expert_work(): jnp.einsum('jlmcd,ldf->jlmcf', received, w_gate, preferred_element_type=j...  15 us
    all_gather x1, blocking collectives, on_device(): lax.all_gather(attended, 'tp', axis=1, tiled=True)  14.9 us
    dot_general x1, matrix products, expert_work(): jnp.einsum('jlmcd,ldf->jlmcf', received, w_up, preferred_element_type=jnp...  14.8 us
    dot_general x1, matrix products, expert_work(): jnp.einsum('jlmcf,lfd->jlmcd', activated, w_down, preferred_element_type=...  10.7 us
  transfers between devices with their start and end apart: 2, of which 2 were waited for; matrix products, arithmetic and copies ran while one was open for 0% of the time, Pallas kernels for 0%

commit v1 on v0

v1 whole, which is shorter than its diff:
```python
import functools
import math

import jax
import jax.numpy as jnp
from jax import lax
from jax.experimental import pallas as pl
from jax.experimental.pallas import tpu as pltpu
from jax.sharding import PartitionSpec as P

HEAD_DIM = 128
ROWS_STEP = 8
MIB = 1 << 20

epsilon = 1e-05


def largest_divisor(total, choices):
    return next(c for c in choices if total % c == 0)


def attend_kernel(lengths_ref, query_ref, new_ref, resid_ref, cache_ref, attended_ref, hidden_ref, *, kv_local, group):
    step = pl.program_id(0)
    rows = ROWS_STEP
    cache_len = cache_ref.shape[2]
    stacked = group * rows
    factor = 1.0 / math.sqrt(HEAD_DIM)
    row_of = lax.broadcasted_iota(jnp.int32, (stacked, 1), 0) % rows
    length_col = jnp.zeros((stacked, 1), jnp.int32)
    for n in range(rows):
        length_col = jnp.where(row_of == n, lengths_ref[step * rows + n], length_col)
    valid = lax.broadcasted_iota(jnp.int32, (stacked, cache_len), 1) < length_col
    for head in range(kv_local):
        lanes = pl.ds(head * HEAD_DIM, HEAD_DIM)
        first = head * group
        query = jnp.concatenate(
            [
                query_ref[:, pl.ds((first + g) * HEAD_DIM, HEAD_DIM)].astype(jnp.float32)
                for g in range(group)
            ],
            axis=0,
        )
        query_bf = query.astype(jnp.bfloat16)
        new_key = new_ref[:, 0, lanes].astype(jnp.float32)
        new_value = new_ref[:, 1, lanes].astype(jnp.float32)
        scores = jnp.zeros((stacked, cache_len), jnp.float32)
        for n in range(rows):
            full = lax.dot_general(
                query_bf,
                cache_ref[n, 0, :, lanes],
                (((1,), (1,)), ((), ())),
                preferred_element_type=jnp.float32,
            )
            scores = jnp.where(row_of == n, full, scores)
        scores = jnp.where(valid, scores * factor, -jnp.inf)
        fresh = (
            jnp.sum(query * jnp.concatenate([new_key] * group, axis=0), axis=1, keepdims=True)
            * factor
        )
        largest = jnp.maximum(jnp.max(scores, axis=1, keepdims=True), fresh)
        weights = jnp.exp(scores - largest)
        fresh_weight = jnp.exp(fresh - largest)
        denominator = jnp.sum(weights, axis=1, keepdims=True) + fresh_weight
        probabilities = (weights / denominator).astype(jnp.bfloat16)
        fresh_prob = (fresh_weight / denominator).astype(jnp.bfloat16).astype(jnp.float32)
        output = jnp.zeros((stacked, HEAD_DIM), jnp.float32)
        for n in range(rows):
            full = jnp.dot(
                probabilities, cache_ref[n, 1, :, lanes], preferred_element_type=jnp.float32
            )
            output = jnp.where(row_of == n, full, output)
        output = output + fresh_prob * jnp.concatenate([new_value] * group, axis=0)
        attended = output.astype(jnp.bfloat16)
        for g in range(group):
            columns = pl.ds((first + g) * HEAD_DIM, HEAD_DIM)
            piece = output[g * rows : (g + 1) * rows].astype(jnp.bfloat16)
            attended_ref[:, columns] = piece
            hidden_ref[:, columns] = (
                resid_ref[:, columns].astype(jnp.float32) + piece.astype(jnp.float32)
            ).astype(jnp.bfloat16)


def attend(lengths, queries, new_kv, resid_in, cache):
    sequences, part_cols = queries.shape
    cache_len, kv_cols = cache.shape[2:]
    kv_local = kv_cols // HEAD_DIM
    group = part_cols // kv_cols
    rows = ROWS_STEP
    flat = pl.BlockSpec((rows, part_cols), lambda i, _: (i, 0))
    return pl.pallas_call(
        functools.partial(attend_kernel, kv_local=kv_local, group=group),
        grid_spec=pltpu.PrefetchScalarGridSpec(
            num_scalar_prefetch=1,
            grid=(sequences // rows,),
            in_specs=[
                flat,
                pl.BlockSpec((rows, 2, kv_cols), lambda i, _: (i, 0, 0)),
                flat,
                pl.BlockSpec((rows, 2, cache_len, kv_cols), lambda i, _: (i, 0, 0, 0)),
            ],
            out_specs=[flat, flat],
        ),
        out_shape=[jax.ShapeDtypeStruct((sequences, part_cols), jnp.bfloat16)] * 2,
        compiler_params=pltpu.CompilerParams(vmem_limit_bytes=16 * MIB),
        name="attend",
    )(lengths, queries, new_kv, resid_in, cache)


def experts_kernel(
    place_ref, gain_ref, router_ref, gate_hbm, up_hbm, down_hbm, *rest, pieces, rows, part_cols, tps, split, kb, nb, depth_in, depth_out
):
    piece_refs = rest[:pieces]
    out_refs = rest[pieces : 2 * pieces]
    gate_buf, up_buf, down_buf, acc_gate, acc_up, act_ref, in_sem, out_sem = rest[2 * pieces :]
    held, width, ff = gate_hbm.shape
    tokens = pieces * rows
    experts = router_ref.shape[0]
    grp, tp = place_ref[0], place_ref[1]
    per_part = part_cols // kb
    in_steps = width // kb
    out_per_part = part_cols // nb
    out_steps = width // nb

    def offset_in(k):
        return pl.multiple_of((k // per_part ^ tp) * part_cols + k % per_part * kb, kb)

    def offset_out(k):
        return pl.multiple_of((k // out_per_part ^ tp) * part_cols + k % out_per_part * nb, nb)

    def in_copies(k):
        slot = lax.rem(k, depth_in)
        source = pl.ds(offset_in(k), kb)
        found = []
        for e in range(held):
            found.append(
                pltpu.make_async_copy(gate_hbm.at[e, source], gate_buf.at[slot, e], in_sem.at[slot, 2 * e])
            )
            found.append(
                pltpu.make_async_copy(up_hbm.at[e, source], up_buf.at[slot, e], in_sem.at[slot, 2 * e + 1])
            )
        return found

    def out_copies(k):
        slot = lax.rem(k, depth_out)
        source = pl.ds(offset_out(k), nb)
        return [
            pltpu.make_async_copy(down_hbm.at[e, :, source], down_buf.at[slot, pl.ds(e * ff, ff)], out_sem.at[slot, e])
            for e in range(held)
        ]

    for k in range(min(depth_in, in_steps)):
        for copy in in_copies(k):
            copy.start()
    for k in range(min(depth_out, out_steps)):
        for copy in out_copies(k):
            copy.start()
    acc_gate[...] = jnp.zeros_like(acc_gate)
    acc_up[...] = jnp.zeros_like(acc_up)

    def in_body(k, carry):
        squares, logits = carry
        local = pl.ds(pl.multiple_of(k * kb, kb), kb)
        there = pl.ds(offset_in(k), kb)
        slot = lax.rem(k, depth_in)
        raw = jnp.concatenate([ref[:, local].astype(jnp.float32) for ref in piece_refs], axis=0)
        squares = squares + jnp.sum(raw * raw, axis=1, keepdims=True)
        scaled = (raw * gain_ref[:, there]).astype(jnp.bfloat16)
        router = router_ref[:, there]
        high = router.astype(jnp.bfloat16)
        low = (router - high.astype(jnp.float32)).astype(jnp.bfloat16)
        for part in (high, low):
            logits = logits + lax.dot_general(
                scaled, part, (((1,), (1,)), ((), ())), preferred_element_type=jnp.float32
            )
        for copy in in_copies(k):
            copy.wait()
        for e in range(held):
            acc_gate[e] += jnp.dot(scaled, gate_buf[slot, e], preferred_element_type=jnp.float32)
            acc_up[e] += jnp.dot(scaled, up_buf[slot, e], preferred_element_type=jnp.float32)

        @pl.when(k + depth_in < in_steps)
        def _():
            for copy in in_copies(k + depth_in):
                copy.start()

        return squares, logits

    squares, logits = lax.fori_loop(
        0,
        in_steps,
        in_body,
        (jnp.zeros((tokens, 1), jnp.float32), jnp.zeros((tokens, experts), jnp.float32)),
    )
    row_scale = lax.rsqrt(squares / width + epsilon)
    logits = logits * row_scale
    ids = jnp.concatenate([ref[:, pl.ds(width, 128)].astype(jnp.float32) for ref in piece_refs], axis=0)
    names = [ids[:, k : k + 1].astype(jnp.int32) for k in range(2)]
    lane = lax.broadcasted_iota(jnp.int32, (tokens, experts), 1)
    picked = [jnp.sum(jnp.where(lane == name, logits, 0.0), axis=1, keepdims=True) for name in names]
    mixes = [
        1.0 / (1.0 + jnp.exp(picked[1] - picked[0])),
        1.0 / (1.0 + jnp.exp(picked[0] - picked[1])),
    ]
    for e in range(held):
        expert = (grp * held + e) // split
        share = sum(jnp.where(name == expert, mix, 0.0) for name, mix in zip(names, mixes))
        gate = acc_gate[e] * row_scale
        up = acc_up[e] * (row_scale * share)
        act_ref[:, pl.ds(e * ff, ff)] = (gate / (1.0 + jnp.exp(-gate)) * up).astype(jnp.bfloat16)

    def out_body(k, carry):
        slot = lax.rem(k, depth_out)
        for copy in out_copies(k):
            copy.wait()
        partial = jnp.dot(act_ref[...], down_buf[slot], preferred_element_type=jnp.float32)
        columns = pl.ds(pl.multiple_of(k * nb, nb), nb)
        for p, ref in enumerate(out_refs):
            ref[:, columns] = partial[p * rows : (p + 1) * rows].astype(jnp.bfloat16)

        @pl.when(k + depth_out < out_steps)
        def _():
            for copy in out_copies(k + depth_out):
                copy.start()

        return carry

    lax.fori_loop(0, out_steps, out_body, 0)


def run_experts(place, norm_gain, router, w_gate, w_up, w_down, pieces, part_cols, tps, split):
    held, width, ff = w_gate.shape
    rows = pieces[0].shape[0]
    count = len(pieces)
    tokens = rows * count
    kb = largest_divisor(part_cols, (512, 384, 256, 128))
    nb = largest_divisor(part_cols, (512, 384, 256, 128))
    depth_in, depth_out = 3, 4
    vmem = pl.BlockSpec(memory_space=pltpu.VMEM)
    hbm = pl.BlockSpec(memory_space=pltpu.HBM)
    return pl.pallas_call(
        functools.partial(
            experts_kernel,
            pieces=count,
            rows=rows,
            part_cols=part_cols,
            tps=tps,
            split=split,
            kb=kb,
            nb=nb,
            depth_in=depth_in,
            depth_out=depth_out,
        ),
        in_specs=[pl.BlockSpec(memory_space=pltpu.SMEM), vmem, vmem, hbm, hbm, hbm] + [vmem] * count,
        out_specs=[vmem] * count,
        out_shape=[jax.ShapeDtypeStruct((rows, width), jnp.bfloat16)] * count,
        scratch_shapes=[
            pltpu.VMEM((depth_in, held, kb, ff), jnp.bfloat16),
            pltpu.VMEM((depth_in, held, kb, ff), jnp.bfloat16),
            pltpu.VMEM((depth_out, held * ff, nb), jnp.bfloat16),
            pltpu.VMEM((held, tokens, ff), jnp.float32),
            pltpu.VMEM((held, tokens, ff), jnp.float32),
            pltpu.VMEM((tokens, held * ff), jnp.bfloat16),
            pltpu.SemaphoreType.DMA((depth_in, 2 * held)),
            pltpu.SemaphoreType.DMA((depth_out, held)),
        ],
        compiler_params=pltpu.CompilerParams(vmem_limit_bytes=52 * MIB),
        name="experts",
    )(place, norm_gain.reshape(1, width), router.T, w_gate, w_up, w_down, *pieces)


def swap(array, axis, offset):
    size = lax.axis_size(axis)
    return lax.ppermute(array, axis, [(i, i ^ offset) for i in range(size)])


def on_device(
    resid_in, queries, new_kv, cache, lengths, norm_gain, router, route_ids, w_gate, w_up, w_down
):
    sequences, part_cols = resid_in.shape
    tps, grps, secs = lax.axis_size("tp"), lax.axis_size("grp"), lax.axis_size("sec")
    held = w_gate.shape[0]
    split = max(1, grps * held // router.shape[1])
    place = jnp.stack([lax.axis_index("grp"), lax.axis_index("tp")]).astype(jnp.int32)

    attended, hidden = attend(lengths, queries, new_kv, resid_in, cache)

    ids = jnp.pad(route_ids.astype(jnp.bfloat16), ((0, 0), (0, 128 - route_ids.shape[1])))
    columns = [hidden] + [swap(hidden, "tp", j) for j in range(1, tps)]
    own = jnp.concatenate(columns + [ids], axis=1)
    near = [own] + [swap(own, "grp", d) for d in range(1, grps)]
    pieces = near + [swap(piece, "sec", s) for s in range(1, secs) for piece in near]

    partial = run_experts(
        place, norm_gain, router, w_gate, w_up, w_down, pieces, part_cols, tps, split
    )

    def total(arrays):
        result = arrays[0].astype(jnp.float32)
        for array in arrays[1:]:
            result = result + array.astype(jnp.float32)
        return result

    sums = []
    for d in range(grps):
        terms = [partial[d]] + [swap(partial[s * grps + d], "sec", s) for s in range(1, secs)]
        sums.append(total(terms).astype(jnp.bfloat16))
    rows_sum = total([sums[0]] + [swap(sums[d], "grp", d) for d in range(1, grps)])
    parts = [
        rows_sum[:, j * part_cols : (j + 1) * part_cols].astype(jnp.bfloat16) for j in range(tps)
    ]
    mixed = total([parts[0]] + [swap(parts[j], "tp", j) for j in range(1, tps)])
    hidden_part = resid_in.astype(jnp.float32) + attended.astype(jnp.float32)
    return (hidden_part + mixed).astype(jnp.bfloat16)


def solution(mesh):
    return jax.shard_map(
        on_device,
        mesh=mesh,
        in_specs=(
            P(("sec", "grp"), "tp"),
            P(("sec", "grp"), "tp"),
            P(("sec", "grp"), None, "tp"),
            P(("sec", "grp"), None, None, "tp"),
            P(("sec", "grp")),
            P(),
            P(),
            P(("sec", "grp"), None),
            P("grp", None, ("sec", "tp")),
            P("grp", None, ("sec", "tp")),
            P("grp", ("sec", "tp"), None),
        ),
        out_specs=P(("sec", "grp"), "tp"),
        check_vma=False,
    )
```

time: 235 us -> 102 us (0.43)
  blocking collectives: 63.3 us -> 0 us
  matrix products: 54.7 us -> 0 us
  waiting for transfers between devices: 74.9 us -> 37.7 us
  Pallas kernels: 0 us -> 35.4 us
  starting transfers between devices: 4.76 us -> 18.4 us
  between operations: 13.6 us -> 0.14 us
  local copies, waits for them, and re-layouts: 19.7 us -> 8.46 us
    dot_general x9 -> x0, matrix products: 54.7 us -> none  [the longest x1 15 us: expert_work(): jnp.einsum('jlmcd,ldf->jlmcf', received, w_gate, preferred_element_type=j...]
    all_to_all x1 -> x0, waiting for transfers between devices: 53.3 us -> none  [expert_work(): lax.all_to_all(partial_out, ('sec', 'grp'), split_axis=0, concat_axis=0,...]
    ppermute x0 -> x20, waiting for transfers between devices: none -> 37.7 us  [swap(): return lax.ppermute(array, axis, [(i, i ^ offset) for i in range(size)])]
    pallas_call x0 -> x2, Pallas kernels: none -> 35.4 us  [the longest x1 31.3 us: run_experts(): pl.pallas_call(functools.partial(experts_kernel, pieces=count, rows=rows,...]
    all_to_all x1 -> x0, blocking collectives: 32.6 us -> none  [on_device(): lax.all_to_all(dispatch_buffer, ('sec', 'grp'), split_axis=0, concat_axis...]
    all_gather x2 -> x0, blocking collectives: 30.7 us -> none  [the longest x1 15.9 us: on_device(): lax.all_gather(resid_in, 'tp', axis=1, tiled=True)]
    reduce_scatter x1 -> x0, waiting for transfers between devices: 21.6 us -> none  [on_device(): mixed = lax.psum_scatter(combined, 'tp', scatter_dimension=1, tiled=True)]
    ppermute x0 -> x20, starting transfers between devices: none -> 18.4 us  [swap(): return lax.ppermute(array, axis, [(i, i ^ offset) for i in range(size)])]
  transfers between devices with their start and end apart: 2 -> 20, of which waited for: 2 -> 13; matrix products, arithmetic and copies ran while one was open for 0% -> 1% of each run, Pallas kernels for 0% -> 0%
where the time goes in v1:
time: 102 us
  waiting for transfers between devices  37.7 us (37%)
  Pallas kernels  35.4 us (35%)
  starting transfers between devices  18.4 us (18%)
  local copies, waits for them, and re-layouts  8.46 us (8%)
  other arithmetic  1.85 us (2%)
    ppermute x20, waiting for transfers between devices, swap(): return lax.ppermute(array, axis, [(i, i ^ offset) for i in range(size)])  37.7 us
    pallas_call x1, Pallas kernels, run_experts(): pl.pallas_call(functools.partial(experts_kernel, pieces=count, rows=rows,...  31.3 us
    ppermute x20, starting transfers between devices, swap(): return lax.ppermute(array, axis, [(i, i ^ offset) for i in range(size)])  18.4 us
    unnamed x36, local copies, waits for them, and re-layouts  8.33 us
    pallas_call x1, Pallas kernels, attend(): pl.pallas_call(functools.partial(attend_kernel, kv_local=kv_local, group=...  4.14 us
  transfers between devices with their start and end apart: 20, of which 13 were waited for; matrix products, arithmetic and copies ran while one was open for 1% of the time, Pallas kernels for 0%

profile of v1, /device:TPU:0, one launch (start us, length us, event | category | flops | bytes accessed | tf_op | source)
XLA Modules:
  0.0 102.0 jit_solution(11406030689346374808)
XLA Ops:
  0.0 2.8 %copy-done = bf16[24,2,256,256]{3,2,1,0:T(8,128)(2,1)S(1)} copy-done((bf16[24,2,256,256]{3,2,1,0:T(8,128)(2,1)S(1)}, bf16[24,2,256,256]{3,2,1,0:T(8,128)(2,1)}, u32[]{:S(2)}) %copy-start) | copy-done | bytes 6291480
  2.8 0.9 copy-done.1
  3.7 0.9 copy-done.4
  4.6 0.7 copy-done.5
  5.3 0.7 copy-done.7
  5.9 4.1 %attend.1 = (bf16[24,1536]{1,0:T(8,128)(2,1)S(1)}, bf16[24,1536]{1,0:T(8,128)(2,1)S(1)}) custom-call(s32[24]{0:T(128)S(1)} %copy-done.7, bf16[24,1536]{1,0:T(8,128)(2,1)S(1)} %copy-done.4, bf16[24,2,256]{2,1,0:T(2,128)(2,1)S(1)} %copy-done.5, bf16[24,1536]{1,0:T(8,128)(2,1)S(1)} %copy-done.1, bf16[24,2,256,256]{3,2,1,0:T(8,128)(2,1)S(1)} %copy-done), custom_call_target="tpu_custom_call" | custom-call | tf_op jit(solution)/shard_map/attend/pallas_call | solution.py:90
  10.1 5.1 %collective-permute-start.2 = (bf16[24,1536]{1,0:T(8,128)(2,1)S(1)}, bf16[24,1536]{1,0:T(8,128)(2,1)S(1)}, u32[]{:S(2)}, u32[]{:S(2)}) collective-permute-start(bf16[24,1536]{1,0:T(8,128)(2,1)S(1)} %get-tuple-element.16), channel_id=1, source_target_pairs={{0,3},{1,2},{2,1},{3,0},{4,7},{5,6},{6,5},{7,4},{8,11},{9,10},{10,... | collective-permute-start | bytes 221192 | tf_op jit(solution)/shard_map/ppermute | solution.py:273
  15.2 0.0 collective-permute-start.1
  15.2 0.6 collective-permute-start
  15.9 0.7 convert_element_type.80
  16.5 0.1 copy.13
  16.6 3.3 %collective-permute-done = bf16[24,1536]{1,0:T(8,128)(2,1)S(1)} collective-permute-done((bf16[24,1536]{1,0:T(8,128)(2,1)S(1)}, bf16[24,1536]{1,0:T(8,128)(2,1)S(1)}, u32[]{:S(2)}, u32[]{:S(2)}) %collective-permute-start) | collective-permute-done | bytes 73760 | tf_op jit(solution)/shard_map/ppermute | solution.py:273
  19.9 1.5 %collective-permute-done.1 = bf16[24,1536]{1,0:T(8,128)(2,1)S(1)} collective-permute-done((bf16[24,1536]{1,0:T(8,128)(2,1)S(1)}, bf16[24,1536]{1,0:T(8,128)(2,1)S(1)}, u32[]{:S(2)}, u32[]{:S(2)}) %collective-permute-start.1) | collective-permute-done | bytes 73760 | tf_op jit(solution)/shard_map/ppermute | solution.py:273
  21.4 0.0 collective-permute-done.2
  21.5 0.0 copy-start.8
  21.5 2.5 %collective-permute-start.5 = (bf16[24,6272]{1,0:T(8,128)(2,1)S(1)}, bf16[24,6272]{1,0:T(8,128)(2,1)S(1)}, u32[]{:S(2)}, u32[]{:S(2)}) collective-permute-start(bf16[24,6272]{1,0:T(8,128)(2,1)S(1)} %constant_dynamic-update-slice_fusion.rest_0_), channel_id=1, source_target_pairs={{0,12},{4,8},{8,4},{12,0},{1,13},{5,9},{9,5},{13,1},{2,14},{6,10},... | collective-permute-start | bytes 903176 | tf_op jit(solution)/shard_map/ppermute | solution.py:273
  24.0 0.5 collective-permute-start.4
  24.5 0.5 collective-permute-start.3
  25.0 0.0 collective-permute-start.6
  25.0 7.5 %collective-permute-done.5.rest_3_ = bf16[24,6272]{1,0:T(8,128)(2,1)S(1)} collective-permute-done((bf16[24,6272]{1,0:T(8,128)(2,1)S(1)}, bf16[24,6272]{1,0:T(8,128)(2,1)S(1)}, u32[]{:S(2)}, u32[]{:S(2)}) %collective-permute-start.5) | collective-permute-done | bytes 301088 | tf_op jit(solution)/shard_map/ppermute | solution.py:273
  32.6 0.0 collective-permute-start.9
  32.6 4.8 %collective-permute-done.4.rest_2_ = bf16[24,6272]{1,0:T(8,128)(2,1)S(1)} collective-permute-done((bf16[24,6272]{1,0:T(8,128)(2,1)S(1)}, bf16[24,6272]{1,0:T(8,128)(2,1)S(1)}, u32[]{:S(2)}, u32[]{:S(2)}) %collective-permute-start.4) | collective-permute-done | bytes 301088 | tf_op jit(solution)/shard_map/ppermute | solution.py:273
  37.4 0.0 collective-permute-start.8
  37.4 0.3 collective-permute-done.3.rest_1_
  37.7 0.2 collective-permute-start.7
  37.9 0.1 pad_add_fusion.place_ref
  38.0 0.0 collective-permute-done.6.rest_4_
  38.0 0.0 collective-permute-done.9.rest_7_
  38.0 0.0 copy-start.13
  38.0 1.0 collective-permute-done.8.rest_6_
  39.0 0.4 collective-permute-done.7.rest_5_
  39.4 0.0 copy-done.8
  39.4 0.0 copy-done.9
  39.4 0.0 copy-done.10
  39.5 0.2 copy-done.14
  39.7 0.4 copy-done.15
  40.1 0.9 copy-done.3
  41.1 0.7 copy-done.6
  41.8 31.3 %experts.1 = (bf16[24,6144]{1,0:T(8,128)(2,1)S(1)}, bf16[24,6144]{1,0:T(8,128)(2,1)S(1)}, bf16[24,6144]{1,0:T(8,128)(2,1)S(1)}, bf16[24,6144]{1,0:T(8,128)(2,1)S...) custom-call(s32[2]{0:T(128)S(1)} %pad_add_fusion.place_ref, ...), custom_call_target="tpu_custom_call" | custom-call | tf_op jit(solution)/shard_map/experts/pallas_call | solution.py:240
  73.1 0.2 collective-permute-start.11
  73.3 0.4 collective-permute-start.10
  73.7 0.1 collective-permute-start.13
  73.8 0.4 collective-permute-start.15
  74.2 0.6 collective-permute-done.11
  74.8 0.1 add_convert_fusion.3
  74.8 1.8 %collective-permute-start.12 = (bf16[24,6144]{1,0:T(8,128)(2,1)S(1)}, bf16[24,6144]{1,0:T(8,128)(2,1)S(1)}, u32[]{:S(2)}, u32[]{:S(2)}) collective-permute-start(bf16[24,6144]{1,0:T(8,128)(2,1)S(1)} %add_convert_fusion.3), channel_id=1, source_target_pairs={{0,4},{4,0},{8,12},{12,8},{1,5},{5,1},{9,13},{13,9},{2,6},{6,2},{1... | collective-permute-start | bytes 884744 | tf_op jit(solution)/shard_map/ppermute | solution.py:273
  76.6 0.0 collective-permute-done.13
  76.6 0.1 add_convert_fusion.2
  76.7 1.0 collective-permute-start.14
  77.7 0.0 collective-permute-done.15
  77.7 0.1 add_convert_fusion.1
  77.8 1.5 %collective-permute-start.16 = (bf16[24,6144]{1,0:T(8,128)(2,1)S(1)}, bf16[24,6144]{1,0:T(8,128)(2,1)S(1)}, u32[]{:S(2)}, u32[]{:S(2)}) collective-permute-start(bf16[24,6144]{1,0:T(8,128)(2,1)S(1)} %add_convert_fusion.1), channel_id=1, source_target_pairs={{0,12},{4,8},{8,4},{12,0},{1,13},{5,9},{9,5},{13,1},{2,14},{6,10},... | collective-permute-start | bytes 884744 | tf_op jit(solution)/shard_map/ppermute | solution.py:273
  79.3 0.0 collective-permute-done.10
  79.3 5.5 %collective-permute-done.12 = bf16[24,6144]{1,0:T(8,128)(2,1)S(1)} collective-permute-done((bf16[24,6144]{1,0:T(8,128)(2,1)S(1)}, bf16[24,6144]{1,0:T(8,128)(2,1)S(1)}, u32[]{:S(2)}, u32[]{:S(2)}) %collective-permute-start.12) | collective-permute-done | bytes 294944 | tf_op jit(solution)/shard_map/ppermute | solution.py:273
  84.8 7.1 %collective-permute-done.14 = bf16[24,6144]{1,0:T(8,128)(2,1)S(1)} collective-permute-done((bf16[24,6144]{1,0:T(8,128)(2,1)S(1)}, bf16[24,6144]{1,0:T(8,128)(2,1)S(1)}, u32[]{:S(2)}, u32[]{:S(2)}) %collective-permute-start.14) | collective-permute-done | bytes 294944 | tf_op jit(solution)/shard_map/ppermute | solution.py:273
  91.8 0.0 collective-permute-done.16
  91.8 0.2 add_convert_fusion
  92.0 0.1 collective-permute-start.17
  92.2 1.6 %collective-permute-start.19 = (bf16[24,1536]{1,0:T(8,128)(2,1)S(1)}, bf16[24,1536]{1,0:T(8,128)(2,1)S(1)}, u32[]{:S(2)}, u32[]{:S(2)}) collective-permute-start(bf16[24,1536]{1,0:T(8,128)(2,1)S(1)} %get-tuple-element.26), channel_id=1, source_target_pairs={{0,3},{1,2},{2,1},{3,0},{4,7},{5,6},{6,5},{7,4},{8,11},{9,10},{10,... | collective-permute-start | bytes 221192 | tf_op jit(solution)/shard_map/ppermute | solution.py:273
  93.8 1.8 %collective-permute-start.18 = (bf16[24,1536]{1,0:T(8,128)(2,1)S(1)}, bf16[24,1536]{1,0:T(8,128)(2,1)S(1)}, u32[]{:S(2)}, u32[]{:S(2)}) collective-permute-start(bf16[24,1536]{1,0:T(8,128)(2,1)S(1)} %get-tuple-element.27), channel_id=1, source_target_pairs={{0,2},{1,3},{2,0},{3,1},{4,6},{5,7},{6,4},{7,5},{8,10},{9,11},{10,... | collective-permute-start | bytes 221192 | tf_op jit(solution)/shard_map/ppermute | solution.py:273
  95.6 2.0 %collective-permute-done.17 = bf16[24,1536]{1,0:T(8,128)(2,1)S(1)} collective-permute-done((bf16[24,1536]{1,0:T(8,128)(2,1)S(1)}, bf16[24,1536]{1,0:T(8,128)(2,1)S(1)}, u32[]{:S(2)}, u32[]{:S(2)}) %collective-permute-start.17) | collective-permute-done | bytes 73760 | tf_op jit(solution)/shard_map/ppermute | solution.py:273
  97.6 1.0 collective-permute-done.19
  98.5 2.8 %collective-permute-done.18 = bf16[24,1536]{1,0:T(8,128)(2,1)S(1)} collective-permute-done((bf16[24,1536]{1,0:T(8,128)(2,1)S(1)}, bf16[24,1536]{1,0:T(8,128)(2,1)S(1)}, u32[]{:S(2)}, u32[]{:S(2)}) %collective-permute-start.18) | collective-permute-done | bytes 73760 | tf_op jit(solution)/shard_map/ppermute | solution.py:273
  101.3 0.7 add_convert_fusion.5
  (24 shorter events, 0.1 us)
Async XLA Ops:
  0.0 2.8 %copy-start = (bf16[24,2,256,256]{3,2,1,0:T(8,128)(2,1)S(1)}, bf16[24,2,256,256]{3,2,1,0:T(8,128)(2,1)}, u32[]{:S(2)}) copy-start(bf16[24,2,256,256]{3,2,1,0:T(8,128)(2,1)} %cache_ref.1) | copy-start | bytes 18874372
  2.8 0.9 copy-start.1
  3.7 0.9 copy-start.4
  4.6 0.7 copy-start.5
  5.3 0.7 copy-start.7
  10.1 11.3 %collective-permute-start.2 = (bf16[24,1536]{1,0:T(8,128)(2,1)S(1)}, bf16[24,1536]{1,0:T(8,128)(2,1)S(1)}, u32[]{:S(2)}, u32[]{:S(2)}) collective-permute-start(bf16[24,1536]{1,0:T(8,128)(2,1)S(1)} %get-tuple-element.16), channel_id=1, source_target_pairs={{0,3},{1,2},{2,1},{3,0},{4,7},{5,6},{6,5},{7,4},{8,11},{9,10},{10,... | collective-permute-start | bytes 221192 | tf_op jit(solution)/shard_map/ppermute | solution.py:273
  15.2 6.2 %collective-permute-start.1 = (bf16[24,1536]{1,0:T(8,128)(2,1)S(1)}, bf16[24,1536]{1,0:T(8,128)(2,1)S(1)}, u32[]{:S(2)}, u32[]{:S(2)}) collective-permute-start(bf16[24,1536]{1,0:T(8,128)(2,1)S(1)} %get-tuple-element.16), channel_id=1, source_target_pairs={{0,2},{1,3},{2,0},{3,1},{4,6},{5,7},{6,4},{7,5},{8,10},{9,11},{10,... | collective-permute-start | bytes 221192 | tf_op jit(solution)/shard_map/ppermute | solution.py:273
  15.2 4.7 %collective-permute-start = (bf16[24,1536]{1,0:T(8,128)(2,1)S(1)}, bf16[24,1536]{1,0:T(8,128)(2,1)S(1)}, u32[]{:S(2)}, u32[]{:S(2)}) collective-permute-start(bf16[24,1536]{1,0:T(8,128)(2,1)S(1)} %get-tuple-element.16), channel_id=1, source_target_pairs={{0,1},{1,0},{2,3},{3,2},{4,5},{5,4},{6,7},{7,6},{8,9},{9,8},{10,11... | collective-permute-start | bytes 221192 | tf_op jit(solution)/shard_map/ppermute | solution.py:273
  21.5 18.0 %copy-start.8 = (bf16[24,6272]{1,0:T(8,128)(2,1)}, bf16[24,6272]{1,0:T(8,128)(2,1)S(1)}, u32[]{:S(2)}) copy-start(bf16[24,6272]{1,0:T(8,128)(2,1)S(1)} %constant_dynamic-update-slice_fusion.rest_0_) | copy-start | bytes 903172
  21.5 11.1 %collective-permute-start.5 = (bf16[24,6272]{1,0:T(8,128)(2,1)S(1)}, bf16[24,6272]{1,0:T(8,128)(2,1)S(1)}, u32[]{:S(2)}, u32[]{:S(2)}) collective-permute-start(bf16[24,6272]{1,0:T(8,128)(2,1)S(1)} %constant_dynamic-update-slice_fusion.rest_0_), channel_id=1, source_target_pairs={{0,12},{4,8},{8,4},{12,0},{1,13},{5,9},{9,5},{13,1},{2,14},{6,10},... | collective-permute-start | bytes 903176 | tf_op jit(solution)/shard_map/ppermute | solution.py:273
  24.0 13.4 %collective-permute-start.4 = (bf16[24,6272]{1,0:T(8,128)(2,1)S(1)}, bf16[24,6272]{1,0:T(8,128)(2,1)S(1)}, u32[]{:S(2)}, u32[]{:S(2)}) collective-permute-start(bf16[24,6272]{1,0:T(8,128)(2,1)S(1)} %constant_dynamic-update-slice_fusion.rest_0_), channel_id=1, source_target_pairs={{0,8},{4,12},{8,0},{12,4},{1,9},{5,13},{9,1},{13,5},{2,10},{6,14},... | collective-permute-start | bytes 903176 | tf_op jit(solution)/shard_map/ppermute | solution.py:273
  24.5 13.2 %collective-permute-start.3 = (bf16[24,6272]{1,0:T(8,128)(2,1)S(1)}, bf16[24,6272]{1,0:T(8,128)(2,1)S(1)}, u32[]{:S(2)}, u32[]{:S(2)}) collective-permute-start(bf16[24,6272]{1,0:T(8,128)(2,1)S(1)} %constant_dynamic-update-slice_fusion.rest_0_), channel_id=1, source_target_pairs={{0,4},{4,0},{8,12},{12,8},{1,5},{5,1},{9,13},{13,9},{2,6},{6,2},{1... | collective-permute-start | bytes 903176 | tf_op jit(solution)/shard_map/ppermute | solution.py:273
  25.0 13.0 %collective-permute-start.6 = (bf16[24,6272]{1,0:T(8,128)(2,1)S(1)}, bf16[24,6272]{1,0:T(8,128)(2,1)S(1)}, u32[]{:S(2)}, u32[]{:S(2)}) collective-permute-start(bf16[24,6272]{1,0:T(8,128)(2,1)S(1)} %constant_dynamic-update-slice_fusion.rest_0_), channel_id=1, source_target_pairs={{0,16},{16,0},{1,17},{17,1},{2,18},{18,2},{3,19},{19,3},{4,20},{20... | collective-permute-start | bytes 903176 | tf_op jit(solution)/shard_map/ppermute | solution.py:273
  32.6 6.9 %copy-start.9 = (bf16[24,6272]{1,0:T(8,128)(2,1)}, bf16[24,6272]{1,0:T(8,128)(2,1)S(1)}, u32[]{:S(2)}) copy-start(bf16[24,6272]{1,0:T(8,128)(2,1)S(1)} %collective-permute-done.5.rest_3_) | copy-start | bytes 903172
  32.6 5.4 %collective-permute-start.9 = (bf16[24,6272]{1,0:T(8,128)(2,1)S(1)}, bf16[24,6272]{1,0:T(8,128)(2,1)S(1)}, u32[]{:S(2)}, u32[]{:S(2)}) collective-permute-start(bf16[24,6272]{1,0:T(8,128)(2,1)S(1)} %collective-permute-done.5.rest_3_), channel_id=1, source_target_pairs={{0,16},{16,0},{1,17},{17,1},{2,18},{18,2},{3,19},{19,3},{4,20},{20... | collective-permute-start | bytes 903176 | tf_op jit(solution)/shard_map/ppermute | solution.py:273
  37.4 2.0 %copy-start.10 = (bf16[24,6272]{1,0:T(8,128)(2,1)}, bf16[24,6272]{1,0:T(8,128)(2,1)S(1)}, u32[]{:S(2)}) copy-start(bf16[24,6272]{1,0:T(8,128)(2,1)S(1)} %collective-permute-done.4.rest_2_) | copy-start | bytes 903172
  37.4 1.6 %collective-permute-start.8 = (bf16[24,6272]{1,0:T(8,128)(2,1)S(1)}, bf16[24,6272]{1,0:T(8,128)(2,1)S(1)}, u32[]{:S(2)}, u32[]{:S(2)}) collective-permute-start(bf16[24,6272]{1,0:T(8,128)(2,1)S(1)} %collective-permute-done.4.rest_2_), channel_id=1, source_target_pairs={{0,16},{16,0},{1,17},{17,1},{2,18},{18,2},{3,19},{19,3},{4,20},{20... | collective-permute-start | bytes 903176 | tf_op jit(solution)/shard_map/ppermute | solution.py:273
  37.7 1.7 %copy-start.11 = (bf16[24,6272]{1,0:T(8,128)(2,1)}, bf16[24,6272]{1,0:T(8,128)(2,1)S(1)}, u32[]{:S(2)}) copy-start(bf16[24,6272]{1,0:T(8,128)(2,1)S(1)} %collective-permute-done.3.rest_1_) | copy-start | bytes 903172
  37.7 1.7 %collective-permute-start.7 = (bf16[24,6272]{1,0:T(8,128)(2,1)S(1)}, bf16[24,6272]{1,0:T(8,128)(2,1)S(1)}, u32[]{:S(2)}, u32[]{:S(2)}) collective-permute-start(bf16[24,6272]{1,0:T(8,128)(2,1)S(1)} %collective-permute-done.3.rest_1_), channel_id=1, source_target_pairs={{0,16},{16,0},{1,17},{17,1},{2,18},{18,2},{3,19},{19,3},{4,20},{20... | collective-permute-start | bytes 903176 | tf_op jit(solution)/shard_map/ppermute | solution.py:273
  38.0 1.5 %copy-start.12 = (bf16[24,6272]{1,0:T(8,128)(2,1)}, bf16[24,6272]{1,0:T(8,128)(2,1)S(1)}, u32[]{:S(2)}) copy-start(bf16[24,6272]{1,0:T(8,128)(2,1)S(1)} %collective-permute-done.6.rest_4_) | copy-start | bytes 903172
  38.0 1.5 %copy-start.13 = (bf16[24,6272]{1,0:T(8,128)(2,1)}, bf16[24,6272]{1,0:T(8,128)(2,1)S(1)}, u32[]{:S(2)}) copy-start(bf16[24,6272]{1,0:T(8,128)(2,1)S(1)} %collective-permute-done.9.rest_7_) | copy-start | bytes 903172
  39.0 0.7 copy-start.14
  39.4 0.7 copy-start.15
  40.1 0.9 copy-start.3
  41.1 0.7 copy-start.6
  41.8 59.5 %copy-start.2 = (bf16[24,1536]{1,0:T(8,128)(2,1)S(1)}, bf16[24,1536]{1,0:T(8,128)(2,1)}, u32[]{:S(2)}) copy-start(bf16[24,1536]{1,0:T(8,128)(2,1)} %resid_ref.1) | copy-start | bytes 221188
  73.1 1.6 %collective-permute-start.11 = (bf16[24,6144]{1,0:T(8,128)(2,1)S(1)}, bf16[24,6144]{1,0:T(8,128)(2,1)S(1)}, u32[]{:S(2)}, u32[]{:S(2)}) collective-permute-start(bf16[24,6144]{1,0:T(8,128)(2,1)S(1)} %get-tuple-element.20), channel_id=1, source_target_pairs={{0,16},{16,0},{1,17},{17,1},{2,18},{18,2},{3,19},{19,3},{4,20},{20... | collective-permute-start | bytes 884744 | tf_op jit(solution)/shard_map/ppermute | solution.py:273
  73.3 5.9 %collective-permute-start.10 = (bf16[24,6144]{1,0:T(8,128)(2,1)S(1)}, bf16[24,6144]{1,0:T(8,128)(2,1)S(1)}, u32[]{:S(2)}, u32[]{:S(2)}) collective-permute-start(bf16[24,6144]{1,0:T(8,128)(2,1)S(1)} %get-tuple-element.18), channel_id=1, source_target_pairs={{0,16},{16,0},{1,17},{17,1},{2,18},{18,2},{3,19},{19,3},{4,20},{20... | collective-permute-start | bytes 884744 | tf_op jit(solution)/shard_map/ppermute | solution.py:273
  73.7 2.9 %collective-permute-start.13 = (bf16[24,6144]{1,0:T(8,128)(2,1)}, bf16[24,6144]{1,0:T(8,128)(2,1)S(1)}, u32[]{:S(2)}, u32[]{:S(2)}) collective-permute-start(bf16[24,6144]{1,0:T(8,128)(2,1)} %get-tuple-element.22), channel_id=1, source_target_pairs={{0,16},{16,0},{1,17},{17,1},{2,18},{18,2},{3,19},{19,3},{4,20},{20... | collective-permute-start | bytes 884744 | tf_op jit(solution)/shard_map/ppermute | solution.py:273
  73.8 3.8 %collective-permute-start.15 = (bf16[24,6144]{1,0:T(8,128)(2,1)}, bf16[24,6144]{1,0:T(8,128)(2,1)S(1)}, u32[]{:S(2)}, u32[]{:S(2)}) collective-permute-start(bf16[24,6144]{1,0:T(8,128)(2,1)} %get-tuple-element.24), channel_id=1, source_target_pairs={{0,16},{16,0},{1,17},{17,1},{2,18},{18,2},{3,19},{19,3},{4,20},{20... | collective-permute-start | bytes 884744 | tf_op jit(solution)/shard_map/ppermute | solution.py:273
  74.8 9.9 %collective-permute-start.12 = (bf16[24,6144]{1,0:T(8,128)(2,1)S(1)}, bf16[24,6144]{1,0:T(8,128)(2,1)S(1)}, u32[]{:S(2)}, u32[]{:S(2)}) collective-permute-start(bf16[24,6144]{1,0:T(8,128)(2,1)S(1)} %add_convert_fusion.3), channel_id=1, source_target_pairs={{0,4},{4,0},{8,12},{12,8},{1,5},{5,1},{9,13},{13,9},{2,6},{6,2},{1... | collective-permute-start | bytes 884744 | tf_op jit(solution)/shard_map/ppermute | solution.py:273
  76.7 15.2 %collective-permute-start.14 = (bf16[24,6144]{1,0:T(8,128)(2,1)S(1)}, bf16[24,6144]{1,0:T(8,128)(2,1)S(1)}, u32[]{:S(2)}, u32[]{:S(2)}) collective-permute-start(bf16[24,6144]{1,0:T(8,128)(2,1)S(1)} %add_convert_fusion.2), channel_id=1, source_target_pairs={{0,8},{4,12},{8,0},{12,4},{1,9},{5,13},{9,1},{13,5},{2,10},{6,14},... | collective-permute-start | bytes 884744 | tf_op jit(solution)/shard_map/ppermute | solution.py:273
  77.8 14.1 %collective-permute-start.16 = (bf16[24,6144]{1,0:T(8,128)(2,1)S(1)}, bf16[24,6144]{1,0:T(8,128)(2,1)S(1)}, u32[]{:S(2)}, u32[]{:S(2)}) collective-permute-start(bf16[24,6144]{1,0:T(8,128)(2,1)S(1)} %add_convert_fusion.1), channel_id=1, source_target_pairs={{0,12},{4,8},{8,4},{12,0},{1,13},{5,9},{9,5},{13,1},{2,14},{6,10},... | collective-permute-start | bytes 884744 | tf_op jit(solution)/shard_map/ppermute | solution.py:273
  92.0 5.5 %collective-permute-start.17 = (bf16[24,1536]{1,0:T(8,128)(2,1)S(1)}, bf16[24,1536]{1,0:T(8,128)(2,1)S(1)}, u32[]{:S(2)}, u32[]{:S(2)}) collective-permute-start(bf16[24,1536]{1,0:T(8,128)(2,1)S(1)} %get-tuple-element.25), channel_id=1, source_target_pairs={{0,1},{1,0},{2,3},{3,2},{4,5},{5,4},{6,7},{7,6},{8,9},{9,8},{10,11... | collective-permute-start | bytes 221192 | tf_op jit(solution)/shard_map/ppermute | solution.py:273
  92.2 6.4 %collective-permute-start.19 = (bf16[24,1536]{1,0:T(8,128)(2,1)S(1)}, bf16[24,1536]{1,0:T(8,128)(2,1)S(1)}, u32[]{:S(2)}, u32[]{:S(2)}) collective-permute-start(bf16[24,1536]{1,0:T(8,128)(2,1)S(1)} %get-tuple-element.26), channel_id=1, source_target_pairs={{0,3},{1,2},{2,1},{3,0},{4,7},{5,6},{6,5},{7,4},{8,11},{9,10},{10,... | collective-permute-start | bytes 221192 | tf_op jit(solution)/shard_map/ppermute | solution.py:273
  93.8 7.5 %collective-permute-start.18 = (bf16[24,1536]{1,0:T(8,128)(2,1)S(1)}, bf16[24,1536]{1,0:T(8,128)(2,1)S(1)}, u32[]{:S(2)}, u32[]{:S(2)}) collective-permute-start(bf16[24,1536]{1,0:T(8,128)(2,1)S(1)} %get-tuple-element.27), channel_id=1, source_target_pairs={{0,2},{1,3},{2,0},{3,1},{4,6},{5,7},{6,4},{7,5},{8,10},{9,11},{10,... | collective-permute-start | bytes 221192 | tf_op jit(solution)/shard_map/ppermute | solution.py:273

commit v2 on v1

v2 whole, which is shorter than its diff:
```python
import functools
import math

import jax
import jax.numpy as jnp
from jax import lax
from jax.experimental import pallas as pl
from jax.experimental.pallas import tpu as pltpu
from jax.sharding import PartitionSpec as P

HEAD_DIM = 128
ROWS_STEP = 8
MIB = 1 << 20
VMEM_GATE_UP = 22

epsilon = 1e-05


def largest_divisor(total, choices):
    return next(c for c in choices if total % c == 0)


def attend_kernel(lengths_ref, query_ref, new_ref, resid_ref, cache_ref, attended_ref, hidden_ref, *, heads, group):
    step = pl.program_id(0)
    rows = ROWS_STEP
    cache_len = cache_ref.shape[2]
    factor = 1.0 / math.sqrt(HEAD_DIM)
    for kv_head, lead, count in heads:
        stacked = count * rows
        row_of = lax.broadcasted_iota(jnp.int32, (stacked, 1), 0) % rows
        length_col = jnp.zeros((stacked, 1), jnp.int32)
        for n in range(rows):
            length_col = jnp.where(row_of == n, lengths_ref[step * rows + n], length_col)
        valid = lax.broadcasted_iota(jnp.int32, (stacked, cache_len), 1) < length_col
        lanes = pl.ds(kv_head * HEAD_DIM, HEAD_DIM)
        columns = [pl.ds((lead + g) * HEAD_DIM, HEAD_DIM) for g in range(count)]
        query = jnp.concatenate([query_ref[:, c].astype(jnp.float32) for c in columns], axis=0)
        query_bf = query.astype(jnp.bfloat16)
        new_key = new_ref[:, 0, lanes].astype(jnp.float32)
        new_value = new_ref[:, 1, lanes].astype(jnp.float32)
        scores = jnp.zeros((stacked, cache_len), jnp.float32)
        for n in range(rows):
            full = lax.dot_general(
                query_bf,
                cache_ref[n, 0, :, lanes],
                (((1,), (1,)), ((), ())),
                preferred_element_type=jnp.float32,
            )
            scores = jnp.where(row_of == n, full, scores)
        scores = jnp.where(valid, scores * factor, -jnp.inf)
        fresh = (
            jnp.sum(query * jnp.concatenate([new_key] * count, axis=0), axis=1, keepdims=True) * factor
        )
        largest = jnp.maximum(jnp.max(scores, axis=1, keepdims=True), fresh)
        weights = jnp.exp(scores - largest)
        fresh_weight = jnp.exp(fresh - largest)
        denominator = jnp.sum(weights, axis=1, keepdims=True) + fresh_weight
        probabilities = (weights / denominator).astype(jnp.bfloat16)
        fresh_prob = (fresh_weight / denominator).astype(jnp.bfloat16).astype(jnp.float32)
        output = jnp.zeros((stacked, HEAD_DIM), jnp.float32)
        for n in range(rows):
            full = jnp.dot(
                probabilities, cache_ref[n, 1, :, lanes], preferred_element_type=jnp.float32
            )
            output = jnp.where(row_of == n, full, output)
        output = output + fresh_prob * jnp.concatenate([new_value] * count, axis=0)
        for g, c in enumerate(columns):
            piece = output[g * rows : (g + 1) * rows].astype(jnp.bfloat16)
            attended_ref[:, c] = piece
            hidden_ref[:, c] = (
                resid_ref[:, c].astype(jnp.float32) + piece.astype(jnp.float32)
            ).astype(jnp.bfloat16)


def attend(lengths, queries, new_kv, resid_in, cache, chunk, chunks):
    sequences, part_cols = queries.shape
    cache_len, kv_cols = cache.shape[2:]
    kv_local = kv_cols // HEAD_DIM
    group = part_cols // kv_cols
    rows = ROWS_STEP
    width = part_cols // chunks
    count = width // HEAD_DIM
    lead = chunk * count
    spans = [
        (kv, max(kv * group, lead), min((kv + 1) * group, lead + count)) for kv in range(kv_local)
    ]
    spans = [span for span in spans if span[1] < span[2]]
    first_kv = spans[0][0]
    lanes = (spans[-1][0] - first_kv + 1) * HEAD_DIM
    assert kv_cols % lanes == 0 and first_kv * HEAD_DIM % lanes == 0
    heads = [(kv - first_kv, start - lead, stop - start) for kv, start, stop in spans]
    block = first_kv * HEAD_DIM // lanes

    def flat(index):
        return pl.BlockSpec((rows, width), lambda i, _: (i, index))

    return pl.pallas_call(
        functools.partial(attend_kernel, heads=heads, group=group),
        grid_spec=pltpu.PrefetchScalarGridSpec(
            num_scalar_prefetch=1,
            grid=(sequences // rows,),
            in_specs=[
                flat(chunk),
                pl.BlockSpec((rows, 2, lanes), lambda i, _: (i, 0, block)),
                flat(chunk),
                pl.BlockSpec((rows, 2, cache_len, lanes), lambda i, _: (i, 0, 0, block)),
            ],
            out_specs=[flat(0)] * 2,
        ),
        out_shape=[jax.ShapeDtypeStruct((sequences, width), jnp.bfloat16)] * 2,
        cost_estimate=pl.CostEstimate(
            flops=0, bytes_accessed=2 * cache.size // chunks, transcendentals=0
        ),
        compiler_params=pltpu.CompilerParams(vmem_limit_bytes=32 * MIB),
        name="attend",
    )(lengths, *(pin(array, pltpu.HBM) for array in (queries, new_kv, resid_in, cache)))


def fetch_kernel(after_ref, earlier_ref, source_hbm, *rest, index, extras):
    extra_hbm, (target_ref, token_ref, *extra_refs, sem) = rest[:extras], rest[extras:]
    pieces = sem.shape[0] - extras
    step = target_ref.shape[0] // pieces
    copies = [
        pltpu.make_async_copy(source, target, sem.at[pieces + i])
        for i, (source, target) in enumerate(zip(extra_hbm, extra_refs))
    ]
    copies += [
        pltpu.make_async_copy(
            source_hbm.at[index, pl.ds(i * step, step)], target_ref.at[pl.ds(i * step, step)], sem.at[i]
        )
        for i in range(pieces)
    ]
    for copy in copies:
        copy.start()
    token_ref[...] = jnp.zeros_like(token_ref)
    for copy in copies:
        copy.wait()


def fetch(after, earlier, weights, index, extra=()):
    shape = weights.shape[1:]
    pieces = 8
    hbm = pl.BlockSpec(memory_space=pltpu.HBM)
    return pl.pallas_call(
        functools.partial(fetch_kernel, index=index, extras=len(extra)),
        in_specs=[pl.BlockSpec(memory_space=pl.ANY)] * 2 + [hbm] * (1 + len(extra)),
        out_specs=[pl.BlockSpec(memory_space=pltpu.VMEM)] * (2 + len(extra)),
        out_shape=[pltpu.VMEM(shape, weights.dtype), pltpu.VMEM((8, 128), jnp.float32)]
        + [pltpu.VMEM(array.shape, array.dtype) for array in extra],
        scratch_shapes=[pltpu.SemaphoreType.DMA((pieces + len(extra),))],
        cost_estimate=pl.CostEstimate(flops=0, bytes_accessed=2 * math.prod(shape), transcendentals=0),
        compiler_params=pltpu.CompilerParams(vmem_limit_bytes=1 * MIB),
        name="fetch",
    )(after, earlier, *(pin(array, pltpu.HBM) for array in (weights, *extra)))


def norm_kernel(gain_ref, router_ref, ids_ref, *rest):
    part_refs, own_ref = rest[:-1], rest[-1]
    tps = len(part_refs)
    rows, part_cols = part_refs[0].shape
    width = tps * part_cols
    experts = router_ref.shape[0]
    tp = lax.axis_index("tp")
    places = [pl.ds(pl.multiple_of((j ^ tp) * part_cols, 128), part_cols) for j in range(tps)]
    raws = [ref[...].astype(jnp.float32) for ref in part_refs]
    squares = sum(jnp.sum(raw * raw, axis=1, keepdims=True) for raw in raws)
    row_scale = lax.rsqrt(squares / width + epsilon)
    logits = jnp.zeros((rows, 2 * experts), jnp.float32)
    for raw, there in zip(raws, places):
        normed = (raw * row_scale * gain_ref[:, there]).astype(jnp.bfloat16)
        own_ref[:, there] = normed
        router = router_ref[:, there]
        high = router.astype(jnp.bfloat16).astype(jnp.float32)
        both = jnp.concatenate([high, router - high], axis=0).astype(jnp.bfloat16)
        logits += lax.dot_general(
            normed, both, (((1,), (1,)), ((), ())), preferred_element_type=jnp.float32
        )
    logits = logits[:, :experts] + logits[:, experts:]
    square = [lax.broadcasted_iota(jnp.int32, (rows, rows), axis) for axis in range(2)]
    identity = jnp.where(square[0] == square[1], 1.0, 0.0)
    ids = lax.dot_general(
        identity, ids_ref[...].astype(jnp.float32), (((1,), (1,)), ((), ())), preferred_element_type=jnp.float32
    ).astype(jnp.int32)
    names = [ids[:, k : k + 1] for k in range(2)]
    lane = lax.broadcasted_iota(jnp.int32, (rows, experts), 1)
    picked = [jnp.sum(jnp.where(lane == name, logits, 0.0), axis=1, keepdims=True) for name in names]
    mixes = [
        1.0 / (1.0 + jnp.exp(picked[1] - picked[0])),
        1.0 / (1.0 + jnp.exp(picked[0] - picked[1])),
    ]
    lane = lax.broadcasted_iota(jnp.int32, (rows, 128), 1)
    share = sum(jnp.where(lane % experts == name, mix, 0.0) for name, mix in zip(names, mixes))
    high = share.astype(jnp.bfloat16).astype(jnp.float32)
    own_ref[:, pl.ds(width, 128)] = jnp.where(lane < experts, high, share - high).astype(jnp.bfloat16)


def norm(gain, router, route_ids, parts):
    rows, part_cols = parts[0].shape
    vmem = pl.BlockSpec(memory_space=pltpu.VMEM)
    near = [pin(a, pltpu.VMEM) for a in (gain, router, route_ids, *parts)]
    return pl.pallas_call(
        norm_kernel,
        in_specs=[vmem] * len(near),
        out_specs=vmem,
        out_shape=pltpu.VMEM((rows, part_cols * len(parts) + 128), jnp.bfloat16),
        compiler_params=pltpu.CompilerParams(vmem_limit_bytes=2 * MIB),
        name="norm",
    )(*near)


def split_kernel(first_ref, second_ref, left_ref, right_ref):
    cut = left_ref.shape[1]
    left_ref[...] = first_ref[:, pl.ds(0, cut)]
    right_ref[...] = second_ref[:, pl.ds(cut, right_ref.shape[1])]


def split(first, second, cut):
    rows, width = first.shape
    vmem = pl.BlockSpec(memory_space=pltpu.VMEM)
    return pl.pallas_call(
        split_kernel,
        in_specs=[vmem] * 2,
        out_specs=[vmem] * 2,
        out_shape=[pltpu.VMEM((rows, cut), first.dtype), pltpu.VMEM((rows, width - cut), first.dtype)],
        compiler_params=pltpu.CompilerParams(vmem_limit_bytes=1 * MIB),
        name="split",
    )(pin(first, pltpu.VMEM), pin(second, pltpu.VMEM))


def gate_up_kernel(gate_hbm, up_hbm, token_ref, gate_ref, *rest, layout, experts, blocks_held, depth, nb):
    pieces = sum(layout)
    piece_refs, (act_ref, buf, rows_ref, sem) = rest[:pieces], rest[pieces:]
    held, width, ff = gate_hbm.shape
    ready = 1
    blocks = ff // nb
    deep = buf.shape[1]
    cuts = width // deep
    steps = (2 * held - ready) * blocks * cuts
    grp = lax.axis_index("grp")

    def block_copy(hbm, e, n, i):
        slot = lax.rem(i, depth)
        columns = pl.ds(pl.multiple_of(n * nb, 128), nb)
        there = pl.ds(pl.multiple_of(i % cuts * deep, 128), deep)
        return pltpu.make_async_copy(hbm.at[e, there, columns], buf.at[slot], sem.at[slot])

    def start(i):
        first = 0
        for e in range(held):
            kinds = (up_hbm,) if e < ready else (gate_hbm, up_hbm)
            for which, hbm in enumerate(kinds):
                inside = i // cuts - first
                hit = (inside >= 0) & (inside < len(kinds) * blocks) & (inside % len(kinds) == which)

                @pl.when(hit)
                def _():
                    block_copy(hbm, e, inside // len(kinds), i).start()

            first += len(kinds) * blocks

    def prime(i, carry):
        start(i)
        return carry

    lax.fori_loop(0, min(depth, steps), prime, 0)

    rows_of, first = [], 0
    for parts in layout:
        rows_of.append(piece_refs[first : first + parts])
        first += parts

    def gather(start_column, size):
        found = []
        for refs in rows_of:
            at = start_column
            for ref in refs:
                if at < ref.shape[1]:
                    found.append(ref[:, pl.ds(at, size)].astype(jnp.float32))
                    break
                at -= ref.shape[1]
        return jnp.concatenate(found, axis=0)

    for k in range(width // deep):
        rows_ref[:, pl.ds(k * deep, deep)] = gather(k * deep, deep).astype(jnp.bfloat16)
    shares = gather(width, 128)
    shares = shares[:, :experts] + shares[:, experts : 2 * experts]
    lane = lax.broadcasted_iota(jnp.int32, shares.shape, 1)

    def streamed(block):
        product = 0.0
        for cut in range(cuts):
            i = block * cuts + cut
            block_copy(gate_hbm, 0, 0, i).wait()
            there = pl.ds(cut * deep, deep)
            product += jnp.dot(
                rows_ref[:, there], buf[lax.rem(i, depth)], preferred_element_type=jnp.float32
            )

            @pl.when(i + depth < steps)
            def _():
                start(i + depth)

        return product

    first = 0
    for e in range(held):
        expert = (grp * held + e) // blocks_held
        share = jnp.sum(jnp.where(lane == expert, shares, 0.0), axis=1, keepdims=True)

        def body(n, carry, e=e, first=first, share=share):
            columns = pl.ds(pl.multiple_of(n * nb, 128), nb)
            if e < ready:
                i = first + n
                gate = jnp.dot(rows_ref[...], gate_ref[:, columns], preferred_element_type=jnp.float32)
            else:
                i = first + 2 * n + 1
                gate = streamed(i - 1)
            up = streamed(i) * share
            out = pl.ds(pl.multiple_of(e * ff + n * nb, 128), nb)
            act_ref[:, out] = (gate / (1.0 + jnp.exp(-gate)) * up).astype(jnp.bfloat16)
            return carry

        lax.fori_loop(0, blocks, body, 0)
        first += (1 if e < ready else 2) * blocks


def gate_up(w_gate, w_up, token, gate_ready, pieces, experts, blocks_held):
    held, width, ff = w_gate.shape
    tokens = sum(parts[0].shape[0] for parts in pieces)
    nb = largest_divisor(ff, (1024, 512, 256, 128))
    depth, cuts = 4, 4
    vmem = pl.BlockSpec(memory_space=pltpu.VMEM)
    hbm = pl.BlockSpec(memory_space=pltpu.HBM)
    near = [pin(a, pltpu.VMEM) for a in (gate_ready, *(part for parts in pieces for part in parts))]
    return pl.pallas_call(
        functools.partial(
            gate_up_kernel,
            layout=tuple(len(parts) for parts in pieces),
            experts=experts,
            blocks_held=blocks_held,
            depth=depth,
            nb=nb,
        ),
        in_specs=[hbm] * 2 + [pl.BlockSpec(memory_space=pl.ANY)] + [vmem] * len(near),
        out_specs=vmem,
        out_shape=pltpu.VMEM((tokens, held * ff), jnp.bfloat16),
        scratch_shapes=[
            pltpu.VMEM((depth, width // cuts, nb), jnp.bfloat16),
            pltpu.VMEM((tokens, width), jnp.bfloat16),
            pltpu.SemaphoreType.DMA((depth,)),
        ],
        cost_estimate=pl.CostEstimate(
            flops=4 * held * tokens * width * ff, bytes_accessed=4 * held * width * ff, transcendentals=0
        ),
        compiler_params=pltpu.CompilerParams(vmem_limit_bytes=VMEM_GATE_UP * MIB),
        name="gate_up",
    )(pin(w_gate, pltpu.HBM), pin(w_up, pltpu.HBM), token, *near)


def down_kernel(act_ref, *rest, first, part_cols, cuts):
    down_refs, (own_ref, other_ref) = rest[:-2], rest[-2:]
    ff = down_refs[0].shape[0]
    half = own_ref.shape[0]
    nb = part_cols // cuts
    tp = lax.axis_index("tp")

    def body(i, carry):
        j = first + i // cuts
        there = pl.ds(pl.multiple_of((j ^ tp) * part_cols + i % cuts * nb, 128), nb)
        partial = sum(
            jnp.dot(act_ref[:, pl.ds(e * ff, ff)], ref[:, there], preferred_element_type=jnp.float32)
            for e, ref in enumerate(down_refs)
        )
        columns = pl.ds(pl.multiple_of(i * nb, 128), nb)
        own_ref[:, columns] = partial[:half].astype(jnp.bfloat16)
        other_ref[:, columns] = partial[half:].astype(jnp.bfloat16)
        return carry

    lax.fori_loop(0, own_ref.shape[1] // nb, body, 0)


def down(act, weights, first, parts, part_cols, secs):
    tokens, depth = act.shape
    vmem = pl.BlockSpec(memory_space=pltpu.VMEM)
    near = [pin(a, pltpu.VMEM) for a in (act, *weights)]
    return pl.pallas_call(
        functools.partial(down_kernel, first=first, part_cols=part_cols, cuts=2),
        in_specs=[vmem] * len(near),
        out_specs=[vmem] * secs,
        out_shape=[pltpu.VMEM((tokens // secs, parts * part_cols), jnp.bfloat16)] * secs,
        cost_estimate=pl.CostEstimate(
            flops=2 * tokens * depth * parts * part_cols, bytes_accessed=0, transcendentals=0
        ),
        compiler_params=pltpu.CompilerParams(vmem_limit_bytes=4 * MIB),
        name="down",
    )(*near)


def pin(array, space):
    return pltpu.with_memory_space_constraint(array, space)


def swap(array, axis, offset):
    size = lax.axis_size(axis)
    return lax.ppermute(array, axis, [(i, i ^ offset) for i in range(size)])


def on_device(
    resid_in, queries, new_kv, cache, lengths, norm_gain, router, route_ids, w_gate, w_up, w_down
):
    sequences, part_cols = resid_in.shape
    tps, grps, secs = lax.axis_size("tp"), lax.axis_size("grp"), lax.axis_size("sec")
    held = w_gate.shape[0]
    blocks_held = max(1, grps * held // router.shape[1])
    tie = lax.optimization_barrier
    attended, hidden = attend(lengths, queries, new_kv, resid_in, cache, 0, 1)

    parts = [hidden] + [swap(hidden, "tp", j) for j in range(1, tps)]
    gain, router_rows = norm_gain.reshape(1, -1), router.T
    gate_ready, token, gain, router_rows, ids = fetch(
        hidden, hidden, w_gate, 0, (gain, router_rows, route_ids.T)
    )
    own = norm(gain, router_rows, ids, parts)
    down_ready = []
    if grps == 4:
        near = [own, swap(own, "grp", 1), swap(own, "grp", 2)]
        ready, token = fetch(own, token, w_down, 0)
        down_ready.append(ready)
        near, token = tie((near, token))
        after, right = split(near[2], near[1], tps // 2 * part_cols)
        across = [swap(after, "grp", 1), swap(right, "grp", 2)]
        near = [[array] for array in near]
    else:
        near = [[own]] + [[swap(own, "grp", d)] for d in range(1, grps - 1)]
        after = own
        across = [swap(own, "grp", grps - 1)]
    for e in range(len(down_ready), held):
        ready, token = fetch(after, token, w_down, e)
        down_ready.append(ready)
    across, token = tie((across, token))
    near.append(across)
    pieces = near + [[swap(array, "sec", 1) for array in arrays] for arrays in near]
    act = gate_up(w_gate, w_up, token, gate_ready, pieces, router.shape[1], blocks_held)

    def total(arrays):
        result = arrays[0].astype(jnp.float32)
        for array in arrays[1:]:
            result = result + array.astype(jnp.float32)
        return result

    halves = []
    for c in range(2):
        kept, sent = down(act, down_ready, c * tps // 2, tps // 2, part_cols, secs)
        act, _ = tie((act, sent))
        halves.append((kept, swap(sent, "sec", 1)))
    size = sequences
    sums = [
        [total([array[d * size : (d + 1) * size] for array in half]) for half in halves]
        for d in range(grps)
    ]

    def send(array, name, offset):
        return swap(array.astype(jnp.bfloat16), name, offset).astype(jnp.float32)

    if grps == 4:
        left, right = send(sums[3][0], "grp", 1), send(sums[3][1], "grp", 2)
        sums[2][0] += left
        sums[1][1] += right
        del sums[3]
    sums = [jnp.concatenate(pair, axis=1) for pair in sums]
    rows_sum = total([sums[0]] + [send(sums[d], "grp", d) for d in range(1, len(sums))])
    parts = [rows_sum[:, j * part_cols : (j + 1) * part_cols] for j in range(tps)]
    mixed = total([parts[0]] + [send(parts[j], "tp", j) for j in range(1, tps)])
    hidden_part = resid_in.astype(jnp.float32) + attended.astype(jnp.float32)
    return (hidden_part + mixed).astype(jnp.bfloat16)


def solution(mesh):
    return jax.shard_map(
        on_device,
        mesh=mesh,
        in_specs=(
            P(("sec", "grp"), "tp"),
            P(("sec", "grp"), "tp"),
            P(("sec", "grp"), None, "tp"),
            P(("sec", "grp"), None, None, "tp"),
            P(("sec", "grp")),
            P(),
            P(),
            P(("sec", "grp"), None),
            P("grp", None, ("sec", "tp")),
            P("grp", None, ("sec", "tp")),
            P("grp", ("sec", "tp"), None),
        ),
        out_specs=P(("sec", "grp"), "tp"),
        check_vma=False,
    )
```

time: 102 us -> 84.9 us (0.83)
  waiting for transfers between devices: 37.7 us -> 21.7 us
  local copies, waits for them, and re-layouts: 8.46 us -> 0.68 us
  Pallas kernels: 35.4 us -> 40.6 us
  starting transfers between devices: 18.4 us -> 20.4 us
    ppermute x20 -> x21, waiting for transfers between devices: 37.7 us -> 21.7 us  [swap(): return lax.ppermute(array, axis, [(i, i ^ offset) for i in range(size)])]
    unnamed x36 -> x4, local copies, waits for them, and re-layouts: 8.33 us -> 0.66 us
    pallas_call x2 -> x9, Pallas kernels: 35.4 us -> 40.6 us  [the longest x3 14.3 us: fetch(): pl.pallas_call(functools.partial(fetch_kernel, index=index, extras=len(ex...]
    ppermute x20 -> x21, starting transfers between devices: 18.4 us -> 20.4 us  [swap(): return lax.ppermute(array, axis, [(i, i ^ offset) for i in range(size)])]
  transfers between devices with their start and end apart: 20 -> 21, of which waited for: 13 -> 12; matrix products, arithmetic and copies ran while one was open for 1% -> 0% of each run, Pallas kernels for 0% -> 21%
where the time goes in v2:
time: 84.9 us; the launch traced here: 84.8 us
  Pallas kernels  40.6 us (48%)
  waiting for transfers between devices  21.7 us (26%)
  starting transfers between devices  20.4 us (24%)
  other arithmetic  1.14 us (1%)
    ppermute x21, waiting for transfers between devices, swap(): return lax.ppermute(array, axis, [(i, i ^ offset) for i in range(size)])  21.7 us
    ppermute x21, starting transfers between devices, swap(): return lax.ppermute(array, axis, [(i, i ^ offset) for i in range(size)])  20.4 us
    pallas_call x3, Pallas kernels, fetch(): pl.pallas_call(functools.partial(fetch_kernel, index=index, extras=len(ex...  14.3 us
    pallas_call x1, Pallas kernels, gate_up(): pl.pallas_call(functools.partial(gate_up_kernel, layout=tuple((len(parts)...  13 us
    pallas_call x2, Pallas kernels, down(): pl.pallas_call(functools.partial(down_kernel, first=first, part_cols=part...  6.5 us
    pallas_call x1, Pallas kernels, attend(): pl.pallas_call(functools.partial(attend_kernel, heads=heads, group=group)...  6.24 us
  transfers between devices with their start and end apart: 21, of which 12 were waited for; matrix products, arithmetic and copies ran while one was open for 0% of the time, Pallas kernels for 21%

profile of v2, /device:TPU:0, one launch (start us, length us, event | category | flops | bytes accessed | tf_op | source)
XLA Modules:
  0.0 84.8 jit_solution(17628395910846997791)
XLA Ops:
  0.0 0.0 copy-start
  0.0 0.7 copy-done
  0.7 6.2 %attend.1 = (bf16[24,1536]{1,0:T(8,128)(2,1)S(1)}, bf16[24,1536]{1,0:T(8,128)(2,1)S(1)}) custom-call(s32[24]{0:T(128)S(1)} %copy-done, bf16[24,1536]{1,0:T(8,128)(2,1)} %query_ref.1, bf16[24,2,256]{2,1,0:T(2,128)(2,1)} %new_ref.1, bf16[24,1536]{1,0:T(8,128)(2,1)} %resid_ref.1, bf16[24,2,256,256]{3,2,1,0:T(8,128)(2,1)} %cache_ref.1), custom_call_target="tpu_custom_call" | custom-call | bytes 6291456 | tf_op jit(solution)/shard_map/attend/pallas_call | solution.py:97
  6.9 5.1 %collective-permute-start.2 = (bf16[24,1536]{1,0:T(8,128)(2,1)S(1)}, bf16[24,1536]{1,0:T(8,128)(2,1)S(1)}, u32[]{:S(2)}, u32[]{:S(2)}) collective-permute-start(bf16[24,1536]{1,0:T(8,128)(2,1)S(1)} %get-tuple-element.31.after_ref.earlier_ref.rest_0_), channel_id=1, source_target_pairs={{0,3},{1,2},{2,1},{3,0},{4,7},{5,6},{6,5},{7,4},{8,11},{9,10},{10,... | collective-permute-start | bytes 221192 | tf_op jit(solution)/shard_map/ppermute | solution.py:405
  12.0 0.0 collective-permute-start.1
  12.0 0.6 collective-permute-start
  12.7 4.9 %fetch.3 = (bf16[6144,1024]{1,0:T(8,128)(2,1)S(1)}, f32[8,128]{1,0:T(8,128)S(1)}, f32[1,6144]{1,0:T(1,128)S(1)}, f32[8,6144]{1,0:T(8,128)S(1)}, s32[2,24]{1,0:T(2,128)S(1)}) custom-call(bf16[24,1536]{1,0:T(8,128)(2,1)S(1)} %get-tuple-element.31.after_ref.earlier_ref.rest_0_, bf16[24,1536]{1,0:T(8,128)(2,1)S(1)} %get-tuple-element.31.after_ref.earlier_ref.rest_0_, ...), custom_call_target="tpu_custom_call" | custom-call | bytes 12582912 | tf_op jit(solution)/shard_map/fetch/pallas_call | solution.py:144
  17.5 0.0 collective-permute-done.2.rest_3_
  17.5 0.7 collective-permute-done.1.rest_2_
  18.2 0.0 collective-permute-done.rest_1_
  18.2 0.6 norm.1.after_ref.rest_0_
  18.8 1.6 %collective-permute-start.4 = (bf16[24,6272]{1,0:T(8,128)(2,1)S(1)}, bf16[24,6272]{1,0:T(8,128)(2,1)S(1)}, u32[]{:S(2)}, u32[]{:S(2)}) collective-permute-start(bf16[24,6272]{1,0:T(8,128)(2,1)S(1)} %norm.1.after_ref.rest_0_), channel_id=1, source_target_pairs={{0,8},{4,12},{8,0},{12,4},{1,9},{5,13},{9,1},{13,5},{2,10},{6,14},... | collective-permute-start | bytes 903176 | tf_op jit(solution)/shard_map/ppermute | solution.py:405
  20.4 1.5 %collective-permute-start.3 = (bf16[24,6272]{1,0:T(8,128)(2,1)S(1)}, bf16[24,6272]{1,0:T(8,128)(2,1)S(1)}, u32[]{:S(2)}, u32[]{:S(2)}) collective-permute-start(bf16[24,6272]{1,0:T(8,128)(2,1)S(1)} %norm.1.after_ref.rest_0_), channel_id=1, source_target_pairs={{0,4},{4,0},{8,12},{12,8},{1,5},{5,1},{9,13},{13,9},{2,6},{6,2},{1... | collective-permute-start | bytes 903176 | tf_op jit(solution)/shard_map/ppermute | solution.py:405
  21.9 4.7 %fetch.4 = (bf16[1024,6144]{1,0:T(8,128)(2,1)S(1)}, f32[8,128]{1,0:T(8,128)S(1)}) custom-call(bf16[24,6272]{1,0:T(8,128)(2,1)S(1)} %norm.1.after_ref.rest_0_, f32[8,128]{1,0:T(8,128)S(1)} %get-tuple-element.35.earlier_ref, bf16[2,1024,6144]{2,1,0:T(8,128)(2,1)} %source_hbm.5), custom_call_target="tpu_custom_call" | custom-call | bytes 12582912 | tf_op jit(solution)/shard_map/fetch/pallas_call | solution.py:144
  26.6 0.8 collective-permute-done.4.first_ref.rest_2_
  27.4 1.4 %collective-permute-done.3.second_ref.rest_1_ = bf16[24,6272]{1,0:T(8,128)(2,1)S(1)} collective-permute-done((bf16[24,6272]{1,0:T(8,128)(2,1)S(1)}, bf16[24,6272]{1,0:T(8,128)(2,1)S(1)}, u32[]{:S(2)}, u32[]{:S(2)}) %collective-permute-start.3) | collective-permute-done | bytes 301088 | tf_op jit(solution)/shard_map/ppermute | solution.py:405
  28.8 0.4 collective-permute-start.6
  29.3 1.6 %collective-permute-start.5 = (bf16[24,3072]{1,0:T(8,128)(2,1)S(1)}, bf16[24,3072]{1,0:T(8,128)(2,1)S(1)}, u32[]{:S(2)}, u32[]{:S(2)}) collective-permute-start(bf16[24,3072]{1,0:T(8,128)(2,1)S(1)} %get-tuple-element.39.after_ref), channel_id=1, source_target_pairs={{0,4},{4,0},{8,12},{12,8},{1,5},{5,1},{9,13},{13,9},{2,6},{6,2},{1... | collective-permute-start | bytes 442376 | tf_op jit(solution)/shard_map/ppermute | solution.py:405
  30.9 0.0 collective-permute-start.7
  30.9 0.5 collective-permute-start.9
  31.4 0.0 collective-permute-start.8
  31.4 4.7 %fetch.5 = (bf16[1024,6144]{1,0:T(8,128)(2,1)S(1)}, f32[8,128]{1,0:T(8,128)S(1)}) custom-call(bf16[24,3072]{1,0:T(8,128)(2,1)S(1)} %get-tuple-element.39.after_ref, f32[8,128]{1,0:T(8,128)S(1)} %get-tuple-element.41.earlier_ref, bf16[2,1024,6144]{2,1,0:T(8,128)(2,1)} %source_hbm.5), custom_call_target="tpu_custom_call" | custom-call | bytes 12582912 | tf_op jit(solution)/shard_map/fetch/pallas_call | solution.py:144
  36.1 0.0 collective-permute-done.5.rest_3_
  36.1 0.0 collective-permute-done.6.rest_4_
  36.2 0.6 collective-permute-start.11
  36.7 0.1 collective-permute-start.10
  36.8 0.0 collective-permute-done.7.rest_5_
  36.8 0.0 collective-permute-done.9.rest_7_
  36.8 0.0 collective-permute-done.8.rest_6_
  36.8 1.3 %collective-permute-done.10.rest_8_ = bf16[24,3072]{1,0:T(8,128)(2,1)S(1)} collective-permute-done((bf16[24,3072]{1,0:T(8,128)(2,1)S(1)}, bf16[24,3072]{1,0:T(8,128)(2,1)S(1)}, u32[]{:S(2)}, u32[]{:S(2)}) %collective-permute-start.10) | collective-permute-done | bytes 147488 | tf_op jit(solution)/shard_map/ppermute | solution.py:405
  38.1 0.0 collective-permute-done.11.rest_9_
  38.1 13.0 %gate_up.1.act_ref = bf16[192,2048]{1,0:T(8,128)(2,1)S(1)} custom-call(bf16[2,6144,1024]{2,1,0:T(8,128)(2,1)} %gate_hbm.1, bf16[2,6144,1024]{2,1,0:T(8,128)(2,1)} %up_hbm.1, f32[8,128]{1,0:T(8,128)S(1)} %get-tuple-element.43.token_ref, bf16[6144,1024]{1,0:T(8,128)(2,1)S(1)} %get-tuple-element.44.gate_ref, bf16[24,6272]{1,0:T(8,128)(2,1)S(1)} %norm.1.after_ref.rest_0_, ...), custom_call_target="tpu_custom_call" | custom-call | flops 9663676416 | bytes 50331648 | tf_op jit(solution)/shard_map/gate_up/pallas_call | solution.py:335
  51.1 3.2 %down.2 = (bf16[96,3072]{1,0:T(8,128)(2,1)S(1)}, bf16[96,3072]{1,0:T(8,128)(2,1)S(1)}) custom-call(bf16[192,2048]{1,0:T(8,128)(2,1)S(1)} %gate_up.1.act_ref, bf16[1024,6144]{1,0:T(8,128)(2,1)S(1)} %get-tuple-element.48.rest_0_, bf16[1024,6144]{1,0:T(8,128)(2,1)S(1)} %get-tuple-element.49.rest_1_), custom_call_target="tpu_custom_call" | custom-call | flops 2415919104 | tf_op jit(solution)/shard_map/down/pallas_call | solution.py:386
  54.4 0.0 copy-start.1
  54.4 0.3 collective-permute-start.12
  54.7 3.3 %down.3 = (bf16[96,3072]{1,0:T(8,128)(2,1)S(1)}, bf16[96,3072]{1,0:T(8,128)(2,1)S(1)}) custom-call(bf16[192,2048]{1,0:T(8,128)(2,1)S(1)} %gate_up.1.act_ref, bf16[1024,6144]{1,0:T(8,128)(2,1)S(1)} %get-tuple-element.48.rest_0_, bf16[1024,6144]{1,0:T(8,128)(2,1)S(1)} %get-tuple-element.49.rest_1_), custom_call_target="tpu_custom_call" | custom-call | flops 2415919104 | tf_op jit(solution)/shard_map/down/pallas_call | solution.py:386
  58.0 0.3 collective-permute-start.13
  58.3 0.0 collective-permute-done.12
  58.3 0.1 convert_add_fusion.1
  58.4 0.5 collective-permute-start.16
  58.9 1.1 %collective-permute-done.13 = bf16[96,3072]{1,0:T(8,128)(2,1)S(1)} collective-permute-done((bf16[96,3072]{1,0:T(8,128)(2,1)S(1)}, bf16[96,3072]{1,0:T(8,128)(2,1)S(1)}, u32[]{:S(2)}, u32[]{:S(2)}) %collective-permute-start.13) | collective-permute-done | bytes 589856 | tf_op jit(solution)/shard_map/ppermute | solution.py:405
  60.1 0.1 convert_add_fusion
  60.2 1.6 %collective-permute-start.14 = (bf16[24,3072]{1,0:T(8,128)(2,1)S(1)}, bf16[24,3072]{1,0:T(8,128)(2,1)S(1)}, u32[]{:S(2)}, u32[]{:S(2)}) collective-permute-start(bf16[24,3072]{1,0:T(8,128)(2,1)S(1)} %get-tuple-element.62), channel_id=1, source_target_pairs={{0,8},{4,12},{8,0},{12,4},{1,9},{5,13},{9,1},{13,5},{2,10},{6,14},... | collective-permute-start | bytes 442376 | tf_op jit(solution)/shard_map/ppermute | solution.py:405
  61.7 2.7 %collective-permute-done.16 = bf16[24,3072]{1,0:T(8,128)(2,1)S(1)} collective-permute-done((bf16[24,3072]{1,0:T(8,128)(2,1)S(1)}, bf16[24,3072]{1,0:T(8,128)(2,1)S(1)}, u32[]{:S(2)}, u32[]{:S(2)}) %collective-permute-start.16) | collective-permute-done | bytes 147488 | tf_op jit(solution)/shard_map/ppermute | solution.py:405
  64.5 0.1 add_convert_fusion.1
  64.6 1.6 %collective-permute-start.17 = (bf16[24,6144]{1,0:T(8,128)(2,1)S(1)}, bf16[24,6144]{1,0:T(8,128)(2,1)S(1)}, u32[]{:S(2)}, u32[]{:S(2)}) collective-permute-start(bf16[24,6144]{1,0:T(8,128)(2,1)S(1)} %pad_maximum_fusion.1), channel_id=1, source_target_pairs={{0,8},{4,12},{8,0},{12,4},{1,9},{5,13},{9,1},{13,5},{2,10},{6,14},... | collective-permute-start | bytes 884744 | tf_op jit(solution)/shard_map/ppermute | solution.py:405
  66.2 0.1 collective-permute-done.14
  66.2 0.1 add_convert_fusion.3
  66.3 0.5 collective-permute-start.15
  66.8 6.1 %collective-permute-done.17 = bf16[24,6144]{1,0:T(8,128)(2,1)S(1)} collective-permute-done((bf16[24,6144]{1,0:T(8,128)(2,1)S(1)}, bf16[24,6144]{1,0:T(8,128)(2,1)S(1)}, u32[]{:S(2)}, u32[]{:S(2)}) %collective-permute-start.17) | collective-permute-done | bytes 294944 | tf_op jit(solution)/shard_map/ppermute | solution.py:405
  73.0 1.8 %collective-permute-done.15 = bf16[24,6144]{1,0:T(8,128)(2,1)S(1)} collective-permute-done((bf16[24,6144]{1,0:T(8,128)(2,1)S(1)}, bf16[24,6144]{1,0:T(8,128)(2,1)S(1)}, u32[]{:S(2)}, u32[]{:S(2)}) %collective-permute-start.15) | collective-permute-done | bytes 294944 | tf_op jit(solution)/shard_map/ppermute | solution.py:405
  74.8 0.1 fusion.5
  74.9 0.5 collective-permute-start.18
  75.4 2.3 %collective-permute-start.20 = (bf16[24,1536]{1,0:T(8,128)(2,1)S(1)}, bf16[24,1536]{1,0:T(8,128)(2,1)S(1)}, u32[]{:S(2)}, u32[]{:S(2)}) collective-permute-start(bf16[24,1536]{1,0:T(8,128)(2,1)S(1)} %get-tuple-element.64), channel_id=1, source_target_pairs={{0,3},{1,2},{2,1},{3,0},{4,7},{5,6},{6,5},{7,4},{8,11},{9,10},{10,... | collective-permute-start | bytes 221192 | tf_op jit(solution)/shard_map/ppermute | solution.py:405
  77.7 0.8 collective-permute-start.19
  78.4 1.6 %collective-permute-done.18 = bf16[24,1536]{1,0:T(8,128)(2,1)S(1)} collective-permute-done((bf16[24,1536]{1,0:T(8,128)(2,1)S(1)}, bf16[24,1536]{1,0:T(8,128)(2,1)S(1)}, u32[]{:S(2)}, u32[]{:S(2)}) %collective-permute-start.18) | collective-permute-done | bytes 73760 | tf_op jit(solution)/shard_map/ppermute | solution.py:405
  80.1 1.6 %collective-permute-done.20 = bf16[24,1536]{1,0:T(8,128)(2,1)S(1)} collective-permute-done((bf16[24,1536]{1,0:T(8,128)(2,1)S(1)}, bf16[24,1536]{1,0:T(8,128)(2,1)S(1)}, u32[]{:S(2)}, u32[]{:S(2)}) %collective-permute-start.20) | collective-permute-done | bytes 73760 | tf_op jit(solution)/shard_map/ppermute | solution.py:405
  81.7 2.4 %collective-permute-done.19 = bf16[24,1536]{1,0:T(8,128)(2,1)S(1)} collective-permute-done((bf16[24,1536]{1,0:T(8,128)(2,1)S(1)}, bf16[24,1536]{1,0:T(8,128)(2,1)S(1)}, u32[]{:S(2)}, u32[]{:S(2)}) %collective-permute-start.19) | collective-permute-done | bytes 73760 | tf_op jit(solution)/shard_map/ppermute | solution.py:405
  84.1 0.0 copy-done.1
  84.1 0.7 fusion.4
  (4 shorter events, 0.1 us)
Async XLA Ops:
  0.0 0.7 copy-start
  6.9 10.6 %collective-permute-start.2 = (bf16[24,1536]{1,0:T(8,128)(2,1)S(1)}, bf16[24,1536]{1,0:T(8,128)(2,1)S(1)}, u32[]{:S(2)}, u32[]{:S(2)}) collective-permute-start(bf16[24,1536]{1,0:T(8,128)(2,1)S(1)} %get-tuple-element.31.after_ref.earlier_ref.rest_0_), channel_id=1, source_target_pairs={{0,3},{1,2},{2,1},{3,0},{4,7},{5,6},{6,5},{7,4},{8,11},{9,10},{10,... | collective-permute-start | bytes 221192 | tf_op jit(solution)/shard_map/ppermute | solution.py:405
  12.0 6.2 %collective-permute-start.1 = (bf16[24,1536]{1,0:T(8,128)(2,1)S(1)}, bf16[24,1536]{1,0:T(8,128)(2,1)S(1)}, u32[]{:S(2)}, u32[]{:S(2)}) collective-permute-start(bf16[24,1536]{1,0:T(8,128)(2,1)S(1)} %get-tuple-element.31.after_ref.earlier_ref.rest_0_), channel_id=1, source_target_pairs={{0,2},{1,3},{2,0},{3,1},{4,6},{5,7},{6,4},{7,5},{8,10},{9,11},{10,... | collective-permute-start | bytes 221192 | tf_op jit(solution)/shard_map/ppermute | solution.py:405
  12.0 6.2 %collective-permute-start = (bf16[24,1536]{1,0:T(8,128)(2,1)S(1)}, bf16[24,1536]{1,0:T(8,128)(2,1)S(1)}, u32[]{:S(2)}, u32[]{:S(2)}) collective-permute-start(bf16[24,1536]{1,0:T(8,128)(2,1)S(1)} %get-tuple-element.31.after_ref.earlier_ref.rest_0_), channel_id=1, source_target_pairs={{0,1},{1,0},{2,3},{3,2},{4,5},{5,4},{6,7},{7,6},{8,9},{9,8},{10,11... | collective-permute-start | bytes 221192 | tf_op jit(solution)/shard_map/ppermute | solution.py:405
  18.8 8.6 %collective-permute-start.4 = (bf16[24,6272]{1,0:T(8,128)(2,1)S(1)}, bf16[24,6272]{1,0:T(8,128)(2,1)S(1)}, u32[]{:S(2)}, u32[]{:S(2)}) collective-permute-start(bf16[24,6272]{1,0:T(8,128)(2,1)S(1)} %norm.1.after_ref.rest_0_), channel_id=1, source_target_pairs={{0,8},{4,12},{8,0},{12,4},{1,9},{5,13},{9,1},{13,5},{2,10},{6,14},... | collective-permute-start | bytes 903176 | tf_op jit(solution)/shard_map/ppermute | solution.py:405
  20.4 8.4 %collective-permute-start.3 = (bf16[24,6272]{1,0:T(8,128)(2,1)S(1)}, bf16[24,6272]{1,0:T(8,128)(2,1)S(1)}, u32[]{:S(2)}, u32[]{:S(2)}) collective-permute-start(bf16[24,6272]{1,0:T(8,128)(2,1)S(1)} %norm.1.after_ref.rest_0_), channel_id=1, source_target_pairs={{0,4},{4,0},{8,12},{12,8},{1,5},{5,1},{9,13},{13,9},{2,6},{6,2},{1... | collective-permute-start | bytes 903176 | tf_op jit(solution)/shard_map/ppermute | solution.py:405
  28.8 7.3 %collective-permute-start.6 = (bf16[24,3200]{1,0:T(8,128)(2,1)S(1)}, bf16[24,3200]{1,0:T(8,128)(2,1)S(1)}, u32[]{:S(2)}, u32[]{:S(2)}) collective-permute-start(bf16[24,3200]{1,0:T(8,128)(2,1)S(1)} %get-tuple-element.40), channel_id=1, source_target_pairs={{0,8},{4,12},{8,0},{12,4},{1,9},{5,13},{9,1},{13,5},{2,10},{6,14},... | collective-permute-start | bytes 460808 | tf_op jit(solution)/shard_map/ppermute | solution.py:405
  29.3 6.9 %collective-permute-start.5 = (bf16[24,3072]{1,0:T(8,128)(2,1)S(1)}, bf16[24,3072]{1,0:T(8,128)(2,1)S(1)}, u32[]{:S(2)}, u32[]{:S(2)}) collective-permute-start(bf16[24,3072]{1,0:T(8,128)(2,1)S(1)} %get-tuple-element.39.after_ref), channel_id=1, source_target_pairs={{0,4},{4,0},{8,12},{12,8},{1,5},{5,1},{9,13},{13,9},{2,6},{6,2},{1... | collective-permute-start | bytes 442376 | tf_op jit(solution)/shard_map/ppermute | solution.py:405
  30.9 5.9 %collective-permute-start.7 = (bf16[24,6272]{1,0:T(8,128)(2,1)S(1)}, bf16[24,6272]{1,0:T(8,128)(2,1)S(1)}, u32[]{:S(2)}, u32[]{:S(2)}) collective-permute-start(bf16[24,6272]{1,0:T(8,128)(2,1)S(1)} %norm.1.after_ref.rest_0_), channel_id=1, source_target_pairs={{0,16},{16,0},{1,17},{17,1},{2,18},{18,2},{3,19},{19,3},{4,20},{20... | collective-permute-start | bytes 903176 | tf_op jit(solution)/shard_map/ppermute | solution.py:405
  30.9 5.9 %collective-permute-start.9 = (bf16[24,6272]{1,0:T(8,128)(2,1)S(1)}, bf16[24,6272]{1,0:T(8,128)(2,1)S(1)}, u32[]{:S(2)}, u32[]{:S(2)}) collective-permute-start(bf16[24,6272]{1,0:T(8,128)(2,1)S(1)} %collective-permute-done.4.first_ref.rest_2_), channel_id=1, source_target_pairs={{0,16},{16,0},{1,17},{17,1},{2,18},{18,2},{3,19},{19,3},{4,20},{20... | collective-permute-start | bytes 903176 | tf_op jit(solution)/shard_map/ppermute | solution.py:405
  31.4 5.4 %collective-permute-start.8 = (bf16[24,6272]{1,0:T(8,128)(2,1)S(1)}, bf16[24,6272]{1,0:T(8,128)(2,1)S(1)}, u32[]{:S(2)}, u32[]{:S(2)}) collective-permute-start(bf16[24,6272]{1,0:T(8,128)(2,1)S(1)} %collective-permute-done.3.second_ref.rest_1_), channel_id=1, source_target_pairs={{0,16},{16,0},{1,17},{17,1},{2,18},{18,2},{3,19},{19,3},{4,20},{20... | collective-permute-start | bytes 903176 | tf_op jit(solution)/shard_map/ppermute | solution.py:405
  36.2 1.9 %collective-permute-start.11 = (bf16[24,3200]{1,0:T(8,128)(2,1)S(1)}, bf16[24,3200]{1,0:T(8,128)(2,1)S(1)}, u32[]{:S(2)}, u32[]{:S(2)}) collective-permute-start(bf16[24,3200]{1,0:T(8,128)(2,1)S(1)} %collective-permute-done.6.rest_4_), channel_id=1, source_target_pairs={{0,16},{16,0},{1,17},{17,1},{2,18},{18,2},{3,19},{19,3},{4,20},{20... | collective-permute-start | bytes 460808 | tf_op jit(solution)/shard_map/ppermute | solution.py:405
  36.7 1.4 %collective-permute-start.10 = (bf16[24,3072]{1,0:T(8,128)(2,1)S(1)}, bf16[24,3072]{1,0:T(8,128)(2,1)S(1)}, u32[]{:S(2)}, u32[]{:S(2)}) collective-permute-start(bf16[24,3072]{1,0:T(8,128)(2,1)S(1)} %collective-permute-done.5.rest_3_), channel_id=1, source_target_pairs={{0,16},{16,0},{1,17},{17,1},{2,18},{18,2},{3,19},{19,3},{4,20},{20... | collective-permute-start | bytes 442376 | tf_op jit(solution)/shard_map/ppermute | solution.py:405
  54.4 29.7 %copy-start.1 = (bf16[24,1536]{1,0:T(8,128)(2,1)S(1)}, bf16[24,1536]{1,0:T(8,128)(2,1)}, u32[]{:S(2)}) copy-start(bf16[24,1536]{1,0:T(8,128)(2,1)} %resid_ref.1) | copy-start | bytes 221188
  54.4 3.9 %collective-permute-start.12 = (bf16[96,3072]{1,0:T(8,128)(2,1)S(1)}, bf16[96,3072]{1,0:T(8,128)(2,1)S(1)}, u32[]{:S(2)}, u32[]{:S(2)}) collective-permute-start(bf16[96,3072]{1,0:T(8,128)(2,1)S(1)} %get-tuple-element.51), channel_id=1, source_target_pairs={{0,16},{16,0},{1,17},{17,1},{2,18},{18,2},{3,19},{19,3},{4,20},{20... | collective-permute-start | bytes 1769480 | tf_op jit(solution)/shard_map/ppermute | solution.py:405
  58.0 2.1 %collective-permute-start.13 = (bf16[96,3072]{1,0:T(8,128)(2,1)S(1)}, bf16[96,3072]{1,0:T(8,128)(2,1)S(1)}, u32[]{:S(2)}, u32[]{:S(2)}) collective-permute-start(bf16[96,3072]{1,0:T(8,128)(2,1)S(1)} %get-tuple-element.54), channel_id=1, source_target_pairs={{0,16},{16,0},{1,17},{17,1},{2,18},{18,2},{3,19},{19,3},{4,20},{20... | collective-permute-start | bytes 1769480 | tf_op jit(solution)/shard_map/ppermute | solution.py:405
  58.4 6.1 %collective-permute-start.16 = (bf16[24,3072]{1,0:T(8,128)(2,1)S(1)}, bf16[24,3072]{1,0:T(8,128)(2,1)S(1)}, u32[]{:S(2)}, u32[]{:S(2)}) collective-permute-start(bf16[24,3072]{1,0:T(8,128)(2,1)S(1)} %get-tuple-element.58), channel_id=1, source_target_pairs={{0,4},{4,0},{8,12},{12,8},{1,5},{5,1},{9,13},{13,9},{2,6},{6,2},{1... | collective-permute-start | bytes 442376 | tf_op jit(solution)/shard_map/ppermute | solution.py:405
  60.2 6.1 %collective-permute-start.14 = (bf16[24,3072]{1,0:T(8,128)(2,1)S(1)}, bf16[24,3072]{1,0:T(8,128)(2,1)S(1)}, u32[]{:S(2)}, u32[]{:S(2)}) collective-permute-start(bf16[24,3072]{1,0:T(8,128)(2,1)S(1)} %get-tuple-element.62), channel_id=1, source_target_pairs={{0,8},{4,12},{8,0},{12,4},{1,9},{5,13},{9,1},{13,5},{2,10},{6,14},... | collective-permute-start | bytes 442376 | tf_op jit(solution)/shard_map/ppermute | solution.py:405
  64.6 8.4 %collective-permute-start.17 = (bf16[24,6144]{1,0:T(8,128)(2,1)S(1)}, bf16[24,6144]{1,0:T(8,128)(2,1)S(1)}, u32[]{:S(2)}, u32[]{:S(2)}) collective-permute-start(bf16[24,6144]{1,0:T(8,128)(2,1)S(1)} %pad_maximum_fusion.1), channel_id=1, source_target_pairs={{0,8},{4,12},{8,0},{12,4},{1,9},{5,13},{9,1},{13,5},{2,10},{6,14},... | collective-permute-start | bytes 884744 | tf_op jit(solution)/shard_map/ppermute | solution.py:405
  66.3 8.4 %collective-permute-start.15 = (bf16[24,6144]{1,0:T(8,128)(2,1)S(1)}, bf16[24,6144]{1,0:T(8,128)(2,1)S(1)}, u32[]{:S(2)}, u32[]{:S(2)}) collective-permute-start(bf16[24,6144]{1,0:T(8,128)(2,1)S(1)} %pad_maximum_fusion), channel_id=1, source_target_pairs={{0,4},{4,0},{8,12},{12,8},{1,5},{5,1},{9,13},{13,9},{2,6},{6,2},{1... | collective-permute-start | bytes 884744 | tf_op jit(solution)/shard_map/ppermute | solution.py:405
  74.9 5.2 %collective-permute-start.18 = (bf16[24,1536]{1,0:T(8,128)(2,1)S(1)}, bf16[24,1536]{1,0:T(8,128)(2,1)S(1)}, u32[]{:S(2)}, u32[]{:S(2)}) collective-permute-start(bf16[24,1536]{1,0:T(8,128)(2,1)S(1)} %get-tuple-element.63), channel_id=1, source_target_pairs={{0,1},{1,0},{2,3},{3,2},{4,5},{5,4},{6,7},{7,6},{8,9},{9,8},{10,11... | collective-permute-start | bytes 221192 | tf_op jit(solution)/shard_map/ppermute | solution.py:405
  75.4 6.3 %collective-permute-start.20 = (bf16[24,1536]{1,0:T(8,128)(2,1)S(1)}, bf16[24,1536]{1,0:T(8,128)(2,1)S(1)}, u32[]{:S(2)}, u32[]{:S(2)}) collective-permute-start(bf16[24,1536]{1,0:T(8,128)(2,1)S(1)} %get-tuple-element.64), channel_id=1, source_target_pairs={{0,3},{1,2},{2,1},{3,0},{4,7},{5,6},{6,5},{7,4},{8,11},{9,10},{10,... | collective-permute-start | bytes 221192 | tf_op jit(solution)/shard_map/ppermute | solution.py:405
  77.7 6.4 %collective-permute-start.19 = (bf16[24,1536]{1,0:T(8,128)(2,1)S(1)}, bf16[24,1536]{1,0:T(8,128)(2,1)S(1)}, u32[]{:S(2)}, u32[]{:S(2)}) collective-permute-start(bf16[24,1536]{1,0:T(8,128)(2,1)S(1)} %get-tuple-element.65), channel_id=1, source_target_pairs={{0,2},{1,3},{2,0},{3,1},{4,6},{5,7},{6,4},{7,5},{8,10},{9,11},{10,... | collective-permute-start | bytes 221192 | tf_op jit(solution)/shard_map/ppermute | solution.py:405

commit v3 on v2

--- a/solution.py
+++ b/solution.py
@@ -20,113 +20,162 @@
     return next(c for c in choices if total % c == 0)
 
 
-def attend_kernel(lengths_ref, query_ref, new_ref, resid_ref, cache_ref, attended_ref, hidden_ref, *, heads, group):
-    step = pl.program_id(0)
+def attend_kernel(
+    lengths_hbm, query_hbm, new_hbm, resid_hbm, cache_hbm, *rest, extras, kv_local, group
+):
+    extra_hbm, rest = rest[:extras], rest[extras:]
+    (attended_ref, hidden_ref), extra_refs, rest = rest[:2], rest[2 : 2 + extras], rest[2 + extras :]
+    lengths_ref, query_ref, new_ref, resid_ref, cache_ref, query_buf, output_buf, *sems = rest
+    small_sem, cache_sem, extra_sem = sems
     rows = ROWS_STEP
+    blocks = query_ref.shape[0] // rows
     cache_len = cache_ref.shape[2]
+    stacked = group * rows
     factor = 1.0 / math.sqrt(HEAD_DIM)
-    for kv_head, lead, count in heads:
-        stacked = count * rows
-        row_of = lax.broadcasted_iota(jnp.int32, (stacked, 1), 0) % rows
+
+    def cache_copy(b, kind):
+        span = pl.ds(b * rows, rows)
+        return pltpu.make_async_copy(
+            cache_hbm.at[span, kind], cache_ref.at[span, kind], cache_sem.at[kind, b]
+        )
+
+    pairs = ((query_hbm, query_ref), (lengths_hbm, lengths_ref), (new_hbm, new_ref), (resid_hbm, resid_ref))
+    small = [pltpu.make_async_copy(*pair, small_sem.at[i]) for i, pair in enumerate(pairs)]
+    later = [
+        pltpu.make_async_copy(*pair, extra_sem.at[i]) for i, pair in enumerate(zip(extra_hbm, extra_refs))
+    ]
+    for copy in small:
+        copy.start()
+    for b in range(blocks):
+        for kind in range(2):
+            cache_copy(b, kind).start()
+    for copy in later:
+        copy.start()
+    small[0].wait()
+    for head in range(kv_local):
+        for b in range(blocks):
+            query_buf[head, b] = jnp.concatenate(
+                [
+                    query_ref[pl.ds(b * rows, rows), pl.ds((head * group + g) * HEAD_DIM, HEAD_DIM)]
+                    for g in range(group)
+                ],
+                axis=0,
+            )
+    row_of = lax.broadcasted_iota(jnp.int32, (stacked, 1), 0) % rows
+
+    def lanes_of(head):
+        return pl.ds(head * HEAD_DIM, HEAD_DIM)
+
+    def block(b, carry):
+        span = pl.ds(pl.multiple_of(b * rows, rows), rows)
         length_col = jnp.zeros((stacked, 1), jnp.int32)
         for n in range(rows):
-            length_col = jnp.where(row_of == n, lengths_ref[step * rows + n], length_col)
+            length_col = jnp.where(row_of == n, lengths_ref[b * rows + n], length_col)
         valid = lax.broadcasted_iota(jnp.int32, (stacked, cache_len), 1) < length_col
-        lanes = pl.ds(kv_head * HEAD_DIM, HEAD_DIM)
-        columns = [pl.ds((lead + g) * HEAD_DIM, HEAD_DIM) for g in range(count)]
-        query = jnp.concatenate([query_ref[:, c].astype(jnp.float32) for c in columns], axis=0)
-        query_bf = query.astype(jnp.bfloat16)
-        new_key = new_ref[:, 0, lanes].astype(jnp.float32)
-        new_value = new_ref[:, 1, lanes].astype(jnp.float32)
-        scores = jnp.zeros((stacked, cache_len), jnp.float32)
-        for n in range(rows):
-            full = lax.dot_general(
-                query_bf,
-                cache_ref[n, 0, :, lanes],
-                (((1,), (1,)), ((), ())),
-                preferred_element_type=jnp.float32,
+        cache_copy(b, 0).wait()
+        scores = []
+        for head in range(kv_local):
+            query = query_buf[head, b]
+            total = jnp.zeros((stacked, cache_len), jnp.float32)
+            for n in range(rows):
+                full = lax.dot_general(
+                    query,
+                    cache_ref[b * rows + n, 0, :, lanes_of(head)],
+                    (((1,), (1,)), ((), ())),
+                    preferred_element_type=jnp.float32,
+                )
+                total = jnp.where(row_of == n, full, total)
+            scores.append(jnp.where(valid, total * factor, -jnp.inf))
+        chances = []
+        for head in range(kv_local):
+            new_key = new_ref[span, 0, lanes_of(head)].astype(jnp.float32)
+            query = query_buf[head, b].astype(jnp.float32)
+            fresh = (
+                jnp.sum(query * jnp.concatenate([new_key] * group, axis=0), axis=1, keepdims=True) * factor
             )
-            scores = jnp.where(row_of == n, full, scores)
-        scores = jnp.where(valid, scores * factor, -jnp.inf)
-        fresh = (
-            jnp.sum(query * jnp.concatenate([new_key] * count, axis=0), axis=1, keepdims=True) * factor
-        )
-        largest = jnp.maximum(jnp.max(scores, axis=1, keepdims=True), fresh)
-        weights = jnp.exp(scores - largest)
-        fresh_weight = jnp.exp(fresh - largest)
-        denominator = jnp.sum(weights, axis=1, keepdims=True) + fresh_weight
-        probabilities = (weights / denominator).astype(jnp.bfloat16)
-        fresh_prob = (fresh_weight / denominator).astype(jnp.bfloat16).astype(jnp.float32)
-        output = jnp.zeros((stacked, HEAD_DIM), jnp.float32)
-        for n in range(rows):
-            full = jnp.dot(
-                probabilities, cache_ref[n, 1, :, lanes], preferred_element_type=jnp.float32
-            )
-            output = jnp.where(row_of == n, full, output)
-        output = output + fresh_prob * jnp.concatenate([new_value] * count, axis=0)
-        for g, c in enumerate(columns):
-            piece = output[g * rows : (g + 1) * rows].astype(jnp.bfloat16)
-            attended_ref[:, c] = piece
-            hidden_ref[:, c] = (
-                resid_ref[:, c].astype(jnp.float32) + piece.astype(jnp.float32)
+            largest = jnp.maximum(jnp.max(scores[head], axis=1, keepdims=True), fresh)
+            weights = jnp.exp(scores[head] - largest)
+            fresh_weight = jnp.exp(fresh - largest)
+            denominator = jnp.sum(weights, axis=1, keepdims=True) + fresh_weight
+            probabilities = (weights / denominator).astype(jnp.bfloat16)
+            fresh_prob = (fresh_weight / denominator).astype(jnp.bfloat16).astype(jnp.float32)
+            chances.append((probabilities, fresh_prob))
+        cache_copy(b, 1).wait()
+        for head in range(kv_local):
+            probabilities, fresh_prob = chances[head]
+            new_value = new_ref[span, 1, lanes_of(head)].astype(jnp.float32)
+            output = jnp.zeros((stacked, HEAD_DIM), jnp.float32)
+            for n in range(rows):
+                full = jnp.dot(
+                    probabilities,
+                    cache_ref[b * rows + n, 1, :, lanes_of(head)],
+                    preferred_element_type=jnp.float32,
+                )
+                output = jnp.where(row_of == n, full, output)
+            output_buf[head, b] = output + fresh_prob * jnp.concatenate([new_value] * group, axis=0)
+        return carry
+
+    for copy in small[1:]:
+        copy.wait()
+    lax.fori_loop(0, blocks, block, 0)
+    for head in range(kv_local):
+        for g in range(group):
+            columns = pl.ds((head * group + g) * HEAD_DIM, HEAD_DIM)
+            piece = jnp.concatenate(
+                [output_buf[head, b, pl.ds(g * rows, rows)] for b in range(blocks)], axis=0
             ).astype(jnp.bfloat16)
-
-
-def attend(lengths, queries, new_kv, resid_in, cache, chunk, chunks):
+            attended_ref[:, columns] = piece
+            hidden_ref[:, columns] = (
+                resid_ref[:, columns].astype(jnp.float32) + piece.astype(jnp.float32)
+            ).astype(jnp.bfloat16)
+    for copy in later:
+        copy.wait()
+
+
+def attend(lengths, queries, new_kv, resid_in, cache, extra):
     sequences, part_cols = queries.shape
     cache_len, kv_cols = cache.shape[2:]
     kv_local = kv_cols // HEAD_DIM
     group = part_cols // kv_cols
-    rows = ROWS_STEP
-    width = part_cols // chunks
-    count = width // HEAD_DIM
-    lead = chunk * count
-    spans = [
-        (kv, max(kv * group, lead), min((kv + 1) * group, lead + count)) for kv in range(kv_local)
-    ]
-    spans = [span for span in spans if span[1] < span[2]]
-    first_kv = spans[0][0]
-    lanes = (spans[-1][0] - first_kv + 1) * HEAD_DIM
-    assert kv_cols % lanes == 0 and first_kv * HEAD_DIM % lanes == 0
-    heads = [(kv - first_kv, start - lead, stop - start) for kv, start, stop in spans]
-    block = first_kv * HEAD_DIM // lanes
-
-    def flat(index):
-        return pl.BlockSpec((rows, width), lambda i, _: (i, index))
-
+    blocks = sequences // ROWS_STEP
+    stacked = group * ROWS_STEP
+    hbm = pl.BlockSpec(memory_space=pltpu.HBM)
+    vmem = pl.BlockSpec(memory_space=pltpu.VMEM)
+    far = [pin(a, pltpu.HBM) for a in (lengths, queries, new_kv, resid_in, cache, *extra)]
     return pl.pallas_call(
-        functools.partial(attend_kernel, heads=heads, group=group),
-        grid_spec=pltpu.PrefetchScalarGridSpec(
-            num_scalar_prefetch=1,
-            grid=(sequences // rows,),
-            in_specs=[
-                flat(chunk),
-                pl.BlockSpec((rows, 2, lanes), lambda i, _: (i, 0, block)),
-                flat(chunk),
-                pl.BlockSpec((rows, 2, cache_len, lanes), lambda i, _: (i, 0, 0, block)),
-            ],
-            out_specs=[flat(0)] * 2,
+        functools.partial(attend_kernel, extras=len(extra), kv_local=kv_local, group=group),
+        in_specs=[hbm] * len(far),
+        out_specs=[vmem] * (2 + len(extra)),
+        out_shape=[pltpu.VMEM((sequences, part_cols), jnp.bfloat16)] * 2
+        + [pltpu.VMEM(array.shape, array.dtype) for array in extra],
+        scratch_shapes=[
+            pltpu.SMEM(lengths.shape, lengths.dtype),
+            pltpu.VMEM(queries.shape, queries.dtype),
+            pltpu.VMEM(new_kv.shape, new_kv.dtype),
+            pltpu.VMEM(resid_in.shape, resid_in.dtype),
+            pltpu.VMEM(cache.shape, cache.dtype),
+            pltpu.VMEM((kv_local, blocks, stacked, HEAD_DIM), jnp.bfloat16),
+            pltpu.VMEM((kv_local, blocks, stacked, HEAD_DIM), jnp.float32),
+            pltpu.SemaphoreType.DMA((4,)),
+            pltpu.SemaphoreType.DMA((2, blocks)),
+            pltpu.SemaphoreType.DMA((len(extra),)),
+        ],
+        cost_estimate=pl.CostEstimate(
+            flops=0, bytes_accessed=2 * cache.size, transcendentals=0
         ),
-        out_shape=[jax.ShapeDtypeStruct((sequences, width), jnp.bfloat16)] * 2,
-        cost_estimate=pl.CostEstimate(
-            flops=0, bytes_accessed=2 * cache.size // chunks, transcendentals=0
-        ),
-        compiler_params=pltpu.CompilerParams(vmem_limit_bytes=32 * MIB),
+        compiler_params=pltpu.CompilerParams(vmem_limit_bytes=16 * MIB),
         name="attend",
-    )(lengths, *(pin(array, pltpu.HBM) for array in (queries, new_kv, resid_in, cache)))
-
-
-def fetch_kernel(after_ref, earlier_ref, source_hbm, *rest, index, extras):
-    extra_hbm, (target_ref, token_ref, *extra_refs, sem) = rest[:extras], rest[extras:]
-    pieces = sem.shape[0] - extras
+    )(*far)
+
+
+def fetch_kernel(after_ref, earlier_ref, source_hbm, target_ref, token_ref, sem, *, index, first):
+    pieces = sem.shape[0]
     step = target_ref.shape[0] // pieces
     copies = [
-        pltpu.make_async_copy(source, target, sem.at[pieces + i])
-        for i, (source, target) in enumerate(zip(extra_hbm, extra_refs))
-    ]
-    copies += [
         pltpu.make_async_copy(
-            source_hbm.at[index, pl.ds(i * step, step)], target_ref.at[pl.ds(i * step, step)], sem.at[i]
+            source_hbm.at[index, pl.ds(first + i * step, step)],
+            target_ref.at[pl.ds(i * step, step)],
+            sem.at[i],
         )
         for i in range(pieces)
     ]
@@ -137,21 +186,19 @@
         copy.wait()
 
 
-def fetch(after, earlier, weights, index, extra=()):
-    shape = weights.shape[1:]
-    pieces = 8
-    hbm = pl.BlockSpec(memory_space=pltpu.HBM)
+def fetch(after, earlier, weights, index, first, rows):
+    shape = (rows, weights.shape[2])
+    pieces = 4
     return pl.pallas_call(
-        functools.partial(fetch_kernel, index=index, extras=len(extra)),
-        in_specs=[pl.BlockSpec(memory_space=pl.ANY)] * 2 + [hbm] * (1 + len(extra)),
-        out_specs=[pl.BlockSpec(memory_space=pltpu.VMEM)] * (2 + len(extra)),
-        out_shape=[pltpu.VMEM(shape, weights.dtype), pltpu.VMEM((8, 128), jnp.float32)]
-        + [pltpu.VMEM(array.shape, array.dtype) for array in extra],
-        scratch_shapes=[pltpu.SemaphoreType.DMA((pieces + len(extra),))],
+        functools.partial(fetch_kernel, index=index, first=first),
+        in_specs=[pl.BlockSpec(memory_space=pl.ANY)] * 2 + [pl.BlockSpec(memory_space=pltpu.HBM)],
+        out_specs=[pl.BlockSpec(memory_space=pltpu.VMEM)] * 2,
+        out_shape=[pltpu.VMEM(shape, weights.dtype), pltpu.VMEM((8, 128), jnp.float32)],
+        scratch_shapes=[pltpu.SemaphoreType.DMA((pieces,))],
         cost_estimate=pl.CostEstimate(flops=0, bytes_accessed=2 * math.prod(shape), transcendentals=0),
         compiler_params=pltpu.CompilerParams(vmem_limit_bytes=1 * MIB),
         name="fetch",
-    )(after, earlier, *(pin(array, pltpu.HBM) for array in (weights, *extra)))
+    )(after, earlier, pin(weights, pltpu.HBM))
 
 
 def norm_kernel(gain_ref, router_ref, ids_ref, *rest):
@@ -359,7 +406,7 @@
 
 def down_kernel(act_ref, *rest, first, part_cols, cuts):
     down_refs, (own_ref, other_ref) = rest[:-2], rest[-2:]
-    ff = down_refs[0].shape[0]
+    starts = [sum(ref.shape[0] for ref in down_refs[:i]) for i in range(len(down_refs))]
     half = own_ref.shape[0]
     nb = part_cols // cuts
     tp = lax.axis_index("tp")
@@ -368,8 +415,10 @@
         j = first + i // cuts
         there = pl.ds(pl.multiple_of((j ^ tp) * part_cols + i % cuts * nb, 128), nb)
         partial = sum(
-            jnp.dot(act_ref[:, pl.ds(e * ff, ff)], ref[:, there], preferred_element_type=jnp.float32)
-            for e, ref in enumerate(down_refs)
+            jnp.dot(
+                act_ref[:, pl.ds(start, ref.shape[0])], ref[:, there], preferred_element_type=jnp.float32
+            )
+            for start, ref in zip(starts, down_refs)
         )
         columns = pl.ds(pl.multiple_of(i * nb, 128), nb)
         own_ref[:, columns] = partial[:half].astype(jnp.bfloat16)
@@ -413,19 +462,28 @@
     held = w_gate.shape[0]
     blocks_held = max(1, grps * held // router.shape[1])
     tie = lax.optimization_barrier
-    attended, hidden = attend(lengths, queries, new_kv, resid_in, cache, 0, 1)
+    attended, hidden, gain, router_rows, ids = attend(
+        lengths, queries, new_kv, resid_in, cache, (norm_gain.reshape(1, -1), router.T, route_ids.T)
+    )
+
+    ff = w_down.shape[1]
+    spans = [(e, 0, ff) for e in range(held - 1)]
+    spans += [(held - 1, 0, ff // 4), (held - 1, ff // 4, ff - ff // 4)]
+    down_ready = []
+
+    def fetch_down(after, token, count):
+        for e, first, rows in spans[len(down_ready) : len(down_ready) + count]:
+            ready, token = fetch(after, token, w_down, e, first, rows)
+            down_ready.append(ready)
+        return token
 
     parts = [hidden] + [swap(hidden, "tp", j) for j in range(1, tps)]
-    gain, router_rows = norm_gain.reshape(1, -1), router.T
-    gate_ready, token, gain, router_rows, ids = fetch(
-        hidden, hidden, w_gate, 0, (gain, router_rows, route_ids.T)
-    )
+    gate_ready, token = fetch(hidden, hidden, w_gate, 0, 0, w_gate.shape[1])
+    parts, token = tie((parts, token))
     own = norm(gain, router_rows, ids, parts)
-    down_ready = []
     if grps == 4:
         near = [own, swap(own, "grp", 1), swap(own, "grp", 2)]
-        ready, token = fetch(own, token, w_down, 0)
-        down_ready.append(ready)
+        token = fetch_down(own, token, len(spans) - 1)
         near, token = tie((near, token))
         after, right = split(near[2], near[1], tps // 2 * part_cols)
         across = [swap(after, "grp", 1), swap(right, "grp", 2)]
@@ -434,9 +492,7 @@
         near = [[own]] + [[swap(own, "grp", d)] for d in range(1, grps - 1)]
         after = own
         across = [swap(own, "grp", grps - 1)]
-    for e in range(len(down_ready), held):
-        ready, token = fetch(after, token, w_down, e)
-        down_ready.append(ready)
+    token = fetch_down(after, token, len(spans))
     across, token = tie((across, token))
     near.append(across)
     pieces = near + [[swap(array, "sec", 1) for array in arrays] for arrays in near]

time: 84.9 us -> 82.4 us (0.971)
  waiting for transfers between devices: 21.7 us -> 19.7 us
    ppermute x21, waiting for transfers between devices: 21.7 us -> 19.7 us  [swap(): return lax.ppermute(array, axis, [(i, i ^ offset) for i in range(size)])]
    pallas_call x4 -> x5, Pallas kernels: 20.5 us -> 20.6 us  [the longest x4 15.1 us: fetch(): pl.pallas_call(functools.partial(fetch_kernel, index=index, first=first),...]
  transfers between devices with their start and end apart: 21 -> 21, of which waited for: 12 -> 11; matrix products, arithmetic and copies ran while one was open for 0% -> 0% of each run, Pallas kernels for 21% -> 22%
where the time goes in v3:
time: 82.4 us; the launch traced here: 82.3 us
  Pallas kernels  40.7 us (49%)
  starting transfers between devices  20.5 us (25%)
  waiting for transfers between devices  19.7 us (24%)
  other arithmetic  1.14 us (1%)
    ppermute x21, starting transfers between devices, swap(): return lax.ppermute(array, axis, [(i, i ^ offset) for i in range(size)])  20.5 us
    ppermute x21, waiting for transfers between devices, swap(): return lax.ppermute(array, axis, [(i, i ^ offset) for i in range(size)])  19.7 us
    pallas_call x4, Pallas kernels, fetch(): pl.pallas_call(functools.partial(fetch_kernel, index=index, first=first),...  15.1 us
    pallas_call x1, Pallas kernels, gate_up(): pl.pallas_call(functools.partial(gate_up_kernel, layout=tuple((len(parts)...  13 us
    pallas_call x2, Pallas kernels, down(): pl.pallas_call(functools.partial(down_kernel, first=first, part_cols=part...  6.51 us
    pallas_call x1, Pallas kernels, attend(): pl.pallas_call(functools.partial(attend_kernel, extras=len(extra), kv_loc...  5.57 us
  transfers between devices with their start and end apart: 21, of which 11 were waited for; matrix products, arithmetic and copies ran while one was open for 0% of the time, Pallas kernels for 22%

profile of v3, /device:TPU:0, one launch (start us, length us, event | category | flops | bytes accessed | tf_op | source)
XLA Modules:
  0.0 82.3 jit_solution(5985295778985014107)
XLA Ops:
  0.0 5.6 %attend.1 = (bf16[24,1536]{1,0:T(8,128)(2,1)S(1)}, bf16[24,1536]{1,0:T(8,128)(2,1)S(1)}, f32[1,6144]{1,0:T(1,128)S(1)}, f32[8,6144]{1,0:T(8,128)S(1)}, s32[2,24]{1,0:T(2,128)S(1)}) custom-call(s32[24]{0:T(128)} %lengths_hbm.1, bf16[24,1536]{1,0:T(8,128)(2,1)} %query_hbm.1, bf16[24,2,256]{2,1,0:T(2,128)(2,1)} %new_hbm.1, bf16[24,1536]{1,0:T(8,128)(2,1)} %resid_hbm.1, ...), custom_call_target="tpu_custom_call" | custom-call | bytes 6291456 | tf_op jit(solution)/shard_map/attend/pallas_call | solution.py:145
  5.6 5.1 %collective-permute-start.2 = (bf16[24,1536]{1,0:T(8,128)(2,1)S(1)}, bf16[24,1536]{1,0:T(8,128)(2,1)S(1)}, u32[]{:S(2)}, u32[]{:S(2)}) collective-permute-start(bf16[24,1536]{1,0:T(8,128)(2,1)S(1)} %get-tuple-element.43.after_ref.earlier_ref.rest_0_), channel_id=1, source_target_pairs={{0,3},{1,2},{2,1},{3,0},{4,7},{5,6},{6,5},{7,4},{8,11},{9,10},{10,... | collective-permute-start | bytes 221192 | tf_op jit(solution)/shard_map/ppermute | solution.py:454
  10.7 0.0 collective-permute-start.1
  10.7 0.6 collective-permute-start
  11.3 4.7 %fetch.4 = (bf16[6144,1024]{1,0:T(8,128)(2,1)S(1)}, f32[8,128]{1,0:T(8,128)S(1)}) custom-call(bf16[24,1536]{1,0:T(8,128)(2,1)S(1)} %get-tuple-element.43.after_ref.earlier_ref.rest_0_, bf16[24,1536]{1,0:T(8,128)(2,1)S(1)} %get-tuple-element.43.after_ref.earlier_ref.rest_0_, bf16[2,6144,1024]{2,1,0:T(8,128)(2,1)} %gate_hbm.1), custom_call_target="tpu_custom_call" | custom-call | bytes 12582912 | tf_op jit(solution)/shard_map/fetch/pallas_call | solution.py:192
  16.0 0.0 collective-permute-done.2.rest_3_
  16.0 0.9 %collective-permute-done.1.rest_2_ = bf16[24,1536]{1,0:T(8,128)(2,1)S(1)} collective-permute-done((bf16[24,1536]{1,0:T(8,128)(2,1)S(1)}, bf16[24,1536]{1,0:T(8,128)(2,1)S(1)}, u32[]{:S(2)}, u32[]{:S(2)}) %collective-permute-start.1) | collective-permute-done | bytes 73760 | tf_op jit(solution)/shard_map/ppermute | solution.py:454
  16.9 0.0 collective-permute-done.rest_1_
  16.9 0.6 norm.1.after_ref.rest_0_
  17.5 1.6 %collective-permute-start.4 = (bf16[24,6272]{1,0:T(8,128)(2,1)S(1)}, bf16[24,6272]{1,0:T(8,128)(2,1)S(1)}, u32[]{:S(2)}, u32[]{:S(2)}) collective-permute-start(bf16[24,6272]{1,0:T(8,128)(2,1)S(1)} %norm.1.after_ref.rest_0_), channel_id=1, source_target_pairs={{0,8},{4,12},{8,0},{12,4},{1,9},{5,13},{9,1},{13,5},{2,10},{6,14},... | collective-permute-start | bytes 903176 | tf_op jit(solution)/shard_map/ppermute | solution.py:454
  19.1 1.5 %collective-permute-start.3 = (bf16[24,6272]{1,0:T(8,128)(2,1)S(1)}, bf16[24,6272]{1,0:T(8,128)(2,1)S(1)}, u32[]{:S(2)}, u32[]{:S(2)}) collective-permute-start(bf16[24,6272]{1,0:T(8,128)(2,1)S(1)} %norm.1.after_ref.rest_0_), channel_id=1, source_target_pairs={{0,4},{4,0},{8,12},{12,8},{1,5},{5,1},{9,13},{13,9},{2,6},{6,2},{1... | collective-permute-start | bytes 903176 | tf_op jit(solution)/shard_map/ppermute | solution.py:454
  20.6 4.7 %fetch.5 = (bf16[1024,6144]{1,0:T(8,128)(2,1)S(1)}, f32[8,128]{1,0:T(8,128)S(1)}) custom-call(bf16[24,6272]{1,0:T(8,128)(2,1)S(1)} %norm.1.after_ref.rest_0_, f32[8,128]{1,0:T(8,128)S(1)} %get-tuple-element.47.earlier_ref, bf16[2,1024,6144]{2,1,0:T(8,128)(2,1)} %source_hbm.7), custom_call_target="tpu_custom_call" | custom-call | bytes 12582912 | tf_op jit(solution)/shard_map/fetch/pallas_call | solution.py:192
  25.2 1.9 %fetch.6 = (bf16[256,6144]{1,0:T(8,128)(2,1)S(1)}, f32[8,128]{1,0:T(8,128)S(1)}) custom-call(bf16[24,6272]{1,0:T(8,128)(2,1)S(1)} %norm.1.after_ref.rest_0_, f32[8,128]{1,0:T(8,128)S(1)} %get-tuple-element.48.earlier_ref, bf16[2,1024,6144]{2,1,0:T(8,128)(2,1)} %source_hbm.7), custom_call_target="tpu_custom_call" | custom-call | bytes 3145728 | tf_op jit(solution)/shard_map/fetch/pallas_call | solution.py:192
  27.1 0.0 collective-permute-done.4.first_ref.rest_2_
  27.1 0.3 collective-permute-done.3.second_ref.rest_1_
  27.5 0.4 collective-permute-start.6
  27.9 1.6 %collective-permute-start.5 = (bf16[24,3072]{1,0:T(8,128)(2,1)S(1)}, bf16[24,3072]{1,0:T(8,128)(2,1)S(1)}, u32[]{:S(2)}, u32[]{:S(2)}) collective-permute-start(bf16[24,3072]{1,0:T(8,128)(2,1)S(1)} %get-tuple-element.52.after_ref), channel_id=1, source_target_pairs={{0,4},{4,0},{8,12},{12,8},{1,5},{5,1},{9,13},{13,9},{2,6},{6,2},{1... | collective-permute-start | bytes 442376 | tf_op jit(solution)/shard_map/ppermute | solution.py:454
  29.6 0.0 collective-permute-start.7
  29.6 0.5 collective-permute-start.9
  30.1 0.0 collective-permute-start.8
  30.1 3.8 %fetch.7 = (bf16[768,6144]{1,0:T(8,128)(2,1)S(1)}, f32[8,128]{1,0:T(8,128)S(1)}) custom-call(bf16[24,3072]{1,0:T(8,128)(2,1)S(1)} %get-tuple-element.52.after_ref, f32[8,128]{1,0:T(8,128)S(1)} %get-tuple-element.54.earlier_ref, bf16[2,1024,6144]{2,1,0:T(8,128)(2,1)} %source_hbm.7), custom_call_target="tpu_custom_call" | custom-call | bytes 9437184 | tf_op jit(solution)/shard_map/fetch/pallas_call | solution.py:192
  33.9 0.0 collective-permute-done.5.rest_3_
  33.9 0.0 collective-permute-done.6.rest_4_
  33.9 0.6 collective-permute-start.11
  34.5 0.1 collective-permute-start.10
  34.6 0.0 collective-permute-done.7.rest_5_
  34.6 0.0 collective-permute-done.9.rest_7_
  34.6 0.0 collective-permute-done.8.rest_6_
  34.6 1.3 %collective-permute-done.10.rest_8_ = bf16[24,3072]{1,0:T(8,128)(2,1)S(1)} collective-permute-done((bf16[24,3072]{1,0:T(8,128)(2,1)S(1)}, bf16[24,3072]{1,0:T(8,128)(2,1)S(1)}, u32[]{:S(2)}, u32[]{:S(2)}) %collective-permute-start.10) | collective-permute-done | bytes 147488 | tf_op jit(solution)/shard_map/ppermute | solution.py:454
  35.9 0.0 collective-permute-done.11.rest_9_
  35.9 13.0 %gate_up.1.act_ref = bf16[192,2048]{1,0:T(8,128)(2,1)S(1)} custom-call(bf16[2,6144,1024]{2,1,0:T(8,128)(2,1)} %gate_hbm.1, bf16[2,6144,1024]{2,1,0:T(8,128)(2,1)} %up_hbm.1, f32[8,128]{1,0:T(8,128)S(1)} %get-tuple-element.56.token_ref, bf16[6144,1024]{1,0:T(8,128)(2,1)S(1)} %get-tuple-element.57.gate_ref, bf16[24,6272]{1,0:T(8,128)(2,1)S(1)} %norm.1.after_ref.rest_0_, ...), custom_call_target="tpu_custom_call" | custom-call | flops 9663676416 | bytes 50331648 | tf_op jit(solution)/shard_map/gate_up/pallas_call | solution.py:382
  48.9 3.3 %down.2 = (bf16[96,3072]{1,0:T(8,128)(2,1)S(1)}, bf16[96,3072]{1,0:T(8,128)(2,1)S(1)}) custom-call(bf16[192,2048]{1,0:T(8,128)(2,1)S(1)} %gate_up.1.act_ref, bf16[1024,6144]{1,0:T(8,128)(2,1)S(1)} %get-tuple-element.61.rest_0_, bf16[256,6144]{1,0:T(8,128)(2,1)S(1)} %get-tuple-element.62.rest_1_, bf16[768,6144]{1,0:T(8,128)(2,1)S(1)} %get-tuple-element.63.rest_2_), custom_call_target="tpu_custom_call" | custom-call | flops 2415919104 | tf_op jit(solution)/shard_map/down/pallas_call | solution.py:435
  52.2 0.0 copy-start
  52.2 0.3 collective-permute-start.12
  52.5 3.2 %down.3 = (bf16[96,3072]{1,0:T(8,128)(2,1)S(1)}, bf16[96,3072]{1,0:T(8,128)(2,1)S(1)}) custom-call(bf16[192,2048]{1,0:T(8,128)(2,1)S(1)} %gate_up.1.act_ref, bf16[1024,6144]{1,0:T(8,128)(2,1)S(1)} %get-tuple-element.61.rest_0_, bf16[256,6144]{1,0:T(8,128)(2,1)S(1)} %get-tuple-element.62.rest_1_, bf16[768,6144]{1,0:T(8,128)(2,1)S(1)} %get-tuple-element.63.rest_2_), custom_call_target="tpu_custom_call" | custom-call | flops 2415919104 | tf_op jit(solution)/shard_map/down/pallas_call | solution.py:435
  55.7 0.3 collective-permute-start.13
  56.1 0.0 collective-permute-done.12
  56.1 0.1 convert_add_fusion.1
  56.2 0.5 collective-permute-start.16
  56.7 1.1 %collective-permute-done.13 = bf16[96,3072]{1,0:T(8,128)(2,1)S(1)} collective-permute-done((bf16[96,3072]{1,0:T(8,128)(2,1)S(1)}, bf16[96,3072]{1,0:T(8,128)(2,1)S(1)}, u32[]{:S(2)}, u32[]{:S(2)}) %collective-permute-start.13) | collective-permute-done | bytes 589856 | tf_op jit(solution)/shard_map/ppermute | solution.py:454
  57.8 0.1 convert_add_fusion
  57.9 1.6 %collective-permute-start.14 = (bf16[24,3072]{1,0:T(8,128)(2,1)S(1)}, bf16[24,3072]{1,0:T(8,128)(2,1)S(1)}, u32[]{:S(2)}, u32[]{:S(2)}) collective-permute-start(bf16[24,3072]{1,0:T(8,128)(2,1)S(1)} %get-tuple-element.76), channel_id=1, source_target_pairs={{0,8},{4,12},{8,0},{12,4},{1,9},{5,13},{9,1},{13,5},{2,10},{6,14},... | collective-permute-start | bytes 442376 | tf_op jit(solution)/shard_map/ppermute | solution.py:454
  59.5 2.7 %collective-permute-done.16 = bf16[24,3072]{1,0:T(8,128)(2,1)S(1)} collective-permute-done((bf16[24,3072]{1,0:T(8,128)(2,1)S(1)}, bf16[24,3072]{1,0:T(8,128)(2,1)S(1)}, u32[]{:S(2)}, u32[]{:S(2)}) %collective-permute-start.16) | collective-permute-done | bytes 147488 | tf_op jit(solution)/shard_map/ppermute | solution.py:454
  62.2 0.1 add_convert_fusion.1
  62.3 1.6 %collective-permute-start.17 = (bf16[24,6144]{1,0:T(8,128)(2,1)S(1)}, bf16[24,6144]{1,0:T(8,128)(2,1)S(1)}, u32[]{:S(2)}, u32[]{:S(2)}) collective-permute-start(bf16[24,6144]{1,0:T(8,128)(2,1)S(1)} %pad_maximum_fusion.1), channel_id=1, source_target_pairs={{0,8},{4,12},{8,0},{12,4},{1,9},{5,13},{9,1},{13,5},{2,10},{6,14},... | collective-permute-start | bytes 884744 | tf_op jit(solution)/shard_map/ppermute | solution.py:454
  63.9 0.1 collective-permute-done.14
  64.0 0.1 add_convert_fusion.3
  64.1 0.5 collective-permute-start.15
  64.6 6.1 %collective-permute-done.17 = bf16[24,6144]{1,0:T(8,128)(2,1)S(1)} collective-permute-done((bf16[24,6144]{1,0:T(8,128)(2,1)S(1)}, bf16[24,6144]{1,0:T(8,128)(2,1)S(1)}, u32[]{:S(2)}, u32[]{:S(2)}) %collective-permute-start.17) | collective-permute-done | bytes 294944 | tf_op jit(solution)/shard_map/ppermute | solution.py:454
  70.7 1.8 %collective-permute-done.15 = bf16[24,6144]{1,0:T(8,128)(2,1)S(1)} collective-permute-done((bf16[24,6144]{1,0:T(8,128)(2,1)S(1)}, bf16[24,6144]{1,0:T(8,128)(2,1)S(1)}, u32[]{:S(2)}, u32[]{:S(2)}) %collective-permute-start.15) | collective-permute-done | bytes 294944 | tf_op jit(solution)/shard_map/ppermute | solution.py:454
  72.5 0.1 fusion.5
  72.7 0.2 collective-permute-start.18
  72.9 2.4 %collective-permute-start.20 = (bf16[24,1536]{1,0:T(8,128)(2,1)S(1)}, bf16[24,1536]{1,0:T(8,128)(2,1)S(1)}, u32[]{:S(2)}, u32[]{:S(2)}) collective-permute-start(bf16[24,1536]{1,0:T(8,128)(2,1)S(1)} %get-tuple-element.78), channel_id=1, source_target_pairs={{0,3},{1,2},{2,1},{3,0},{4,7},{5,6},{6,5},{7,4},{8,11},{9,10},{10,... | collective-permute-start | bytes 221192 | tf_op jit(solution)/shard_map/ppermute | solution.py:454
  75.2 1.0 %collective-permute-start.19 = (bf16[24,1536]{1,0:T(8,128)(2,1)S(1)}, bf16[24,1536]{1,0:T(8,128)(2,1)S(1)}, u32[]{:S(2)}, u32[]{:S(2)}) collective-permute-start(bf16[24,1536]{1,0:T(8,128)(2,1)S(1)} %get-tuple-element.79), channel_id=1, source_target_pairs={{0,2},{1,3},{2,0},{3,1},{4,6},{5,7},{6,4},{7,5},{8,10},{9,11},{10,... | collective-permute-start | bytes 221192 | tf_op jit(solution)/shard_map/ppermute | solution.py:454
  76.2 1.8 %collective-permute-done.18 = bf16[24,1536]{1,0:T(8,128)(2,1)S(1)} collective-permute-done((bf16[24,1536]{1,0:T(8,128)(2,1)S(1)}, bf16[24,1536]{1,0:T(8,128)(2,1)S(1)}, u32[]{:S(2)}, u32[]{:S(2)}) %collective-permute-start.18) | collective-permute-done | bytes 73760 | tf_op jit(solution)/shard_map/ppermute | solution.py:454
  78.0 1.1 %collective-permute-done.20 = bf16[24,1536]{1,0:T(8,128)(2,1)S(1)} collective-permute-done((bf16[24,1536]{1,0:T(8,128)(2,1)S(1)}, bf16[24,1536]{1,0:T(8,128)(2,1)S(1)}, u32[]{:S(2)}, u32[]{:S(2)}) %collective-permute-start.20) | collective-permute-done | bytes 73760 | tf_op jit(solution)/shard_map/ppermute | solution.py:454
  79.1 2.4 %collective-permute-done.19 = bf16[24,1536]{1,0:T(8,128)(2,1)S(1)} collective-permute-done((bf16[24,1536]{1,0:T(8,128)(2,1)S(1)}, bf16[24,1536]{1,0:T(8,128)(2,1)S(1)}, u32[]{:S(2)}, u32[]{:S(2)}) %collective-permute-start.19) | collective-permute-done | bytes 73760 | tf_op jit(solution)/shard_map/ppermute | solution.py:454
  81.6 0.0 copy-done
  81.6 0.7 fusion.4
  (4 shorter events, 0.1 us)
Async XLA Ops:
  5.6 10.4 %collective-permute-start.2 = (bf16[24,1536]{1,0:T(8,128)(2,1)S(1)}, bf16[24,1536]{1,0:T(8,128)(2,1)S(1)}, u32[]{:S(2)}, u32[]{:S(2)}) collective-permute-start(bf16[24,1536]{1,0:T(8,128)(2,1)S(1)} %get-tuple-element.43.after_ref.earlier_ref.rest_0_), channel_id=1, source_target_pairs={{0,3},{1,2},{2,1},{3,0},{4,7},{5,6},{6,5},{7,4},{8,11},{9,10},{10,... | collective-permute-start | bytes 221192 | tf_op jit(solution)/shard_map/ppermute | solution.py:454
  10.7 6.2 %collective-permute-start.1 = (bf16[24,1536]{1,0:T(8,128)(2,1)S(1)}, bf16[24,1536]{1,0:T(8,128)(2,1)S(1)}, u32[]{:S(2)}, u32[]{:S(2)}) collective-permute-start(bf16[24,1536]{1,0:T(8,128)(2,1)S(1)} %get-tuple-element.43.after_ref.earlier_ref.rest_0_), channel_id=1, source_target_pairs={{0,2},{1,3},{2,0},{3,1},{4,6},{5,7},{6,4},{7,5},{8,10},{9,11},{10,... | collective-permute-start | bytes 221192 | tf_op jit(solution)/shard_map/ppermute | solution.py:454
  10.7 6.2 %collective-permute-start = (bf16[24,1536]{1,0:T(8,128)(2,1)S(1)}, bf16[24,1536]{1,0:T(8,128)(2,1)S(1)}, u32[]{:S(2)}, u32[]{:S(2)}) collective-permute-start(bf16[24,1536]{1,0:T(8,128)(2,1)S(1)} %get-tuple-element.43.after_ref.earlier_ref.rest_0_), channel_id=1, source_target_pairs={{0,1},{1,0},{2,3},{3,2},{4,5},{5,4},{6,7},{7,6},{8,9},{9,8},{10,11... | collective-permute-start | bytes 221192 | tf_op jit(solution)/shard_map/ppermute | solution.py:454
  17.5 9.7 %collective-permute-start.4 = (bf16[24,6272]{1,0:T(8,128)(2,1)S(1)}, bf16[24,6272]{1,0:T(8,128)(2,1)S(1)}, u32[]{:S(2)}, u32[]{:S(2)}) collective-permute-start(bf16[24,6272]{1,0:T(8,128)(2,1)S(1)} %norm.1.after_ref.rest_0_), channel_id=1, source_target_pairs={{0,8},{4,12},{8,0},{12,4},{1,9},{5,13},{9,1},{13,5},{2,10},{6,14},... | collective-permute-start | bytes 903176 | tf_op jit(solution)/shard_map/ppermute | solution.py:454
  19.1 8.4 %collective-permute-start.3 = (bf16[24,6272]{1,0:T(8,128)(2,1)S(1)}, bf16[24,6272]{1,0:T(8,128)(2,1)S(1)}, u32[]{:S(2)}, u32[]{:S(2)}) collective-permute-start(bf16[24,6272]{1,0:T(8,128)(2,1)S(1)} %norm.1.after_ref.rest_0_), channel_id=1, source_target_pairs={{0,4},{4,0},{8,12},{12,8},{1,5},{5,1},{9,13},{13,9},{2,6},{6,2},{1... | collective-permute-start | bytes 903176 | tf_op jit(solution)/shard_map/ppermute | solution.py:454
  27.5 6.4 %collective-permute-start.6 = (bf16[24,3200]{1,0:T(8,128)(2,1)S(1)}, bf16[24,3200]{1,0:T(8,128)(2,1)S(1)}, u32[]{:S(2)}, u32[]{:S(2)}) collective-permute-start(bf16[24,3200]{1,0:T(8,128)(2,1)S(1)} %get-tuple-element.53), channel_id=1, source_target_pairs={{0,8},{4,12},{8,0},{12,4},{1,9},{5,13},{9,1},{13,5},{2,10},{6,14},... | collective-permute-start | bytes 460808 | tf_op jit(solution)/shard_map/ppermute | solution.py:454
  27.9 6.0 %collective-permute-start.5 = (bf16[24,3072]{1,0:T(8,128)(2,1)S(1)}, bf16[24,3072]{1,0:T(8,128)(2,1)S(1)}, u32[]{:S(2)}, u32[]{:S(2)}) collective-permute-start(bf16[24,3072]{1,0:T(8,128)(2,1)S(1)} %get-tuple-element.52.after_ref), channel_id=1, source_target_pairs={{0,4},{4,0},{8,12},{12,8},{1,5},{5,1},{9,13},{13,9},{2,6},{6,2},{1... | collective-permute-start | bytes 442376 | tf_op jit(solution)/shard_map/ppermute | solution.py:454
  29.6 5.0 %collective-permute-start.7 = (bf16[24,6272]{1,0:T(8,128)(2,1)S(1)}, bf16[24,6272]{1,0:T(8,128)(2,1)S(1)}, u32[]{:S(2)}, u32[]{:S(2)}) collective-permute-start(bf16[24,6272]{1,0:T(8,128)(2,1)S(1)} %norm.1.after_ref.rest_0_), channel_id=1, source_target_pairs={{0,16},{16,0},{1,17},{17,1},{2,18},{18,2},{3,19},{19,3},{4,20},{20... | collective-permute-start | bytes 903176 | tf_op jit(solution)/shard_map/ppermute | solution.py:454
  29.6 5.0 %collective-permute-start.9 = (bf16[24,6272]{1,0:T(8,128)(2,1)S(1)}, bf16[24,6272]{1,0:T(8,128)(2,1)S(1)}, u32[]{:S(2)}, u32[]{:S(2)}) collective-permute-start(bf16[24,6272]{1,0:T(8,128)(2,1)S(1)} %collective-permute-done.4.first_ref.rest_2_), channel_id=1, source_target_pairs={{0,16},{16,0},{1,17},{17,1},{2,18},{18,2},{3,19},{19,3},{4,20},{20... | collective-permute-start | bytes 903176 | tf_op jit(solution)/shard_map/ppermute | solution.py:454
  30.1 4.5 %collective-permute-start.8 = (bf16[24,6272]{1,0:T(8,128)(2,1)S(1)}, bf16[24,6272]{1,0:T(8,128)(2,1)S(1)}, u32[]{:S(2)}, u32[]{:S(2)}) collective-permute-start(bf16[24,6272]{1,0:T(8,128)(2,1)S(1)} %collective-permute-done.3.second_ref.rest_1_), channel_id=1, source_target_pairs={{0,16},{16,0},{1,17},{17,1},{2,18},{18,2},{3,19},{19,3},{4,20},{20... | collective-permute-start | bytes 903176 | tf_op jit(solution)/shard_map/ppermute | solution.py:454
  33.9 1.9 %collective-permute-start.11 = (bf16[24,3200]{1,0:T(8,128)(2,1)S(1)}, bf16[24,3200]{1,0:T(8,128)(2,1)S(1)}, u32[]{:S(2)}, u32[]{:S(2)}) collective-permute-start(bf16[24,3200]{1,0:T(8,128)(2,1)S(1)} %collective-permute-done.6.rest_4_), channel_id=1, source_target_pairs={{0,16},{16,0},{1,17},{17,1},{2,18},{18,2},{3,19},{19,3},{4,20},{20... | collective-permute-start | bytes 460808 | tf_op jit(solution)/shard_map/ppermute | solution.py:454
  34.5 1.4 %collective-permute-start.10 = (bf16[24,3072]{1,0:T(8,128)(2,1)S(1)}, bf16[24,3072]{1,0:T(8,128)(2,1)S(1)}, u32[]{:S(2)}, u32[]{:S(2)}) collective-permute-start(bf16[24,3072]{1,0:T(8,128)(2,1)S(1)} %collective-permute-done.5.rest_3_), channel_id=1, source_target_pairs={{0,16},{16,0},{1,17},{17,1},{2,18},{18,2},{3,19},{19,3},{4,20},{20... | collective-permute-start | bytes 442376 | tf_op jit(solution)/shard_map/ppermute | solution.py:454
  52.2 29.4 %copy-start = (bf16[24,1536]{1,0:T(8,128)(2,1)S(1)}, bf16[24,1536]{1,0:T(8,128)(2,1)}, u32[]{:S(2)}) copy-start(bf16[24,1536]{1,0:T(8,128)(2,1)} %resid_hbm.1) | copy-start | bytes 221188
  52.2 3.9 %collective-permute-start.12 = (bf16[96,3072]{1,0:T(8,128)(2,1)S(1)}, bf16[96,3072]{1,0:T(8,128)(2,1)S(1)}, u32[]{:S(2)}, u32[]{:S(2)}) collective-permute-start(bf16[96,3072]{1,0:T(8,128)(2,1)S(1)} %get-tuple-element.65), channel_id=1, source_target_pairs={{0,16},{16,0},{1,17},{17,1},{2,18},{18,2},{3,19},{19,3},{4,20},{20... | collective-permute-start | bytes 1769480 | tf_op jit(solution)/shard_map/ppermute | solution.py:454
  55.7 2.1 %collective-permute-start.13 = (bf16[96,3072]{1,0:T(8,128)(2,1)S(1)}, bf16[96,3072]{1,0:T(8,128)(2,1)S(1)}, u32[]{:S(2)}, u32[]{:S(2)}) collective-permute-start(bf16[96,3072]{1,0:T(8,128)(2,1)S(1)} %get-tuple-element.68), channel_id=1, source_target_pairs={{0,16},{16,0},{1,17},{17,1},{2,18},{18,2},{3,19},{19,3},{4,20},{20... | collective-permute-start | bytes 1769480 | tf_op jit(solution)/shard_map/ppermute | solution.py:454
  56.2 6.0 %collective-permute-start.16 = (bf16[24,3072]{1,0:T(8,128)(2,1)S(1)}, bf16[24,3072]{1,0:T(8,128)(2,1)S(1)}, u32[]{:S(2)}, u32[]{:S(2)}) collective-permute-start(bf16[24,3072]{1,0:T(8,128)(2,1)S(1)} %get-tuple-element.72), channel_id=1, source_target_pairs={{0,4},{4,0},{8,12},{12,8},{1,5},{5,1},{9,13},{13,9},{2,6},{6,2},{1... | collective-permute-start | bytes 442376 | tf_op jit(solution)/shard_map/ppermute | solution.py:454
  57.9 6.1 %collective-permute-start.14 = (bf16[24,3072]{1,0:T(8,128)(2,1)S(1)}, bf16[24,3072]{1,0:T(8,128)(2,1)S(1)}, u32[]{:S(2)}, u32[]{:S(2)}) collective-permute-start(bf16[24,3072]{1,0:T(8,128)(2,1)S(1)} %get-tuple-element.76), channel_id=1, source_target_pairs={{0,8},{4,12},{8,0},{12,4},{1,9},{5,13},{9,1},{13,5},{2,10},{6,14},... | collective-permute-start | bytes 442376 | tf_op jit(solution)/shard_map/ppermute | solution.py:454
  62.3 8.4 %collective-permute-start.17 = (bf16[24,6144]{1,0:T(8,128)(2,1)S(1)}, bf16[24,6144]{1,0:T(8,128)(2,1)S(1)}, u32[]{:S(2)}, u32[]{:S(2)}) collective-permute-start(bf16[24,6144]{1,0:T(8,128)(2,1)S(1)} %pad_maximum_fusion.1), channel_id=1, source_target_pairs={{0,8},{4,12},{8,0},{12,4},{1,9},{5,13},{9,1},{13,5},{2,10},{6,14},... | collective-permute-start | bytes 884744 | tf_op jit(solution)/shard_map/ppermute | solution.py:454
  64.1 8.4 %collective-permute-start.15 = (bf16[24,6144]{1,0:T(8,128)(2,1)S(1)}, bf16[24,6144]{1,0:T(8,128)(2,1)S(1)}, u32[]{:S(2)}, u32[]{:S(2)}) collective-permute-start(bf16[24,6144]{1,0:T(8,128)(2,1)S(1)} %pad_maximum_fusion), channel_id=1, source_target_pairs={{0,4},{4,0},{8,12},{12,8},{1,5},{5,1},{9,13},{13,9},{2,6},{6,2},{1... | collective-permute-start | bytes 884744 | tf_op jit(solution)/shard_map/ppermute | solution.py:454
  72.7 5.4 %collective-permute-start.18 = (bf16[24,1536]{1,0:T(8,128)(2,1)S(1)}, bf16[24,1536]{1,0:T(8,128)(2,1)S(1)}, u32[]{:S(2)}, u32[]{:S(2)}) collective-permute-start(bf16[24,1536]{1,0:T(8,128)(2,1)S(1)} %get-tuple-element.77), channel_id=1, source_target_pairs={{0,1},{1,0},{2,3},{3,2},{4,5},{5,4},{6,7},{7,6},{8,9},{9,8},{10,11... | collective-permute-start | bytes 221192 | tf_op jit(solution)/shard_map/ppermute | solution.py:454
  72.9 6.3 %collective-permute-start.20 = (bf16[24,1536]{1,0:T(8,128)(2,1)S(1)}, bf16[24,1536]{1,0:T(8,128)(2,1)S(1)}, u32[]{:S(2)}, u32[]{:S(2)}) collective-permute-start(bf16[24,1536]{1,0:T(8,128)(2,1)S(1)} %get-tuple-element.78), channel_id=1, source_target_pairs={{0,3},{1,2},{2,1},{3,0},{4,7},{5,6},{6,5},{7,4},{8,11},{9,10},{10,... | collective-permute-start | bytes 221192 | tf_op jit(solution)/shard_map/ppermute | solution.py:454
  75.2 6.3 %collective-permute-start.19 = (bf16[24,1536]{1,0:T(8,128)(2,1)S(1)}, bf16[24,1536]{1,0:T(8,128)(2,1)S(1)}, u32[]{:S(2)}, u32[]{:S(2)}) collective-permute-start(bf16[24,1536]{1,0:T(8,128)(2,1)S(1)} %get-tuple-element.79), channel_id=1, source_target_pairs={{0,2},{1,3},{2,0},{3,1},{4,6},{5,7},{6,4},{7,5},{8,10},{9,11},{10,... | collective-permute-start | bytes 221192 | tf_op jit(solution)/shard_map/ppermute | solution.py:454

commit v4 on v3

--- a/solution.py
+++ b/solution.py
@@ -168,17 +168,32 @@
     )(*far)
 
 
-def fetch_kernel(after_ref, earlier_ref, source_hbm, target_ref, token_ref, sem, *, index, first):
-    pieces = sem.shape[0]
-    step = target_ref.shape[0] // pieces
-    copies = [
-        pltpu.make_async_copy(
-            source_hbm.at[index, pl.ds(first + i * step, step)],
-            target_ref.at[pl.ds(i * step, step)],
-            sem.at[i],
-        )
-        for i in range(pieces)
-    ]
+def span_copies(source_hbm, targets, sems, spans, first, part_cols):
+    tp = lax.axis_index("tp")
+    copies = []
+    for (e, row), target, sem in zip(spans, targets, sems):
+        rows, width = target.shape
+        pieces = sem.shape[0]
+        for i in range(pieces):
+            if part_cols:
+                there = pl.ds(pl.multiple_of((first + i ^ tp) * part_cols, 128), part_cols)
+                source, here = source_hbm.at[e, pl.ds(row, rows), there], (slice(None), pl.ds(i * part_cols, part_cols))
+            else:
+                step = rows // pieces
+                source, here = source_hbm.at[e, pl.ds(row + i * step, step)], (pl.ds(i * step, step),)
+            copies.append(pltpu.make_async_copy(source, target.at[here], sem.at[i]))
+    return copies
+
+
+def fetch_kernel(after_ref, earlier_ref, *rest, jobs):
+    sources, rest = rest[: len(jobs)], rest[len(jobs) :]
+    count = sum(len(spans) for spans, _ in jobs)
+    targets, token_ref, sems = rest[:count], rest[count], rest[count + 1 :]
+    copies, at = [], 0
+    for source, (spans, part_cols) in zip(sources, jobs):
+        here = slice(at, at + len(spans))
+        copies += span_copies(source, targets[here], sems[here], spans, 0, part_cols)
+        at += len(spans)
     for copy in copies:
         copy.start()
     token_ref[...] = jnp.zeros_like(token_ref)
@@ -186,19 +201,26 @@
         copy.wait()
 
 
-def fetch(after, earlier, weights, index, first, rows):
-    shape = (rows, weights.shape[2])
-    pieces = 4
+def fetch(after, earlier, jobs):
+    shapes, parts_of = [], []
+    for weights, spans, parts, part_cols in jobs:
+        for _, _, rows in spans:
+            shapes.append((rows, parts * part_cols if parts else weights.shape[2]))
+            parts_of.append(parts or 4)
+    size = sum(math.prod(shape) for shape in shapes)
     return pl.pallas_call(
-        functools.partial(fetch_kernel, index=index, first=first),
-        in_specs=[pl.BlockSpec(memory_space=pl.ANY)] * 2 + [pl.BlockSpec(memory_space=pltpu.HBM)],
-        out_specs=[pl.BlockSpec(memory_space=pltpu.VMEM)] * 2,
-        out_shape=[pltpu.VMEM(shape, weights.dtype), pltpu.VMEM((8, 128), jnp.float32)],
-        scratch_shapes=[pltpu.SemaphoreType.DMA((pieces,))],
-        cost_estimate=pl.CostEstimate(flops=0, bytes_accessed=2 * math.prod(shape), transcendentals=0),
+        functools.partial(
+            fetch_kernel,
+            jobs=[([span[:2] for span in spans], part_cols) for _, spans, _, part_cols in jobs],
+        ),
+        in_specs=[pl.BlockSpec(memory_space=pl.ANY)] * 2 + [pl.BlockSpec(memory_space=pltpu.HBM)] * len(jobs),
+        out_specs=[pl.BlockSpec(memory_space=pltpu.VMEM)] * (len(shapes) + 1),
+        out_shape=[pltpu.VMEM(shape, jnp.bfloat16) for shape in shapes] + [pltpu.VMEM((8, 128), jnp.float32)],
+        scratch_shapes=[pltpu.SemaphoreType.DMA((parts,)) for parts in parts_of],
+        cost_estimate=pl.CostEstimate(flops=0, bytes_accessed=2 * size, transcendentals=0),
         compiler_params=pltpu.CompilerParams(vmem_limit_bytes=1 * MIB),
         name="fetch",
-    )(after, earlier, pin(weights, pltpu.HBM))
+    )(after, earlier, *(pin(job[0], pltpu.HBM) for job in jobs))
 
 
 def norm_kernel(gain_ref, router_ref, ids_ref, *rest):
@@ -274,7 +296,7 @@
     )(pin(first, pltpu.VMEM), pin(second, pltpu.VMEM))
 
 
-def gate_up_kernel(gate_hbm, up_hbm, token_ref, gate_ref, *rest, layout, experts, blocks_held, depth, nb):
+def gate_up_kernel(gate_hbm, up_hbm, token_ref, gate_ref, up_ref, *rest, layout, experts, blocks_held, depth, nb):
     pieces = sum(layout)
     piece_refs, (act_ref, buf, rows_ref, sem) = rest[:pieces], rest[pieces:]
     held, width, ff = gate_hbm.shape
@@ -282,13 +304,13 @@
     blocks = ff // nb
     deep = buf.shape[1]
     cuts = width // deep
-    steps = (2 * held - ready) * blocks * cuts
+    steps = (2 * held - ready) * blocks * cuts - 1
     grp = lax.axis_index("grp")
 
     def block_copy(hbm, e, n, i):
         slot = lax.rem(i, depth)
         columns = pl.ds(pl.multiple_of(n * nb, 128), nb)
-        there = pl.ds(pl.multiple_of(i % cuts * deep, 128), deep)
+        there = pl.ds(pl.multiple_of((i + 1) % cuts * deep, 128), deep)
         return pltpu.make_async_copy(hbm.at[e, there, columns], buf.at[slot], sem.at[slot])
 
     def start(i):
@@ -296,7 +318,7 @@
         for e in range(held):
             kinds = (up_hbm,) if e < ready else (gate_hbm, up_hbm)
             for which, hbm in enumerate(kinds):
-                inside = i // cuts - first
+                inside = (i + 1) // cuts - first
                 hit = (inside >= 0) & (inside < len(kinds) * blocks) & (inside % len(kinds) == which)
 
                 @pl.when(hit)
@@ -333,12 +355,15 @@
     shares = shares[:, :experts] + shares[:, experts : 2 * experts]
     lane = lax.broadcasted_iota(jnp.int32, shares.shape, 1)
 
-    def streamed(block):
+    def streamed(block, has_first=False):
         product = 0.0
         for cut in range(cuts):
-            i = block * cuts + cut
+            there = pl.ds(cut * deep, deep)
+            if cut == 0 and has_first:
+                product += jnp.dot(rows_ref[:, there], up_ref[...], preferred_element_type=jnp.float32)
+                continue
+            i = block * cuts + cut - 1
             block_copy(gate_hbm, 0, 0, i).wait()
-            there = pl.ds(cut * deep, deep)
             product += jnp.dot(
                 rows_ref[:, there], buf[lax.rem(i, depth)], preferred_element_type=jnp.float32
             )
@@ -362,7 +387,7 @@
             else:
                 i = first + 2 * n + 1
                 gate = streamed(i - 1)
-            up = streamed(i) * share
+            up = streamed(i, e < ready) * share
             out = pl.ds(pl.multiple_of(e * ff + n * nb, 128), nb)
             act_ref[:, out] = (gate / (1.0 + jnp.exp(-gate)) * up).astype(jnp.bfloat16)
             return carry
@@ -371,14 +396,14 @@
         first += (1 if e < ready else 2) * blocks
 
 
-def gate_up(w_gate, w_up, token, gate_ready, pieces, experts, blocks_held):
+def gate_up(w_gate, w_up, token, gate_ready, up_ready, pieces, experts, blocks_held):
     held, width, ff = w_gate.shape
     tokens = sum(parts[0].shape[0] for parts in pieces)
     nb = largest_divisor(ff, (1024, 512, 256, 128))
     depth, cuts = 4, 4
     vmem = pl.BlockSpec(memory_space=pltpu.VMEM)
     hbm = pl.BlockSpec(memory_space=pltpu.HBM)
-    near = [pin(a, pltpu.VMEM) for a in (gate_ready, *(part for parts in pieces for part in parts))]
+    near = [pin(a, pltpu.VMEM) for a in (gate_ready, up_ready, *(part for parts in pieces for part in parts))]
     return pl.pallas_call(
         functools.partial(
             gate_up_kernel,
@@ -404,45 +429,61 @@
     )(pin(w_gate, pltpu.HBM), pin(w_up, pltpu.HBM), token, *near)
 
 
-def down_kernel(act_ref, *rest, first, part_cols, cuts):
-    down_refs, (own_ref, other_ref) = rest[:-2], rest[-2:]
-    starts = [sum(ref.shape[0] for ref in down_refs[:i]) for i in range(len(down_refs))]
+def down_kernel(act_ref, *rest, count, nb, spans, first, part_cols):
+    down_refs, rest = rest[:count], rest[count:]
+    if spans:
+        down_hbm, own_ref, other_ref, *rest = rest
+        targets, sems = rest[: len(spans)], rest[len(spans) :]
+        copies = span_copies(down_hbm, targets, sems, spans, first, part_cols)
+    else:
+        copies, (own_ref, other_ref) = [], rest
+    for copy in copies:
+        copy.start()
+    starts = [sum(ref.shape[0] for ref in down_refs[:i]) for i in range(count)]
     half = own_ref.shape[0]
-    nb = part_cols // cuts
-    tp = lax.axis_index("tp")
 
     def body(i, carry):
-        j = first + i // cuts
-        there = pl.ds(pl.multiple_of((j ^ tp) * part_cols + i % cuts * nb, 128), nb)
+        columns = pl.ds(pl.multiple_of(i * nb, 128), nb)
         partial = sum(
             jnp.dot(
-                act_ref[:, pl.ds(start, ref.shape[0])], ref[:, there], preferred_element_type=jnp.float32
+                act_ref[:, pl.ds(start, ref.shape[0])], ref[:, columns], preferred_element_type=jnp.float32
             )
             for start, ref in zip(starts, down_refs)
         )
-        columns = pl.ds(pl.multiple_of(i * nb, 128), nb)
         own_ref[:, columns] = partial[:half].astype(jnp.bfloat16)
         other_ref[:, columns] = partial[half:].astype(jnp.bfloat16)
         return carry
 
     lax.fori_loop(0, own_ref.shape[1] // nb, body, 0)
-
-
-def down(act, weights, first, parts, part_cols, secs):
+    for copy in copies:
+        copy.wait()
+
+
+def down(act, weights, part_cols, secs, w_down=None, spans=(), first=0, parts=0):
     tokens, depth = act.shape
+    width = weights[0].shape[1]
     vmem = pl.BlockSpec(memory_space=pltpu.VMEM)
     near = [pin(a, pltpu.VMEM) for a in (act, *weights)]
+    far = [pin(w_down, pltpu.HBM)] if spans else []
+    out_shape = [pltpu.VMEM((tokens // secs, width), jnp.bfloat16)] * secs
+    out_shape += [pltpu.VMEM((rows, parts * part_cols), jnp.bfloat16) for _, _, rows in spans]
     return pl.pallas_call(
-        functools.partial(down_kernel, first=first, part_cols=part_cols, cuts=2),
-        in_specs=[vmem] * len(near),
-        out_specs=[vmem] * secs,
-        out_shape=[pltpu.VMEM((tokens // secs, parts * part_cols), jnp.bfloat16)] * secs,
-        cost_estimate=pl.CostEstimate(
-            flops=2 * tokens * depth * parts * part_cols, bytes_accessed=0, transcendentals=0
+        functools.partial(
+            down_kernel,
+            count=len(weights),
+            nb=part_cols,
+            spans=[span[:2] for span in spans],
+            first=first,
+            part_cols=part_cols,
         ),
+        in_specs=[vmem] * len(near) + [pl.BlockSpec(memory_space=pltpu.HBM)] * len(far),
+        out_specs=[vmem] * len(out_shape),
+        out_shape=out_shape,
+        scratch_shapes=[pltpu.SemaphoreType.DMA((parts,)) for _ in spans],
+        cost_estimate=pl.CostEstimate(flops=2 * tokens * depth * width, bytes_accessed=0, transcendentals=0),
         compiler_params=pltpu.CompilerParams(vmem_limit_bytes=4 * MIB),
         name="down",
-    )(*near)
+    )(*near, *far)
 
 
 def pin(array, space):
@@ -467,23 +508,20 @@
     )
 
     ff = w_down.shape[1]
-    spans = [(e, 0, ff) for e in range(held - 1)]
-    spans += [(held - 1, 0, ff // 4), (held - 1, ff // 4, ff - ff // 4)]
-    down_ready = []
-
-    def fetch_down(after, token, count):
-        for e, first, rows in spans[len(down_ready) : len(down_ready) + count]:
-            ready, token = fetch(after, token, w_down, e, first, rows)
-            down_ready.append(ready)
-        return token
+    late_parts = max(1, tps // 4)
+    early_parts = tps - late_parts
+    all_spans = [(e, 0, ff) for e in range(held)]
+    spans = all_spans[:-1] + [(held - 1, 0, ff // 4), (held - 1, ff // 4, ff - ff // 4)]
+    down_jobs = [(w_down, chosen, early_parts, part_cols) for chosen in (spans[:-1], spans[-1:])]
+    up_job = (w_up, [(0, 0, w_up.shape[1] // 4)], 0, 0)
 
     parts = [hidden] + [swap(hidden, "tp", j) for j in range(1, tps)]
-    gate_ready, token = fetch(hidden, hidden, w_gate, 0, 0, w_gate.shape[1])
+    gate_ready, token = fetch(hidden, hidden, [(w_gate, [(0, 0, w_gate.shape[1])], 0, 0)])
     parts, token = tie((parts, token))
     own = norm(gain, router_rows, ids, parts)
     if grps == 4:
         near = [own, swap(own, "grp", 1), swap(own, "grp", 2)]
-        token = fetch_down(own, token, len(spans) - 1)
+        *down_ready, up_ready, token = fetch(own, token, [down_jobs[0], up_job])
         near, token = tie((near, token))
         after, right = split(near[2], near[1], tps // 2 * part_cols)
         across = [swap(after, "grp", 1), swap(right, "grp", 2)]
@@ -492,11 +530,13 @@
         near = [[own]] + [[swap(own, "grp", d)] for d in range(1, grps - 1)]
         after = own
         across = [swap(own, "grp", grps - 1)]
-    token = fetch_down(after, token, len(spans))
+        *down_ready, up_ready, token = fetch(own, token, [down_jobs[0], up_job])
+    last_ready, token = fetch(after, token, [down_jobs[1]])
+    down_ready.append(last_ready)
     across, token = tie((across, token))
     near.append(across)
     pieces = near + [[swap(array, "sec", 1) for array in arrays] for arrays in near]
-    act = gate_up(w_gate, w_up, token, gate_ready, pieces, router.shape[1], blocks_held)
+    act = gate_up(w_gate, w_up, token, gate_ready, up_ready, pieces, router.shape[1], blocks_held)
 
     def total(arrays):
         result = arrays[0].astype(jnp.float32)
@@ -504,26 +544,28 @@
             result = result + array.astype(jnp.float32)
         return result
 
-    halves = []
-    for c in range(2):
-        kept, sent = down(act, down_ready, c * tps // 2, tps // 2, part_cols, secs)
-        act, _ = tie((act, sent))
-        halves.append((kept, swap(sent, "sec", 1)))
-    size = sequences
+    def send(array, name, offset):
+        return swap(array.astype(jnp.bfloat16), name, offset).astype(jnp.float32)
+
+    kept, sent, *down_late = down(act, down_ready, part_cols, secs, w_down, all_spans, early_parts, late_parts)
+    early = (kept, swap(sent, "sec", 1))
+    act, _ = tie((act, sent))
+    kept, sent = down(act, down_late, part_cols, secs)
+    late = (kept, swap(sent, "sec", 1))
     sums = [
-        [total([array[d * size : (d + 1) * size] for array in half]) for half in halves]
+        [total([array[d * sequences : (d + 1) * sequences] for array in pair]) for pair in (early, late)]
         for d in range(grps)
     ]
-
-    def send(array, name, offset):
-        return swap(array.astype(jnp.bfloat16), name, offset).astype(jnp.float32)
-
     if grps == 4:
-        left, right = send(sums[3][0], "grp", 1), send(sums[3][1], "grp", 2)
-        sums[2][0] += left
-        sums[1][1] += right
-        del sums[3]
-    sums = [jnp.concatenate(pair, axis=1) for pair in sums]
+        cut = tps // 2 * part_cols
+        to_x, to_y = sums[1], sums[2]
+        left = send(sums[3][0][:, :cut], "grp", 1)
+        right = [send(sums[3][0][:, cut:], "grp", 2), send(sums[3][1], "grp", 2)]
+        left, right = tie((left, right))
+        to_x = [to_x[0][:, :cut], to_x[0][:, cut:] + right[0], to_x[1] + right[1]]
+        to_y = [to_y[0][:, :cut] + left, to_y[0][:, cut:], to_y[1]]
+        sums = [sums[0], to_x, to_y]
+    sums = [jnp.concatenate(pieces, axis=1) for pieces in sums]
     rows_sum = total([sums[0]] + [send(sums[d], "grp", d) for d in range(1, len(sums))])
     parts = [rows_sum[:, j * part_cols : (j + 1) * part_cols] for j in range(tps)]
     mixed = total([parts[0]] + [send(parts[j], "tp", j) for j in range(1, tps)])

time: 82.4 us -> 80.7 us (0.979)
  Pallas kernels: 40.7 us -> 37.5 us
  starting transfers between devices: 20.5 us -> 21.9 us
    pallas_call x6 -> x5, Pallas kernels: 21.6 us -> 19 us  [the longest x3 13.2 us: fetch(): pl.pallas_call(functools.partial(fetch_kernel, jobs=[([span[:2] for span...]
    ppermute x21 -> x22, starting transfers between devices: 20.5 us -> 21.9 us  [swap(): return lax.ppermute(array, axis, [(i, i ^ offset) for i in range(size)])]
    ppermute x21 -> x22, waiting for transfers between devices: 19.7 us -> 19.7 us  [swap(): return lax.ppermute(array, axis, [(i, i ^ offset) for i in range(size)])]
  transfers between devices with their start and end apart: 21 -> 22, of which waited for: 11 -> 12; matrix products, arithmetic and copies ran while one was open for 0% -> 0% of each run, Pallas kernels for 22% -> 18%
where the time goes in v4:
time: 80.7 us; the launch traced here: 80.6 us
  Pallas kernels  37.5 us (46%)
  starting transfers between devices  21.9 us (27%)
  waiting for transfers between devices  19.7 us (24%)
  other arithmetic  1.24 us (2%)
    ppermute x22, starting transfers between devices, swap(): return lax.ppermute(array, axis, [(i, i ^ offset) for i in range(size)])  21.9 us
    ppermute x22, waiting for transfers between devices, swap(): return lax.ppermute(array, axis, [(i, i ^ offset) for i in range(size)])  19.7 us
    pallas_call x3, Pallas kernels, fetch(): pl.pallas_call(functools.partial(fetch_kernel, jobs=[([span[:2] for span...  13.2 us
    pallas_call x1, Pallas kernels, gate_up(): pl.pallas_call(functools.partial(gate_up_kernel, layout=tuple((len(parts)...  12.3 us
    pallas_call x2, Pallas kernels, down(): pl.pallas_call(functools.partial(down_kernel, count=len(weights), nb=part...  5.82 us
    pallas_call x1, Pallas kernels, attend(): pl.pallas_call(functools.partial(attend_kernel, extras=len(extra), kv_loc...  5.56 us
  transfers between devices with their start and end apart: 22, of which 12 were waited for; matrix products, arithmetic and copies ran while one was open for 0% of the time, Pallas kernels for 18%

profile of v4, /device:TPU:0, one launch (start us, length us, event | category | flops | bytes accessed | tf_op | source)
XLA Modules:
  0.0 80.6 jit_solution(9775349712769518174)
XLA Ops:
  0.0 5.6 %attend.1 = (bf16[24,1536]{1,0:T(8,128)(2,1)S(1)}, bf16[24,1536]{1,0:T(8,128)(2,1)S(1)}, f32[1,6144]{1,0:T(1,128)S(1)}, f32[8,6144]{1,0:T(8,128)S(1)}, s32[2,24]{1,0:T(2,128)S(1)}) custom-call(s32[24]{0:T(128)} %lengths_hbm.1, bf16[24,1536]{1,0:T(8,128)(2,1)} %query_hbm.1, bf16[24,2,256]{2,1,0:T(2,128)(2,1)} %new_hbm.1, bf16[24,1536]{1,0:T(8,128)(2,1)} %resid_hbm.1, ...), custom_call_target="tpu_custom_call" | custom-call | bytes 6291456 | tf_op jit(solution)/shard_map/attend/pallas_call | solution.py:145
  5.6 5.1 %collective-permute-start.2 = (bf16[24,1536]{1,0:T(8,128)(2,1)S(1)}, bf16[24,1536]{1,0:T(8,128)(2,1)S(1)}, u32[]{:S(2)}, u32[]{:S(2)}) collective-permute-start(bf16[24,1536]{1,0:T(8,128)(2,1)S(1)} %get-tuple-element.48.after_ref.earlier_ref.rest_0_), channel_id=1, source_target_pairs={{0,3},{1,2},{2,1},{3,0},{4,7},{5,6},{6,5},{7,4},{8,11},{9,10},{10,... | collective-permute-start | bytes 221192 | tf_op jit(solution)/shard_map/ppermute | solution.py:495
  10.7 0.0 collective-permute-start.1
  10.7 0.6 collective-permute-start
  11.3 4.7 %fetch.3 = (bf16[6144,1024]{1,0:T(8,128)(2,1)S(1)}, f32[8,128]{1,0:T(8,128)S(1)}) custom-call(bf16[24,1536]{1,0:T(8,128)(2,1)S(1)} %get-tuple-element.48.after_ref.earlier_ref.rest_0_, bf16[24,1536]{1,0:T(8,128)(2,1)S(1)} %get-tuple-element.48.after_ref.earlier_ref.rest_0_, bf16[2,6144,1024]{2,1,0:T(8,128)(2,1)} %gate_hbm.1), custom_call_target="tpu_custom_call" | custom-call | bytes 12582912 | tf_op jit(solution)/shard_map/fetch/pallas_call | solution.py:211
  16.0 0.0 collective-permute-done.2.rest_3_
  16.0 0.9 %collective-permute-done.1.rest_2_ = bf16[24,1536]{1,0:T(8,128)(2,1)S(1)} collective-permute-done((bf16[24,1536]{1,0:T(8,128)(2,1)S(1)}, bf16[24,1536]{1,0:T(8,128)(2,1)S(1)}, u32[]{:S(2)}, u32[]{:S(2)}) %collective-permute-start.1) | collective-permute-done | bytes 73760 | tf_op jit(solution)/shard_map/ppermute | solution.py:495
  16.9 0.0 collective-permute-done.rest_1_
  16.9 0.6 norm.1.after_ref.rest_0_
  17.5 1.6 %collective-permute-start.4 = (bf16[24,6272]{1,0:T(8,128)(2,1)S(1)}, bf16[24,6272]{1,0:T(8,128)(2,1)S(1)}, u32[]{:S(2)}, u32[]{:S(2)}) collective-permute-start(bf16[24,6272]{1,0:T(8,128)(2,1)S(1)} %norm.1.after_ref.rest_0_), channel_id=1, source_target_pairs={{0,8},{4,12},{8,0},{12,4},{1,9},{5,13},{9,1},{13,5},{2,10},{6,14},... | collective-permute-start | bytes 903176 | tf_op jit(solution)/shard_map/ppermute | solution.py:495
  19.1 1.5 %collective-permute-start.3 = (bf16[24,6272]{1,0:T(8,128)(2,1)S(1)}, bf16[24,6272]{1,0:T(8,128)(2,1)S(1)}, u32[]{:S(2)}, u32[]{:S(2)}) collective-permute-start(bf16[24,6272]{1,0:T(8,128)(2,1)S(1)} %norm.1.after_ref.rest_0_), channel_id=1, source_target_pairs={{0,4},{4,0},{8,12},{12,8},{1,5},{5,1},{9,13},{13,9},{2,6},{6,2},{1... | collective-permute-start | bytes 903176 | tf_op jit(solution)/shard_map/ppermute | solution.py:495
  20.6 5.4 %fetch.4 = (bf16[1024,4608]{1,0:T(8,128)(2,1)S(1)}, bf16[256,4608]{1,0:T(8,128)(2,1)S(1)}, bf16[1536,1024]{1,0:T(8,128)(2,1)S(1)}, f32[8,128]{1,0:T(8,128)S(1)}) custom-call(bf16[24,6272]{1,0:T(8,128)(2,1)S(1)} %norm.1.after_ref.rest_0_, f32[8,128]{1,0:T(8,128)S(1)} %get-tuple-element.52.earlier_ref, bf16[2,1024,6144]{2,1,0:T(8,128)(2,1)} %rest_3_.1, ...), custom_call_target="tpu_custom_call" | custom-call | bytes 14942208 | tf_op jit(solution)/shard_map/fetch/pallas_call | solution.py:211
  25.9 0.1 collective-permute-done.4.first_ref.rest_2_
  26.0 1.4 %collective-permute-done.3.second_ref.rest_1_ = bf16[24,6272]{1,0:T(8,128)(2,1)S(1)} collective-permute-done((bf16[24,6272]{1,0:T(8,128)(2,1)S(1)}, bf16[24,6272]{1,0:T(8,128)(2,1)S(1)}, u32[]{:S(2)}, u32[]{:S(2)}) %collective-permute-start.3) | collective-permute-done | bytes 301088 | tf_op jit(solution)/shard_map/ppermute | solution.py:495
  27.5 0.4 collective-permute-start.6
  27.9 1.6 %collective-permute-start.5 = (bf16[24,3072]{1,0:T(8,128)(2,1)S(1)}, bf16[24,3072]{1,0:T(8,128)(2,1)S(1)}, u32[]{:S(2)}, u32[]{:S(2)}) collective-permute-start(bf16[24,3072]{1,0:T(8,128)(2,1)S(1)} %get-tuple-element.56.after_ref), channel_id=1, source_target_pairs={{0,4},{4,0},{8,12},{12,8},{1,5},{5,1},{9,13},{13,9},{2,6},{6,2},{1... | collective-permute-start | bytes 442376 | tf_op jit(solution)/shard_map/ppermute | solution.py:495
  29.6 0.0 collective-permute-start.7
  29.6 0.5 collective-permute-start.9
  30.1 0.0 collective-permute-start.8
  30.1 3.1 %fetch.5 = (bf16[768,4608]{1,0:T(8,128)(2,1)S(1)}, f32[8,128]{1,0:T(8,128)S(1)}) custom-call(bf16[24,3072]{1,0:T(8,128)(2,1)S(1)} %get-tuple-element.56.after_ref, f32[8,128]{1,0:T(8,128)S(1)} %get-tuple-element.58.earlier_ref, bf16[2,1024,6144]{2,1,0:T(8,128)(2,1)} %rest_3_.1), custom_call_target="tpu_custom_call" | custom-call | bytes 7077888 | tf_op jit(solution)/shard_map/fetch/pallas_call | solution.py:211
  33.2 0.0 collective-permute-done.5.rest_3_
  33.2 0.0 collective-permute-done.6.rest_4_
  33.2 0.6 collective-permute-start.11
  33.8 0.1 collective-permute-start.10
  33.9 0.0 collective-permute-done.7.rest_5_
  33.9 0.0 collective-permute-done.9.rest_7_
  33.9 0.0 collective-permute-done.8.rest_6_
  33.9 1.3 %collective-permute-done.10.rest_8_ = bf16[24,3072]{1,0:T(8,128)(2,1)S(1)} collective-permute-done((bf16[24,3072]{1,0:T(8,128)(2,1)S(1)}, bf16[24,3072]{1,0:T(8,128)(2,1)S(1)}, u32[]{:S(2)}, u32[]{:S(2)}) %collective-permute-start.10) | collective-permute-done | bytes 147488 | tf_op jit(solution)/shard_map/ppermute | solution.py:495
  35.2 0.0 collective-permute-done.11.rest_9_
  35.2 12.3 %gate_up.1.act_ref = bf16[192,2048]{1,0:T(8,128)(2,1)S(1)} custom-call(bf16[2,6144,1024]{2,1,0:T(8,128)(2,1)} %gate_hbm.1, bf16[2,6144,1024]{2,1,0:T(8,128)(2,1)} %up_hbm.1, f32[8,128]{1,0:T(8,128)S(1)} %get-tuple-element.60.token_ref, bf16[6144,1024]{1,0:T(8,128)(2,1)S(1)} %get-tuple-element.61.gate_ref, bf16[1536,1024]{1,0:T(8,128)(2,1)S(1)} %get-tuple-element.62.up_ref, ...), custom_call_target="tpu_custom_call" | custom-call | flops 9663676416 | bytes 50331648 | tf_op jit(solution)/shard_map/gate_up/pallas_call | solution.py:407
  47.5 4.4 %down.2 = (bf16[96,4608]{1,0:T(8,128)(2,1)S(1)}, bf16[96,4608]{1,0:T(8,128)(2,1)S(1)}, bf16[1024,1536]{1,0:T(8,128)(2,1)S(1)}, bf16[1024,1536]{1,0:T(8,128)(2,1)S(1)}) custom-call(bf16[192,2048]{1,0:T(8,128)(2,1)S(1)} %gate_up.1.act_ref, bf16[1024,4608]{1,0:T(8,128)(2,1)S(1)} %get-tuple-element.66.rest_0_, bf16[256,4608]{1,0:T(8,128)(2,1)S(1)} %get-tuple-element.67.rest_1_, ...), custom_call_target="tpu_custom_call" | custom-call | flops 3623878656 | tf_op jit(solution)/shard_map/down/pallas_call | solution.py:470
  51.9 0.3 collective-permute-start.12
  52.2 1.4 %down.3 = (bf16[96,1536]{1,0:T(8,128)(2,1)S(1)}, bf16[96,1536]{1,0:T(8,128)(2,1)S(1)}) custom-call(bf16[192,2048]{1,0:T(8,128)(2,1)S(1)} %gate_up.1.act_ref, bf16[1024,1536]{1,0:T(8,128)(2,1)S(1)} %get-tuple-element.72.rest_0_, bf16[1024,1536]{1,0:T(8,128)(2,1)S(1)} %get-tuple-element.73.rest_1_), custom_call_target="tpu_custom_call" | custom-call | flops 1207959552 | tf_op jit(solution)/shard_map/down/pallas_call | solution.py:470
  53.6 0.0 copy-start
  53.7 0.3 collective-permute-start.13
  54.0 0.4 collective-permute-done.12
  54.4 0.2 convert_add_fusion.2
  54.7 1.2 %collective-permute-start.14 = (bf16[24,3072]{1,0:T(8,128)(2,1)S(1)}, bf16[24,3072]{1,0:T(8,128)(2,1)S(1)}, u32[]{:S(2)}, u32[]{:S(2)}) collective-permute-start(bf16[24,3072]{1,0:T(8,128)(2,1)S(1)} %slice.117), channel_id=1, source_target_pairs={{0,4},{4,0},{8,12},{12,8},{1,5},{5,1},{9,13},{13,9},{2,6},{6,2},{1... | collective-permute-start | bytes 442376 | tf_op jit(solution)/shard_map/ppermute | solution.py:495
  55.8 0.0 collective-permute-done.13
  55.9 1.6 %collective-permute-start.16 = (bf16[24,1536]{1,0:T(8,128)(2,1)S(1)}, bf16[24,1536]{1,0:T(8,128)(2,1)S(1)}, u32[]{:S(2)}, u32[]{:S(2)}) collective-permute-start(bf16[24,1536]{1,0:T(8,128)(2,1)S(1)} %add_convert_fusion.3), channel_id=1, source_target_pairs={{0,8},{4,12},{8,0},{12,4},{1,9},{5,13},{9,1},{13,5},{2,10},{6,14},... | collective-permute-start | bytes 221192 | tf_op jit(solution)/shard_map/ppermute | solution.py:495
  57.5 0.5 collective-permute-start.15
  58.0 2.8 %collective-permute-done.16 = bf16[24,1536]{1,0:T(8,128)(2,1)S(1)} collective-permute-done((bf16[24,1536]{1,0:T(8,128)(2,1)S(1)}, bf16[24,1536]{1,0:T(8,128)(2,1)S(1)}, u32[]{:S(2)}, u32[]{:S(2)}) %collective-permute-start.16) | collective-permute-done | bytes 73760 | tf_op jit(solution)/shard_map/ppermute | solution.py:495
  60.9 1.0 %collective-permute-done.15 = bf16[24,1536]{1,0:T(8,128)(2,1)S(1)} collective-permute-done((bf16[24,1536]{1,0:T(8,128)(2,1)S(1)}, bf16[24,1536]{1,0:T(8,128)(2,1)S(1)}, u32[]{:S(2)}, u32[]{:S(2)}) %collective-permute-start.15) | collective-permute-done | bytes 73760 | tf_op jit(solution)/shard_map/ppermute | solution.py:495
  61.9 0.0 collective-permute-done.14
  62.0 0.1 convert_add_fusion.3
  62.1 1.0 %collective-permute-start.17 = (bf16[24,6144]{1,0:T(8,128)(2,1)S(1)}, bf16[24,6144]{1,0:T(8,128)(2,1)S(1)}, u32[]{:S(2)}, u32[]{:S(2)}) collective-permute-start(bf16[24,6144]{1,0:T(8,128)(2,1)S(1)} %pad_maximum_fusion), channel_id=1, source_target_pairs={{0,4},{4,0},{8,12},{12,8},{1,5},{5,1},{9,13},{13,9},{2,6},{6,2},{1... | collective-permute-start | bytes 884744 | tf_op jit(solution)/shard_map/ppermute | solution.py:495
  63.1 1.4 %collective-permute-start.18 = (bf16[24,6144]{1,0:T(8,128)(2,1)S(1)}, bf16[24,6144]{1,0:T(8,128)(2,1)S(1)}, u32[]{:S(2)}, u32[]{:S(2)}) collective-permute-start(bf16[24,6144]{1,0:T(8,128)(2,1)S(1)} %pad_maximum_fusion.1), channel_id=1, source_target_pairs={{0,8},{4,12},{8,0},{12,4},{1,9},{5,13},{9,1},{13,5},{2,10},{6,14},... | collective-permute-start | bytes 884744 | tf_op jit(solution)/shard_map/ppermute | solution.py:495
  64.4 6.0 %collective-permute-done.17 = bf16[24,6144]{1,0:T(8,128)(2,1)S(1)} collective-permute-done((bf16[24,6144]{1,0:T(8,128)(2,1)S(1)}, bf16[24,6144]{1,0:T(8,128)(2,1)S(1)}, u32[]{:S(2)}, u32[]{:S(2)}) %collective-permute-start.17) | collective-permute-done | bytes 294944 | tf_op jit(solution)/shard_map/ppermute | solution.py:495
  70.4 0.7 collective-permute-done.18
  71.1 0.1 fusion.7
  71.3 0.2 collective-permute-start.19
  71.5 2.4 %collective-permute-start.21 = (bf16[24,1536]{1,0:T(8,128)(2,1)S(1)}, bf16[24,1536]{1,0:T(8,128)(2,1)S(1)}, u32[]{:S(2)}, u32[]{:S(2)}) collective-permute-start(bf16[24,1536]{1,0:T(8,128)(2,1)S(1)} %get-tuple-element.89), channel_id=1, source_target_pairs={{0,3},{1,2},{2,1},{3,0},{4,7},{5,6},{6,5},{7,4},{8,11},{9,10},{10,... | collective-permute-start | bytes 221192 | tf_op jit(solution)/shard_map/ppermute | solution.py:495
  73.9 1.0 %collective-permute-start.20 = (bf16[24,1536]{1,0:T(8,128)(2,1)S(1)}, bf16[24,1536]{1,0:T(8,128)(2,1)S(1)}, u32[]{:S(2)}, u32[]{:S(2)}) collective-permute-start(bf16[24,1536]{1,0:T(8,128)(2,1)S(1)} %get-tuple-element.90), channel_id=1, source_target_pairs={{0,2},{1,3},{2,0},{3,1},{4,6},{5,7},{6,4},{7,5},{8,10},{9,11},{10,... | collective-permute-start | bytes 221192 | tf_op jit(solution)/shard_map/ppermute | solution.py:495
  74.8 1.6 %collective-permute-done.19 = bf16[24,1536]{1,0:T(8,128)(2,1)S(1)} collective-permute-done((bf16[24,1536]{1,0:T(8,128)(2,1)S(1)}, bf16[24,1536]{1,0:T(8,128)(2,1)S(1)}, u32[]{:S(2)}, u32[]{:S(2)}) %collective-permute-start.19) | collective-permute-done | bytes 73760 | tf_op jit(solution)/shard_map/ppermute | solution.py:495
  76.4 1.3 %collective-permute-done.21 = bf16[24,1536]{1,0:T(8,128)(2,1)S(1)} collective-permute-done((bf16[24,1536]{1,0:T(8,128)(2,1)S(1)}, bf16[24,1536]{1,0:T(8,128)(2,1)S(1)}, u32[]{:S(2)}, u32[]{:S(2)}) %collective-permute-start.21) | collective-permute-done | bytes 73760 | tf_op jit(solution)/shard_map/ppermute | solution.py:495
  77.7 2.2 %collective-permute-done.20 = bf16[24,1536]{1,0:T(8,128)(2,1)S(1)} collective-permute-done((bf16[24,1536]{1,0:T(8,128)(2,1)S(1)}, bf16[24,1536]{1,0:T(8,128)(2,1)S(1)}, u32[]{:S(2)}, u32[]{:S(2)}) %collective-permute-start.20) | collective-permute-done | bytes 73760 | tf_op jit(solution)/shard_map/ppermute | solution.py:495
  79.9 0.0 copy-done
  79.9 0.7 fusion.5
  (14 shorter events, 0.2 us)
Async XLA Ops:
  5.6 10.5 %collective-permute-start.2 = (bf16[24,1536]{1,0:T(8,128)(2,1)S(1)}, bf16[24,1536]{1,0:T(8,128)(2,1)S(1)}, u32[]{:S(2)}, u32[]{:S(2)}) collective-permute-start(bf16[24,1536]{1,0:T(8,128)(2,1)S(1)} %get-tuple-element.48.after_ref.earlier_ref.rest_0_), channel_id=1, source_target_pairs={{0,3},{1,2},{2,1},{3,0},{4,7},{5,6},{6,5},{7,4},{8,11},{9,10},{10,... | collective-permute-start | bytes 221192 | tf_op jit(solution)/shard_map/ppermute | solution.py:495
  10.7 6.2 %collective-permute-start.1 = (bf16[24,1536]{1,0:T(8,128)(2,1)S(1)}, bf16[24,1536]{1,0:T(8,128)(2,1)S(1)}, u32[]{:S(2)}, u32[]{:S(2)}) collective-permute-start(bf16[24,1536]{1,0:T(8,128)(2,1)S(1)} %get-tuple-element.48.after_ref.earlier_ref.rest_0_), channel_id=1, source_target_pairs={{0,2},{1,3},{2,0},{3,1},{4,6},{5,7},{6,4},{7,5},{8,10},{9,11},{10,... | collective-permute-start | bytes 221192 | tf_op jit(solution)/shard_map/ppermute | solution.py:495
  10.7 6.2 %collective-permute-start = (bf16[24,1536]{1,0:T(8,128)(2,1)S(1)}, bf16[24,1536]{1,0:T(8,128)(2,1)S(1)}, u32[]{:S(2)}, u32[]{:S(2)}) collective-permute-start(bf16[24,1536]{1,0:T(8,128)(2,1)S(1)} %get-tuple-element.48.after_ref.earlier_ref.rest_0_), channel_id=1, source_target_pairs={{0,1},{1,0},{2,3},{3,2},{4,5},{5,4},{6,7},{7,6},{8,9},{9,8},{10,11... | collective-permute-start | bytes 221192 | tf_op jit(solution)/shard_map/ppermute | solution.py:495
  17.5 8.6 %collective-permute-start.4 = (bf16[24,6272]{1,0:T(8,128)(2,1)S(1)}, bf16[24,6272]{1,0:T(8,128)(2,1)S(1)}, u32[]{:S(2)}, u32[]{:S(2)}) collective-permute-start(bf16[24,6272]{1,0:T(8,128)(2,1)S(1)} %norm.1.after_ref.rest_0_), channel_id=1, source_target_pairs={{0,8},{4,12},{8,0},{12,4},{1,9},{5,13},{9,1},{13,5},{2,10},{6,14},... | collective-permute-start | bytes 903176 | tf_op jit(solution)/shard_map/ppermute | solution.py:495
  19.1 8.4 %collective-permute-start.3 = (bf16[24,6272]{1,0:T(8,128)(2,1)S(1)}, bf16[24,6272]{1,0:T(8,128)(2,1)S(1)}, u32[]{:S(2)}, u32[]{:S(2)}) collective-permute-start(bf16[24,6272]{1,0:T(8,128)(2,1)S(1)} %norm.1.after_ref.rest_0_), channel_id=1, source_target_pairs={{0,4},{4,0},{8,12},{12,8},{1,5},{5,1},{9,13},{13,9},{2,6},{6,2},{1... | collective-permute-start | bytes 903176 | tf_op jit(solution)/shard_map/ppermute | solution.py:495
  27.5 5.7 %collective-permute-start.6 = (bf16[24,3200]{1,0:T(8,128)(2,1)S(1)}, bf16[24,3200]{1,0:T(8,128)(2,1)S(1)}, u32[]{:S(2)}, u32[]{:S(2)}) collective-permute-start(bf16[24,3200]{1,0:T(8,128)(2,1)S(1)} %get-tuple-element.57), channel_id=1, source_target_pairs={{0,8},{4,12},{8,0},{12,4},{1,9},{5,13},{9,1},{13,5},{2,10},{6,14},... | collective-permute-start | bytes 460808 | tf_op jit(solution)/shard_map/ppermute | solution.py:495
  27.9 5.3 %collective-permute-start.5 = (bf16[24,3072]{1,0:T(8,128)(2,1)S(1)}, bf16[24,3072]{1,0:T(8,128)(2,1)S(1)}, u32[]{:S(2)}, u32[]{:S(2)}) collective-permute-start(bf16[24,3072]{1,0:T(8,128)(2,1)S(1)} %get-tuple-element.56.after_ref), channel_id=1, source_target_pairs={{0,4},{4,0},{8,12},{12,8},{1,5},{5,1},{9,13},{13,9},{2,6},{6,2},{1... | collective-permute-start | bytes 442376 | tf_op jit(solution)/shard_map/ppermute | solution.py:495
  29.6 4.3 %collective-permute-start.7 = (bf16[24,6272]{1,0:T(8,128)(2,1)S(1)}, bf16[24,6272]{1,0:T(8,128)(2,1)S(1)}, u32[]{:S(2)}, u32[]{:S(2)}) collective-permute-start(bf16[24,6272]{1,0:T(8,128)(2,1)S(1)} %norm.1.after_ref.rest_0_), channel_id=1, source_target_pairs={{0,16},{16,0},{1,17},{17,1},{2,18},{18,2},{3,19},{19,3},{4,20},{20... | collective-permute-start | bytes 903176 | tf_op jit(solution)/shard_map/ppermute | solution.py:495
  29.6 4.3 %collective-permute-start.9 = (bf16[24,6272]{1,0:T(8,128)(2,1)S(1)}, bf16[24,6272]{1,0:T(8,128)(2,1)S(1)}, u32[]{:S(2)}, u32[]{:S(2)}) collective-permute-start(bf16[24,6272]{1,0:T(8,128)(2,1)S(1)} %collective-permute-done.4.first_ref.rest_2_), channel_id=1, source_target_pairs={{0,16},{16,0},{1,17},{17,1},{2,18},{18,2},{3,19},{19,3},{4,20},{20... | collective-permute-start | bytes 903176 | tf_op jit(solution)/shard_map/ppermute | solution.py:495
  30.1 3.8 %collective-permute-start.8 = (bf16[24,6272]{1,0:T(8,128)(2,1)S(1)}, bf16[24,6272]{1,0:T(8,128)(2,1)S(1)}, u32[]{:S(2)}, u32[]{:S(2)}) collective-permute-start(bf16[24,6272]{1,0:T(8,128)(2,1)S(1)} %collective-permute-done.3.second_ref.rest_1_), channel_id=1, source_target_pairs={{0,16},{16,0},{1,17},{17,1},{2,18},{18,2},{3,19},{19,3},{4,20},{20... | collective-permute-start | bytes 903176 | tf_op jit(solution)/shard_map/ppermute | solution.py:495
  33.2 1.9 %collective-permute-start.11 = (bf16[24,3200]{1,0:T(8,128)(2,1)S(1)}, bf16[24,3200]{1,0:T(8,128)(2,1)S(1)}, u32[]{:S(2)}, u32[]{:S(2)}) collective-permute-start(bf16[24,3200]{1,0:T(8,128)(2,1)S(1)} %collective-permute-done.6.rest_4_), channel_id=1, source_target_pairs={{0,16},{16,0},{1,17},{17,1},{2,18},{18,2},{3,19},{19,3},{4,20},{20... | collective-permute-start | bytes 460808 | tf_op jit(solution)/shard_map/ppermute | solution.py:495
  33.8 1.4 %collective-permute-start.10 = (bf16[24,3072]{1,0:T(8,128)(2,1)S(1)}, bf16[24,3072]{1,0:T(8,128)(2,1)S(1)}, u32[]{:S(2)}, u32[]{:S(2)}) collective-permute-start(bf16[24,3072]{1,0:T(8,128)(2,1)S(1)} %collective-permute-done.5.rest_3_), channel_id=1, source_target_pairs={{0,16},{16,0},{1,17},{17,1},{2,18},{18,2},{3,19},{19,3},{4,20},{20... | collective-permute-start | bytes 442376 | tf_op jit(solution)/shard_map/ppermute | solution.py:495
  51.9 2.5 %collective-permute-start.12 = (bf16[96,4608]{1,0:T(8,128)(2,1)S(1)}, bf16[96,4608]{1,0:T(8,128)(2,1)S(1)}, u32[]{:S(2)}, u32[]{:S(2)}) collective-permute-start(bf16[96,4608]{1,0:T(8,128)(2,1)S(1)} %get-tuple-element.70), channel_id=1, source_target_pairs={{0,16},{16,0},{1,17},{17,1},{2,18},{18,2},{3,19},{19,3},{4,20},{20... | collective-permute-start | bytes 2654216 | tf_op jit(solution)/shard_map/ppermute | solution.py:495
  53.6 26.3 %copy-start = (bf16[24,1536]{1,0:T(8,128)(2,1)S(1)}, bf16[24,1536]{1,0:T(8,128)(2,1)}, u32[]{:S(2)}) copy-start(bf16[24,1536]{1,0:T(8,128)(2,1)} %resid_hbm.1) | copy-start | bytes 221188
  53.7 2.2 %collective-permute-start.13 = (bf16[96,1536]{1,0:T(8,128)(2,1)S(1)}, bf16[96,1536]{1,0:T(8,128)(2,1)S(1)}, u32[]{:S(2)}, u32[]{:S(2)}) collective-permute-start(bf16[96,1536]{1,0:T(8,128)(2,1)S(1)} %get-tuple-element.75), channel_id=1, source_target_pairs={{0,16},{16,0},{1,17},{17,1},{2,18},{18,2},{3,19},{19,3},{4,20},{20... | collective-permute-start | bytes 884744 | tf_op jit(solution)/shard_map/ppermute | solution.py:495
  54.7 7.2 %collective-permute-start.14 = (bf16[24,3072]{1,0:T(8,128)(2,1)S(1)}, bf16[24,3072]{1,0:T(8,128)(2,1)S(1)}, u32[]{:S(2)}, u32[]{:S(2)}) collective-permute-start(bf16[24,3072]{1,0:T(8,128)(2,1)S(1)} %slice.117), channel_id=1, source_target_pairs={{0,4},{4,0},{8,12},{12,8},{1,5},{5,1},{9,13},{13,9},{2,6},{6,2},{1... | collective-permute-start | bytes 442376 | tf_op jit(solution)/shard_map/ppermute | solution.py:495
  55.9 4.9 %collective-permute-start.16 = (bf16[24,1536]{1,0:T(8,128)(2,1)S(1)}, bf16[24,1536]{1,0:T(8,128)(2,1)S(1)}, u32[]{:S(2)}, u32[]{:S(2)}) collective-permute-start(bf16[24,1536]{1,0:T(8,128)(2,1)S(1)} %add_convert_fusion.3), channel_id=1, source_target_pairs={{0,8},{4,12},{8,0},{12,4},{1,9},{5,13},{9,1},{13,5},{2,10},{6,14},... | collective-permute-start | bytes 221192 | tf_op jit(solution)/shard_map/ppermute | solution.py:495
  57.5 4.4 %collective-permute-start.15 = (bf16[24,1536]{1,0:T(8,128)(2,1)S(1)}, bf16[24,1536]{1,0:T(8,128)(2,1)S(1)}, u32[]{:S(2)}, u32[]{:S(2)}) collective-permute-start(bf16[24,1536]{1,0:T(8,128)(2,1)S(1)} %slice.118), channel_id=1, source_target_pairs={{0,8},{4,12},{8,0},{12,4},{1,9},{5,13},{9,1},{13,5},{2,10},{6,14},... | collective-permute-start | bytes 221192 | tf_op jit(solution)/shard_map/ppermute | solution.py:495
  62.1 8.3 %collective-permute-start.17 = (bf16[24,6144]{1,0:T(8,128)(2,1)S(1)}, bf16[24,6144]{1,0:T(8,128)(2,1)S(1)}, u32[]{:S(2)}, u32[]{:S(2)}) collective-permute-start(bf16[24,6144]{1,0:T(8,128)(2,1)S(1)} %pad_maximum_fusion), channel_id=1, source_target_pairs={{0,4},{4,0},{8,12},{12,8},{1,5},{5,1},{9,13},{13,9},{2,6},{6,2},{1... | collective-permute-start | bytes 884744 | tf_op jit(solution)/shard_map/ppermute | solution.py:495
  63.1 8.0 %collective-permute-start.18 = (bf16[24,6144]{1,0:T(8,128)(2,1)S(1)}, bf16[24,6144]{1,0:T(8,128)(2,1)S(1)}, u32[]{:S(2)}, u32[]{:S(2)}) collective-permute-start(bf16[24,6144]{1,0:T(8,128)(2,1)S(1)} %pad_maximum_fusion.1), channel_id=1, source_target_pairs={{0,8},{4,12},{8,0},{12,4},{1,9},{5,13},{9,1},{13,5},{2,10},{6,14},... | collective-permute-start | bytes 884744 | tf_op jit(solution)/shard_map/ppermute | solution.py:495
  71.3 5.1 %collective-permute-start.19 = (bf16[24,1536]{1,0:T(8,128)(2,1)S(1)}, bf16[24,1536]{1,0:T(8,128)(2,1)S(1)}, u32[]{:S(2)}, u32[]{:S(2)}) collective-permute-start(bf16[24,1536]{1,0:T(8,128)(2,1)S(1)} %get-tuple-element.88), channel_id=1, source_target_pairs={{0,1},{1,0},{2,3},{3,2},{4,5},{5,4},{6,7},{7,6},{8,9},{9,8},{10,11... | collective-permute-start | bytes 221192 | tf_op jit(solution)/shard_map/ppermute | solution.py:495
  71.5 6.2 %collective-permute-start.21 = (bf16[24,1536]{1,0:T(8,128)(2,1)S(1)}, bf16[24,1536]{1,0:T(8,128)(2,1)S(1)}, u32[]{:S(2)}, u32[]{:S(2)}) collective-permute-start(bf16[24,1536]{1,0:T(8,128)(2,1)S(1)} %get-tuple-element.89), channel_id=1, source_target_pairs={{0,3},{1,2},{2,1},{3,0},{4,7},{5,6},{6,5},{7,4},{8,11},{9,10},{10,... | collective-permute-start | bytes 221192 | tf_op jit(solution)/shard_map/ppermute | solution.py:495
  73.9 6.0 %collective-permute-start.20 = (bf16[24,1536]{1,0:T(8,128)(2,1)S(1)}, bf16[24,1536]{1,0:T(8,128)(2,1)S(1)}, u32[]{:S(2)}, u32[]{:S(2)}) collective-permute-start(bf16[24,1536]{1,0:T(8,128)(2,1)S(1)} %get-tuple-element.90), channel_id=1, source_target_pairs={{0,2},{1,3},{2,0},{3,1},{4,6},{5,7},{6,4},{7,5},{8,10},{9,11},{10,... | collective-permute-start | bytes 221192 | tf_op jit(solution)/shard_map/ppermute | solution.py:495

commit v5 on v4

--- a/solution.py
+++ b/solution.py
@@ -11,7 +11,7 @@
 HEAD_DIM = 128
 ROWS_STEP = 8
 MIB = 1 << 20
-VMEM_GATE_UP = 22
+VMEM_GATE_UP = 25
 
 epsilon = 1e-05
 
@@ -28,7 +28,7 @@
     lengths_ref, query_ref, new_ref, resid_ref, cache_ref, query_buf, output_buf, *sems = rest
     small_sem, cache_sem, extra_sem = sems
     rows = ROWS_STEP
-    blocks = query_ref.shape[0] // rows
+    blocks = query_ref.shape[0]
     cache_len = cache_ref.shape[2]
     stacked = group * rows
     factor = 1.0 / math.sqrt(HEAD_DIM)
@@ -56,11 +56,11 @@
         for b in range(blocks):
             query_buf[head, b] = jnp.concatenate(
                 [
-                    query_ref[pl.ds(b * rows, rows), pl.ds((head * group + g) * HEAD_DIM, HEAD_DIM)]
+                    query_ref[b, :, pl.ds((head * group + g) * HEAD_DIM, HEAD_DIM)].astype(jnp.float32)
                     for g in range(group)
                 ],
                 axis=0,
-            )
+            ).astype(jnp.bfloat16)
     row_of = lax.broadcasted_iota(jnp.int32, (stacked, 1), 0) % rows
 
     def lanes_of(head):
@@ -125,9 +125,10 @@
                 [output_buf[head, b, pl.ds(g * rows, rows)] for b in range(blocks)], axis=0
             ).astype(jnp.bfloat16)
             attended_ref[:, columns] = piece
-            hidden_ref[:, columns] = (
-                resid_ref[:, columns].astype(jnp.float32) + piece.astype(jnp.float32)
-            ).astype(jnp.bfloat16)
+            resid = jnp.concatenate(
+                [resid_ref[b, :, columns].astype(jnp.float32) for b in range(blocks)], axis=0
+            )
+            hidden_ref[:, columns] = (resid + piece.astype(jnp.float32)).astype(jnp.bfloat16)
     for copy in later:
         copy.wait()
 
@@ -141,6 +142,7 @@
     stacked = group * ROWS_STEP
     hbm = pl.BlockSpec(memory_space=pltpu.HBM)
     vmem = pl.BlockSpec(memory_space=pltpu.VMEM)
+    queries, resid_in = (a.reshape(blocks, ROWS_STEP, part_cols) for a in (queries, resid_in))
     far = [pin(a, pltpu.HBM) for a in (lengths, queries, new_kv, resid_in, cache, *extra)]
     return pl.pallas_call(
         functools.partial(attend_kernel, extras=len(extra), kv_local=kv_local, group=group),
@@ -400,7 +402,7 @@
     held, width, ff = w_gate.shape
     tokens = sum(parts[0].shape[0] for parts in pieces)
     nb = largest_divisor(ff, (1024, 512, 256, 128))
-    depth, cuts = 4, 4
+    depth, cuts = 5, 4
     vmem = pl.BlockSpec(memory_space=pltpu.VMEM)
     hbm = pl.BlockSpec(memory_space=pltpu.HBM)
     near = [pin(a, pltpu.VMEM) for a in (gate_ready, up_ready, *(part for parts in pieces for part in parts))]

time: 80.7 us -> 80.6 us (level)
  no operation moved by 1% of the time
where the time goes in v5:
time: 80.6 us; the launch traced here: 80.4 us
  Pallas kernels  37.3 us (46%)
  starting transfers between devices  21.9 us (27%)
  waiting for transfers between devices  19.7 us (24%)
  other arithmetic  1.24 us (2%)
    ppermute x22, starting transfers between devices, swap(): return lax.ppermute(array, axis, [(i, i ^ offset) for i in range(size)])  21.9 us
    ppermute x22, waiting for transfers between devices, swap(): return lax.ppermute(array, axis, [(i, i ^ offset) for i in range(size)])  19.7 us
    pallas_call x3, Pallas kernels, fetch(): pl.pallas_call(functools.partial(fetch_kernel, jobs=[([span[:2] for span...  13.2 us
    pallas_call x1, Pallas kernels, gate_up(): pl.pallas_call(functools.partial(gate_up_kernel, layout=tuple((len(parts)...  12.1 us
    pallas_call x2, Pallas kernels, down(): pl.pallas_call(functools.partial(down_kernel, count=len(weights), nb=part...  5.82 us
    pallas_call x1, Pallas kernels, attend(): pl.pallas_call(functools.partial(attend_kernel, extras=len(extra), kv_loc...  5.56 us
  transfers between devices with their start and end apart: 22, of which 12 were waited for; matrix products, arithmetic and copies ran while one was open for 0% of the time, Pallas kernels for 18%

profile of v5, /device:TPU:0, one launch (start us, length us, event | category | flops | bytes accessed | tf_op | source)
XLA Modules:
  0.0 80.4 jit_solution(12927612732628998732)
XLA Ops:
  0.0 5.6 %attend.1 = (bf16[24,1536]{1,0:T(8,128)(2,1)S(1)}, bf16[24,1536]{1,0:T(8,128)(2,1)S(1)}, f32[1,6144]{1,0:T(1,128)S(1)}, f32[8,6144]{1,0:T(8,128)S(1)}, s32[2,24]{1,0:T(2,128)S(1)}) custom-call(s32[24]{0:T(128)} %lengths_hbm.1, bf16[3,8,1536]{2,1,0:T(8,128)(2,1)} %bitcast.7, bf16[24,2,256]{2,1,0:T(2,128)(2,1)} %new_hbm.1, bf16[3,8,1536]{2,1,0:T(8,128)(2,1)} %bitcast.5, ...), custom_call_target="tpu_custom_call" | custom-call | bytes 6291456 | tf_op jit(solution)/shard_map/attend/pallas_call | solution.py:147
  5.6 5.1 %collective-permute-start.2 = (bf16[24,1536]{1,0:T(8,128)(2,1)S(1)}, bf16[24,1536]{1,0:T(8,128)(2,1)S(1)}, u32[]{:S(2)}, u32[]{:S(2)}) collective-permute-start(bf16[24,1536]{1,0:T(8,128)(2,1)S(1)} %get-tuple-element.48.after_ref.earlier_ref.rest_0_), channel_id=1, source_target_pairs={{0,3},{1,2},{2,1},{3,0},{4,7},{5,6},{6,5},{7,4},{8,11},{9,10},{10,... | collective-permute-start | bytes 221192 | tf_op jit(solution)/shard_map/ppermute | solution.py:497
  10.7 0.0 collective-permute-start.1
  10.7 0.6 collective-permute-start
  11.3 4.7 %fetch.3 = (bf16[6144,1024]{1,0:T(8,128)(2,1)S(1)}, f32[8,128]{1,0:T(8,128)S(1)}) custom-call(bf16[24,1536]{1,0:T(8,128)(2,1)S(1)} %get-tuple-element.48.after_ref.earlier_ref.rest_0_, bf16[24,1536]{1,0:T(8,128)(2,1)S(1)} %get-tuple-element.48.after_ref.earlier_ref.rest_0_, bf16[2,6144,1024]{2,1,0:T(8,128)(2,1)} %gate_hbm.1), custom_call_target="tpu_custom_call" | custom-call | bytes 12582912 | tf_op jit(solution)/shard_map/fetch/pallas_call | solution.py:213
  16.0 0.0 collective-permute-done.2.rest_3_
  16.0 0.9 %collective-permute-done.1.rest_2_ = bf16[24,1536]{1,0:T(8,128)(2,1)S(1)} collective-permute-done((bf16[24,1536]{1,0:T(8,128)(2,1)S(1)}, bf16[24,1536]{1,0:T(8,128)(2,1)S(1)}, u32[]{:S(2)}, u32[]{:S(2)}) %collective-permute-start.1) | collective-permute-done | bytes 73760 | tf_op jit(solution)/shard_map/ppermute | solution.py:497
  16.9 0.0 collective-permute-done.rest_1_
  16.9 0.6 norm.1.after_ref.rest_0_
  17.5 1.6 %collective-permute-start.4 = (bf16[24,6272]{1,0:T(8,128)(2,1)S(1)}, bf16[24,6272]{1,0:T(8,128)(2,1)S(1)}, u32[]{:S(2)}, u32[]{:S(2)}) collective-permute-start(bf16[24,6272]{1,0:T(8,128)(2,1)S(1)} %norm.1.after_ref.rest_0_), channel_id=1, source_target_pairs={{0,8},{4,12},{8,0},{12,4},{1,9},{5,13},{9,1},{13,5},{2,10},{6,14},... | collective-permute-start | bytes 903176 | tf_op jit(solution)/shard_map/ppermute | solution.py:497
  19.1 1.5 %collective-permute-start.3 = (bf16[24,6272]{1,0:T(8,128)(2,1)S(1)}, bf16[24,6272]{1,0:T(8,128)(2,1)S(1)}, u32[]{:S(2)}, u32[]{:S(2)}) collective-permute-start(bf16[24,6272]{1,0:T(8,128)(2,1)S(1)} %norm.1.after_ref.rest_0_), channel_id=1, source_target_pairs={{0,4},{4,0},{8,12},{12,8},{1,5},{5,1},{9,13},{13,9},{2,6},{6,2},{1... | collective-permute-start | bytes 903176 | tf_op jit(solution)/shard_map/ppermute | solution.py:497
  20.6 5.4 %fetch.4 = (bf16[1024,4608]{1,0:T(8,128)(2,1)S(1)}, bf16[256,4608]{1,0:T(8,128)(2,1)S(1)}, bf16[1536,1024]{1,0:T(8,128)(2,1)S(1)}, f32[8,128]{1,0:T(8,128)S(1)}) custom-call(bf16[24,6272]{1,0:T(8,128)(2,1)S(1)} %norm.1.after_ref.rest_0_, f32[8,128]{1,0:T(8,128)S(1)} %get-tuple-element.52.earlier_ref, bf16[2,1024,6144]{2,1,0:T(8,128)(2,1)} %rest_3_.1, ...), custom_call_target="tpu_custom_call" | custom-call | bytes 14942208 | tf_op jit(solution)/shard_map/fetch/pallas_call | solution.py:213
  25.9 0.1 collective-permute-done.4.first_ref.rest_2_
  26.0 1.4 %collective-permute-done.3.second_ref.rest_1_ = bf16[24,6272]{1,0:T(8,128)(2,1)S(1)} collective-permute-done((bf16[24,6272]{1,0:T(8,128)(2,1)S(1)}, bf16[24,6272]{1,0:T(8,128)(2,1)S(1)}, u32[]{:S(2)}, u32[]{:S(2)}) %collective-permute-start.3) | collective-permute-done | bytes 301088 | tf_op jit(solution)/shard_map/ppermute | solution.py:497
  27.5 0.4 collective-permute-start.6
  27.9 1.6 %collective-permute-start.5 = (bf16[24,3072]{1,0:T(8,128)(2,1)S(1)}, bf16[24,3072]{1,0:T(8,128)(2,1)S(1)}, u32[]{:S(2)}, u32[]{:S(2)}) collective-permute-start(bf16[24,3072]{1,0:T(8,128)(2,1)S(1)} %get-tuple-element.56.after_ref), channel_id=1, source_target_pairs={{0,4},{4,0},{8,12},{12,8},{1,5},{5,1},{9,13},{13,9},{2,6},{6,2},{1... | collective-permute-start | bytes 442376 | tf_op jit(solution)/shard_map/ppermute | solution.py:497
  29.6 0.0 collective-permute-start.7
  29.6 0.5 collective-permute-start.9
  30.1 0.0 collective-permute-start.8
  30.1 3.1 %fetch.5 = (bf16[768,4608]{1,0:T(8,128)(2,1)S(1)}, f32[8,128]{1,0:T(8,128)S(1)}) custom-call(bf16[24,3072]{1,0:T(8,128)(2,1)S(1)} %get-tuple-element.56.after_ref, f32[8,128]{1,0:T(8,128)S(1)} %get-tuple-element.58.earlier_ref, bf16[2,1024,6144]{2,1,0:T(8,128)(2,1)} %rest_3_.1), custom_call_target="tpu_custom_call" | custom-call | bytes 7077888 | tf_op jit(solution)/shard_map/fetch/pallas_call | solution.py:213
  33.2 0.0 collective-permute-done.5.rest_3_
  33.2 0.0 collective-permute-done.6.rest_4_
  33.2 0.6 collective-permute-start.11
  33.8 0.1 collective-permute-start.10
  33.9 0.0 collective-permute-done.7.rest_5_
  33.9 0.0 collective-permute-done.9.rest_7_
  33.9 0.0 collective-permute-done.8.rest_6_
  33.9 1.3 %collective-permute-done.10.rest_8_ = bf16[24,3072]{1,0:T(8,128)(2,1)S(1)} collective-permute-done((bf16[24,3072]{1,0:T(8,128)(2,1)S(1)}, bf16[24,3072]{1,0:T(8,128)(2,1)S(1)}, u32[]{:S(2)}, u32[]{:S(2)}) %collective-permute-start.10) | collective-permute-done | bytes 147488 | tf_op jit(solution)/shard_map/ppermute | solution.py:497
  35.2 0.0 collective-permute-done.11.rest_9_
  35.2 12.1 %gate_up.1.act_ref = bf16[192,2048]{1,0:T(8,128)(2,1)S(1)} custom-call(bf16[2,6144,1024]{2,1,0:T(8,128)(2,1)} %gate_hbm.1, bf16[2,6144,1024]{2,1,0:T(8,128)(2,1)} %up_hbm.1, f32[8,128]{1,0:T(8,128)S(1)} %get-tuple-element.60.token_ref, bf16[6144,1024]{1,0:T(8,128)(2,1)S(1)} %get-tuple-element.61.gate_ref, bf16[1536,1024]{1,0:T(8,128)(2,1)S(1)} %get-tuple-element.62.up_ref, ...), custom_call_target="tpu_custom_call" | custom-call | flops 9663676416 | bytes 50331648 | tf_op jit(solution)/shard_map/gate_up/pallas_call | solution.py:409
  47.4 4.4 %down.2 = (bf16[96,4608]{1,0:T(8,128)(2,1)S(1)}, bf16[96,4608]{1,0:T(8,128)(2,1)S(1)}, bf16[1024,1536]{1,0:T(8,128)(2,1)S(1)}, bf16[1024,1536]{1,0:T(8,128)(2,1)S(1)}) custom-call(bf16[192,2048]{1,0:T(8,128)(2,1)S(1)} %gate_up.1.act_ref, bf16[1024,4608]{1,0:T(8,128)(2,1)S(1)} %get-tuple-element.66.rest_0_, bf16[256,4608]{1,0:T(8,128)(2,1)S(1)} %get-tuple-element.67.rest_1_, ...), custom_call_target="tpu_custom_call" | custom-call | flops 3623878656 | tf_op jit(solution)/shard_map/down/pallas_call | solution.py:472
  51.8 0.3 collective-permute-start.12
  52.1 1.4 %down.3 = (bf16[96,1536]{1,0:T(8,128)(2,1)S(1)}, bf16[96,1536]{1,0:T(8,128)(2,1)S(1)}) custom-call(bf16[192,2048]{1,0:T(8,128)(2,1)S(1)} %gate_up.1.act_ref, bf16[1024,1536]{1,0:T(8,128)(2,1)S(1)} %get-tuple-element.72.rest_0_, bf16[1024,1536]{1,0:T(8,128)(2,1)S(1)} %get-tuple-element.73.rest_1_), custom_call_target="tpu_custom_call" | custom-call | flops 1207959552 | tf_op jit(solution)/shard_map/down/pallas_call | solution.py:472
  53.5 0.0 copy-start
  53.5 0.3 collective-permute-start.13
  53.8 0.4 collective-permute-done.12
  54.3 0.2 convert_add_fusion.2
  54.5 1.2 %collective-permute-start.14 = (bf16[24,3072]{1,0:T(8,128)(2,1)S(1)}, bf16[24,3072]{1,0:T(8,128)(2,1)S(1)}, u32[]{:S(2)}, u32[]{:S(2)}) collective-permute-start(bf16[24,3072]{1,0:T(8,128)(2,1)S(1)} %slice.117), channel_id=1, source_target_pairs={{0,4},{4,0},{8,12},{12,8},{1,5},{5,1},{9,13},{13,9},{2,6},{6,2},{1... | collective-permute-start | bytes 442376 | tf_op jit(solution)/shard_map/ppermute | solution.py:497
  55.7 0.0 collective-permute-done.13
  55.7 1.6 %collective-permute-start.16 = (bf16[24,1536]{1,0:T(8,128)(2,1)S(1)}, bf16[24,1536]{1,0:T(8,128)(2,1)S(1)}, u32[]{:S(2)}, u32[]{:S(2)}) collective-permute-start(bf16[24,1536]{1,0:T(8,128)(2,1)S(1)} %add_convert_fusion.3), channel_id=1, source_target_pairs={{0,8},{4,12},{8,0},{12,4},{1,9},{5,13},{9,1},{13,5},{2,10},{6,14},... | collective-permute-start | bytes 221192 | tf_op jit(solution)/shard_map/ppermute | solution.py:497
  57.3 0.5 collective-permute-start.15
  57.8 2.8 %collective-permute-done.16 = bf16[24,1536]{1,0:T(8,128)(2,1)S(1)} collective-permute-done((bf16[24,1536]{1,0:T(8,128)(2,1)S(1)}, bf16[24,1536]{1,0:T(8,128)(2,1)S(1)}, u32[]{:S(2)}, u32[]{:S(2)}) %collective-permute-start.16) | collective-permute-done | bytes 73760 | tf_op jit(solution)/shard_map/ppermute | solution.py:497
  60.7 1.0 %collective-permute-done.15 = bf16[24,1536]{1,0:T(8,128)(2,1)S(1)} collective-permute-done((bf16[24,1536]{1,0:T(8,128)(2,1)S(1)}, bf16[24,1536]{1,0:T(8,128)(2,1)S(1)}, u32[]{:S(2)}, u32[]{:S(2)}) %collective-permute-start.15) | collective-permute-done | bytes 73760 | tf_op jit(solution)/shard_map/ppermute | solution.py:497
  61.7 0.0 collective-permute-done.14
  61.8 0.1 convert_add_fusion.3
  61.9 1.0 %collective-permute-start.17 = (bf16[24,6144]{1,0:T(8,128)(2,1)S(1)}, bf16[24,6144]{1,0:T(8,128)(2,1)S(1)}, u32[]{:S(2)}, u32[]{:S(2)}) collective-permute-start(bf16[24,6144]{1,0:T(8,128)(2,1)S(1)} %pad_maximum_fusion), channel_id=1, source_target_pairs={{0,4},{4,0},{8,12},{12,8},{1,5},{5,1},{9,13},{13,9},{2,6},{6,2},{1... | collective-permute-start | bytes 884744 | tf_op jit(solution)/shard_map/ppermute | solution.py:497
  62.9 1.4 %collective-permute-start.18 = (bf16[24,6144]{1,0:T(8,128)(2,1)S(1)}, bf16[24,6144]{1,0:T(8,128)(2,1)S(1)}, u32[]{:S(2)}, u32[]{:S(2)}) collective-permute-start(bf16[24,6144]{1,0:T(8,128)(2,1)S(1)} %pad_maximum_fusion.1), channel_id=1, source_target_pairs={{0,8},{4,12},{8,0},{12,4},{1,9},{5,13},{9,1},{13,5},{2,10},{6,14},... | collective-permute-start | bytes 884744 | tf_op jit(solution)/shard_map/ppermute | solution.py:497
  64.3 6.0 %collective-permute-done.17 = bf16[24,6144]{1,0:T(8,128)(2,1)S(1)} collective-permute-done((bf16[24,6144]{1,0:T(8,128)(2,1)S(1)}, bf16[24,6144]{1,0:T(8,128)(2,1)S(1)}, u32[]{:S(2)}, u32[]{:S(2)}) %collective-permute-start.17) | collective-permute-done | bytes 294944 | tf_op jit(solution)/shard_map/ppermute | solution.py:497
  70.3 0.7 collective-permute-done.18
  71.0 0.1 fusion.7
  71.1 0.2 collective-permute-start.19
  71.3 2.4 %collective-permute-start.21 = (bf16[24,1536]{1,0:T(8,128)(2,1)S(1)}, bf16[24,1536]{1,0:T(8,128)(2,1)S(1)}, u32[]{:S(2)}, u32[]{:S(2)}) collective-permute-start(bf16[24,1536]{1,0:T(8,128)(2,1)S(1)} %get-tuple-element.89), channel_id=1, source_target_pairs={{0,3},{1,2},{2,1},{3,0},{4,7},{5,6},{6,5},{7,4},{8,11},{9,10},{10,... | collective-permute-start | bytes 221192 | tf_op jit(solution)/shard_map/ppermute | solution.py:497
  73.7 1.0 %collective-permute-start.20 = (bf16[24,1536]{1,0:T(8,128)(2,1)S(1)}, bf16[24,1536]{1,0:T(8,128)(2,1)S(1)}, u32[]{:S(2)}, u32[]{:S(2)}) collective-permute-start(bf16[24,1536]{1,0:T(8,128)(2,1)S(1)} %get-tuple-element.90), channel_id=1, source_target_pairs={{0,2},{1,3},{2,0},{3,1},{4,6},{5,7},{6,4},{7,5},{8,10},{9,11},{10,... | collective-permute-start | bytes 221192 | tf_op jit(solution)/shard_map/ppermute | solution.py:497
  74.6 1.6 %collective-permute-done.19 = bf16[24,1536]{1,0:T(8,128)(2,1)S(1)} collective-permute-done((bf16[24,1536]{1,0:T(8,128)(2,1)S(1)}, bf16[24,1536]{1,0:T(8,128)(2,1)S(1)}, u32[]{:S(2)}, u32[]{:S(2)}) %collective-permute-start.19) | collective-permute-done | bytes 73760 | tf_op jit(solution)/shard_map/ppermute | solution.py:497
  76.2 1.3 %collective-permute-done.21 = bf16[24,1536]{1,0:T(8,128)(2,1)S(1)} collective-permute-done((bf16[24,1536]{1,0:T(8,128)(2,1)S(1)}, bf16[24,1536]{1,0:T(8,128)(2,1)S(1)}, u32[]{:S(2)}, u32[]{:S(2)}) %collective-permute-start.21) | collective-permute-done | bytes 73760 | tf_op jit(solution)/shard_map/ppermute | solution.py:497
  77.5 2.2 %collective-permute-done.20 = bf16[24,1536]{1,0:T(8,128)(2,1)S(1)} collective-permute-done((bf16[24,1536]{1,0:T(8,128)(2,1)S(1)}, bf16[24,1536]{1,0:T(8,128)(2,1)S(1)}, u32[]{:S(2)}, u32[]{:S(2)}) %collective-permute-start.20) | collective-permute-done | bytes 73760 | tf_op jit(solution)/shard_map/ppermute | solution.py:497
  79.7 0.0 copy-done
  79.7 0.7 fusion.5
  (14 shorter events, 0.2 us)
Async XLA Ops:
  5.6 10.5 %collective-permute-start.2 = (bf16[24,1536]{1,0:T(8,128)(2,1)S(1)}, bf16[24,1536]{1,0:T(8,128)(2,1)S(1)}, u32[]{:S(2)}, u32[]{:S(2)}) collective-permute-start(bf16[24,1536]{1,0:T(8,128)(2,1)S(1)} %get-tuple-element.48.after_ref.earlier_ref.rest_0_), channel_id=1, source_target_pairs={{0,3},{1,2},{2,1},{3,0},{4,7},{5,6},{6,5},{7,4},{8,11},{9,10},{10,... | collective-permute-start | bytes 221192 | tf_op jit(solution)/shard_map/ppermute | solution.py:497
  10.7 6.2 %collective-permute-start.1 = (bf16[24,1536]{1,0:T(8,128)(2,1)S(1)}, bf16[24,1536]{1,0:T(8,128)(2,1)S(1)}, u32[]{:S(2)}, u32[]{:S(2)}) collective-permute-start(bf16[24,1536]{1,0:T(8,128)(2,1)S(1)} %get-tuple-element.48.after_ref.earlier_ref.rest_0_), channel_id=1, source_target_pairs={{0,2},{1,3},{2,0},{3,1},{4,6},{5,7},{6,4},{7,5},{8,10},{9,11},{10,... | collective-permute-start | bytes 221192 | tf_op jit(solution)/shard_map/ppermute | solution.py:497
  10.7 6.2 %collective-permute-start = (bf16[24,1536]{1,0:T(8,128)(2,1)S(1)}, bf16[24,1536]{1,0:T(8,128)(2,1)S(1)}, u32[]{:S(2)}, u32[]{:S(2)}) collective-permute-start(bf16[24,1536]{1,0:T(8,128)(2,1)S(1)} %get-tuple-element.48.after_ref.earlier_ref.rest_0_), channel_id=1, source_target_pairs={{0,1},{1,0},{2,3},{3,2},{4,5},{5,4},{6,7},{7,6},{8,9},{9,8},{10,11... | collective-permute-start | bytes 221192 | tf_op jit(solution)/shard_map/ppermute | solution.py:497
  17.5 8.6 %collective-permute-start.4 = (bf16[24,6272]{1,0:T(8,128)(2,1)S(1)}, bf16[24,6272]{1,0:T(8,128)(2,1)S(1)}, u32[]{:S(2)}, u32[]{:S(2)}) collective-permute-start(bf16[24,6272]{1,0:T(8,128)(2,1)S(1)} %norm.1.after_ref.rest_0_), channel_id=1, source_target_pairs={{0,8},{4,12},{8,0},{12,4},{1,9},{5,13},{9,1},{13,5},{2,10},{6,14},... | collective-permute-start | bytes 903176 | tf_op jit(solution)/shard_map/ppermute | solution.py:497
  19.1 8.4 %collective-permute-start.3 = (bf16[24,6272]{1,0:T(8,128)(2,1)S(1)}, bf16[24,6272]{1,0:T(8,128)(2,1)S(1)}, u32[]{:S(2)}, u32[]{:S(2)}) collective-permute-start(bf16[24,6272]{1,0:T(8,128)(2,1)S(1)} %norm.1.after_ref.rest_0_), channel_id=1, source_target_pairs={{0,4},{4,0},{8,12},{12,8},{1,5},{5,1},{9,13},{13,9},{2,6},{6,2},{1... | collective-permute-start | bytes 903176 | tf_op jit(solution)/shard_map/ppermute | solution.py:497
  27.5 5.7 %collective-permute-start.6 = (bf16[24,3200]{1,0:T(8,128)(2,1)S(1)}, bf16[24,3200]{1,0:T(8,128)(2,1)S(1)}, u32[]{:S(2)}, u32[]{:S(2)}) collective-permute-start(bf16[24,3200]{1,0:T(8,128)(2,1)S(1)} %get-tuple-element.57), channel_id=1, source_target_pairs={{0,8},{4,12},{8,0},{12,4},{1,9},{5,13},{9,1},{13,5},{2,10},{6,14},... | collective-permute-start | bytes 460808 | tf_op jit(solution)/shard_map/ppermute | solution.py:497
  27.9 5.3 %collective-permute-start.5 = (bf16[24,3072]{1,0:T(8,128)(2,1)S(1)}, bf16[24,3072]{1,0:T(8,128)(2,1)S(1)}, u32[]{:S(2)}, u32[]{:S(2)}) collective-permute-start(bf16[24,3072]{1,0:T(8,128)(2,1)S(1)} %get-tuple-element.56.after_ref), channel_id=1, source_target_pairs={{0,4},{4,0},{8,12},{12,8},{1,5},{5,1},{9,13},{13,9},{2,6},{6,2},{1... | collective-permute-start | bytes 442376 | tf_op jit(solution)/shard_map/ppermute | solution.py:497
  29.6 4.3 %collective-permute-start.7 = (bf16[24,6272]{1,0:T(8,128)(2,1)S(1)}, bf16[24,6272]{1,0:T(8,128)(2,1)S(1)}, u32[]{:S(2)}, u32[]{:S(2)}) collective-permute-start(bf16[24,6272]{1,0:T(8,128)(2,1)S(1)} %norm.1.after_ref.rest_0_), channel_id=1, source_target_pairs={{0,16},{16,0},{1,17},{17,1},{2,18},{18,2},{3,19},{19,3},{4,20},{20... | collective-permute-start | bytes 903176 | tf_op jit(solution)/shard_map/ppermute | solution.py:497
  29.6 4.3 %collective-permute-start.9 = (bf16[24,6272]{1,0:T(8,128)(2,1)S(1)}, bf16[24,6272]{1,0:T(8,128)(2,1)S(1)}, u32[]{:S(2)}, u32[]{:S(2)}) collective-permute-start(bf16[24,6272]{1,0:T(8,128)(2,1)S(1)} %collective-permute-done.4.first_ref.rest_2_), channel_id=1, source_target_pairs={{0,16},{16,0},{1,17},{17,1},{2,18},{18,2},{3,19},{19,3},{4,20},{20... | collective-permute-start | bytes 903176 | tf_op jit(solution)/shard_map/ppermute | solution.py:497
  30.1 3.8 %collective-permute-start.8 = (bf16[24,6272]{1,0:T(8,128)(2,1)S(1)}, bf16[24,6272]{1,0:T(8,128)(2,1)S(1)}, u32[]{:S(2)}, u32[]{:S(2)}) collective-permute-start(bf16[24,6272]{1,0:T(8,128)(2,1)S(1)} %collective-permute-done.3.second_ref.rest_1_), channel_id=1, source_target_pairs={{0,16},{16,0},{1,17},{17,1},{2,18},{18,2},{3,19},{19,3},{4,20},{20... | collective-permute-start | bytes 903176 | tf_op jit(solution)/shard_map/ppermute | solution.py:497
  33.2 1.9 %collective-permute-start.11 = (bf16[24,3200]{1,0:T(8,128)(2,1)S(1)}, bf16[24,3200]{1,0:T(8,128)(2,1)S(1)}, u32[]{:S(2)}, u32[]{:S(2)}) collective-permute-start(bf16[24,3200]{1,0:T(8,128)(2,1)S(1)} %collective-permute-done.6.rest_4_), channel_id=1, source_target_pairs={{0,16},{16,0},{1,17},{17,1},{2,18},{18,2},{3,19},{19,3},{4,20},{20... | collective-permute-start | bytes 460808 | tf_op jit(solution)/shard_map/ppermute | solution.py:497
  33.8 1.4 %collective-permute-start.10 = (bf16[24,3072]{1,0:T(8,128)(2,1)S(1)}, bf16[24,3072]{1,0:T(8,128)(2,1)S(1)}, u32[]{:S(2)}, u32[]{:S(2)}) collective-permute-start(bf16[24,3072]{1,0:T(8,128)(2,1)S(1)} %collective-permute-done.5.rest_3_), channel_id=1, source_target_pairs={{0,16},{16,0},{1,17},{17,1},{2,18},{18,2},{3,19},{19,3},{4,20},{20... | collective-permute-start | bytes 442376 | tf_op jit(solution)/shard_map/ppermute | solution.py:497
  51.8 2.5 %collective-permute-start.12 = (bf16[96,4608]{1,0:T(8,128)(2,1)S(1)}, bf16[96,4608]{1,0:T(8,128)(2,1)S(1)}, u32[]{:S(2)}, u32[]{:S(2)}) collective-permute-start(bf16[96,4608]{1,0:T(8,128)(2,1)S(1)} %get-tuple-element.70), channel_id=1, source_target_pairs={{0,16},{16,0},{1,17},{17,1},{2,18},{18,2},{3,19},{19,3},{4,20},{20... | collective-permute-start | bytes 2654216 | tf_op jit(solution)/shard_map/ppermute | solution.py:497
  53.5 26.3 %copy-start = (bf16[24,1536]{1,0:T(8,128)(2,1)S(1)}, bf16[24,1536]{1,0:T(8,128)(2,1)}, u32[]{:S(2)}) copy-start(bf16[24,1536]{1,0:T(8,128)(2,1)} %param.11) | copy-start | bytes 221188
  53.5 2.2 %collective-permute-start.13 = (bf16[96,1536]{1,0:T(8,128)(2,1)S(1)}, bf16[96,1536]{1,0:T(8,128)(2,1)S(1)}, u32[]{:S(2)}, u32[]{:S(2)}) collective-permute-start(bf16[96,1536]{1,0:T(8,128)(2,1)S(1)} %get-tuple-element.75), channel_id=1, source_target_pairs={{0,16},{16,0},{1,17},{17,1},{2,18},{18,2},{3,19},{19,3},{4,20},{20... | collective-permute-start | bytes 884744 | tf_op jit(solution)/shard_map/ppermute | solution.py:497
  54.5 7.2 %collective-permute-start.14 = (bf16[24,3072]{1,0:T(8,128)(2,1)S(1)}, bf16[24,3072]{1,0:T(8,128)(2,1)S(1)}, u32[]{:S(2)}, u32[]{:S(2)}) collective-permute-start(bf16[24,3072]{1,0:T(8,128)(2,1)S(1)} %slice.117), channel_id=1, source_target_pairs={{0,4},{4,0},{8,12},{12,8},{1,5},{5,1},{9,13},{13,9},{2,6},{6,2},{1... | collective-permute-start | bytes 442376 | tf_op jit(solution)/shard_map/ppermute | solution.py:497
  55.7 4.9 %collective-permute-start.16 = (bf16[24,1536]{1,0:T(8,128)(2,1)S(1)}, bf16[24,1536]{1,0:T(8,128)(2,1)S(1)}, u32[]{:S(2)}, u32[]{:S(2)}) collective-permute-start(bf16[24,1536]{1,0:T(8,128)(2,1)S(1)} %add_convert_fusion.3), channel_id=1, source_target_pairs={{0,8},{4,12},{8,0},{12,4},{1,9},{5,13},{9,1},{13,5},{2,10},{6,14},... | collective-permute-start | bytes 221192 | tf_op jit(solution)/shard_map/ppermute | solution.py:497
  57.3 4.4 %collective-permute-start.15 = (bf16[24,1536]{1,0:T(8,128)(2,1)S(1)}, bf16[24,1536]{1,0:T(8,128)(2,1)S(1)}, u32[]{:S(2)}, u32[]{:S(2)}) collective-permute-start(bf16[24,1536]{1,0:T(8,128)(2,1)S(1)} %slice.118), channel_id=1, source_target_pairs={{0,8},{4,12},{8,0},{12,4},{1,9},{5,13},{9,1},{13,5},{2,10},{6,14},... | collective-permute-start | bytes 221192 | tf_op jit(solution)/shard_map/ppermute | solution.py:497
  61.9 8.3 %collective-permute-start.17 = (bf16[24,6144]{1,0:T(8,128)(2,1)S(1)}, bf16[24,6144]{1,0:T(8,128)(2,1)S(1)}, u32[]{:S(2)}, u32[]{:S(2)}) collective-permute-start(bf16[24,6144]{1,0:T(8,128)(2,1)S(1)} %pad_maximum_fusion), channel_id=1, source_target_pairs={{0,4},{4,0},{8,12},{12,8},{1,5},{5,1},{9,13},{13,9},{2,6},{6,2},{1... | collective-permute-start | bytes 884744 | tf_op jit(solution)/shard_map/ppermute | solution.py:497
  62.9 8.0 %collective-permute-start.18 = (bf16[24,6144]{1,0:T(8,128)(2,1)S(1)}, bf16[24,6144]{1,0:T(8,128)(2,1)S(1)}, u32[]{:S(2)}, u32[]{:S(2)}) collective-permute-start(bf16[24,6144]{1,0:T(8,128)(2,1)S(1)} %pad_maximum_fusion.1), channel_id=1, source_target_pairs={{0,8},{4,12},{8,0},{12,4},{1,9},{5,13},{9,1},{13,5},{2,10},{6,14},... | collective-permute-start | bytes 884744 | tf_op jit(solution)/shard_map/ppermute | solution.py:497
  71.1 5.1 %collective-permute-start.19 = (bf16[24,1536]{1,0:T(8,128)(2,1)S(1)}, bf16[24,1536]{1,0:T(8,128)(2,1)S(1)}, u32[]{:S(2)}, u32[]{:S(2)}) collective-permute-start(bf16[24,1536]{1,0:T(8,128)(2,1)S(1)} %get-tuple-element.88), channel_id=1, source_target_pairs={{0,1},{1,0},{2,3},{3,2},{4,5},{5,4},{6,7},{7,6},{8,9},{9,8},{10,11... | collective-permute-start | bytes 221192 | tf_op jit(solution)/shard_map/ppermute | solution.py:497
  71.3 6.2 %collective-permute-start.21 = (bf16[24,1536]{1,0:T(8,128)(2,1)S(1)}, bf16[24,1536]{1,0:T(8,128)(2,1)S(1)}, u32[]{:S(2)}, u32[]{:S(2)}) collective-permute-start(bf16[24,1536]{1,0:T(8,128)(2,1)S(1)} %get-tuple-element.89), channel_id=1, source_target_pairs={{0,3},{1,2},{2,1},{3,0},{4,7},{5,6},{6,5},{7,4},{8,11},{9,10},{10,... | collective-permute-start | bytes 221192 | tf_op jit(solution)/shard_map/ppermute | solution.py:497
  73.7 6.0 %collective-permute-start.20 = (bf16[24,1536]{1,0:T(8,128)(2,1)S(1)}, bf16[24,1536]{1,0:T(8,128)(2,1)S(1)}, u32[]{:S(2)}, u32[]{:S(2)}) collective-permute-start(bf16[24,1536]{1,0:T(8,128)(2,1)S(1)} %get-tuple-element.90), channel_id=1, source_target_pairs={{0,2},{1,3},{2,0},{3,1},{4,6},{5,7},{6,4},{7,5},{8,10},{9,11},{10,... | collective-permute-start | bytes 221192 | tf_op jit(solution)/shard_map/ppermute | solution.py:497

commit v6 on v5

--- a/solution.py
+++ b/solution.py
@@ -24,7 +24,7 @@
     lengths_hbm, query_hbm, new_hbm, resid_hbm, cache_hbm, *rest, extras, kv_local, group
 ):
     extra_hbm, rest = rest[:extras], rest[extras:]
-    (attended_ref, hidden_ref), extra_refs, rest = rest[:2], rest[2 : 2 + extras], rest[2 + extras :]
+    (whole_ref, hidden_ref), extra_refs, rest = rest[:2], rest[2 : 2 + extras], rest[2 + extras :]
     lengths_ref, query_ref, new_ref, resid_ref, cache_ref, query_buf, output_buf, *sems = rest
     small_sem, cache_sem, extra_sem = sems
     rows = ROWS_STEP
@@ -124,11 +124,12 @@
             piece = jnp.concatenate(
                 [output_buf[head, b, pl.ds(g * rows, rows)] for b in range(blocks)], axis=0
             ).astype(jnp.bfloat16)
-            attended_ref[:, columns] = piece
             resid = jnp.concatenate(
                 [resid_ref[b, :, columns].astype(jnp.float32) for b in range(blocks)], axis=0
             )
-            hidden_ref[:, columns] = (resid + piece.astype(jnp.float32)).astype(jnp.bfloat16)
+            hidden = resid + piece.astype(jnp.float32)
+            whole_ref[:, columns] = hidden
+            hidden_ref[:, columns] = hidden.astype(jnp.bfloat16)
     for copy in later:
         copy.wait()
 
@@ -148,7 +149,7 @@
         functools.partial(attend_kernel, extras=len(extra), kv_local=kv_local, group=group),
         in_specs=[hbm] * len(far),
         out_specs=[vmem] * (2 + len(extra)),
-        out_shape=[pltpu.VMEM((sequences, part_cols), jnp.bfloat16)] * 2
+        out_shape=[pltpu.VMEM((sequences, part_cols), dtype) for dtype in (jnp.float32, jnp.bfloat16)]
         + [pltpu.VMEM(array.shape, array.dtype) for array in extra],
         scratch_shapes=[
             pltpu.SMEM(lengths.shape, lengths.dtype),
@@ -300,7 +301,7 @@
 
 def gate_up_kernel(gate_hbm, up_hbm, token_ref, gate_ref, up_ref, *rest, layout, experts, blocks_held, depth, nb):
     pieces = sum(layout)
-    piece_refs, (act_ref, buf, rows_ref, sem) = rest[:pieces], rest[pieces:]
+    piece_refs, (act_ref, buf, rows_ref, early_ref, sem) = rest[:pieces], rest[pieces:]
     held, width, ff = gate_hbm.shape
     ready = 1
     blocks = ff // nb
@@ -351,8 +352,12 @@
                 at -= ref.shape[1]
         return jnp.concatenate(found, axis=0)
 
+    early = 0.0
     for k in range(width // deep):
-        rows_ref[:, pl.ds(k * deep, deep)] = gather(k * deep, deep).astype(jnp.bfloat16)
+        value = gather(k * deep, deep).astype(jnp.bfloat16)
+        rows_ref[:, pl.ds(k * deep, deep)] = value
+        early += jnp.dot(value, gate_ref[pl.ds(k * deep, deep), :], preferred_element_type=jnp.float32)
+    early_ref[...] = early
     shares = gather(width, 128)
     shares = shares[:, :experts] + shares[:, experts : 2 * experts]
     lane = lax.broadcasted_iota(jnp.int32, shares.shape, 1)
@@ -385,7 +390,7 @@
             columns = pl.ds(pl.multiple_of(n * nb, 128), nb)
             if e < ready:
                 i = first + n
-                gate = jnp.dot(rows_ref[...], gate_ref[:, columns], preferred_element_type=jnp.float32)
+                gate = early_ref[:, columns]
             else:
                 i = first + 2 * n + 1
                 gate = streamed(i - 1)
@@ -421,6 +426,7 @@
         scratch_shapes=[
             pltpu.VMEM((depth, width // cuts, nb), jnp.bfloat16),
             pltpu.VMEM((tokens, width), jnp.bfloat16),
+            pltpu.VMEM((tokens, ff), jnp.float32),
             pltpu.SemaphoreType.DMA((depth,)),
         ],
         cost_estimate=pl.CostEstimate(
@@ -505,7 +511,7 @@
     held = w_gate.shape[0]
     blocks_held = max(1, grps * held // router.shape[1])
     tie = lax.optimization_barrier
-    attended, hidden, gain, router_rows, ids = attend(
+    hidden_part, hidden, gain, router_rows, ids = attend(
         lengths, queries, new_kv, resid_in, cache, (norm_gain.reshape(1, -1), router.T, route_ids.T)
     )
 
@@ -571,7 +577,6 @@
     rows_sum = total([sums[0]] + [send(sums[d], "grp", d) for d in range(1, len(sums))])
     parts = [rows_sum[:, j * part_cols : (j + 1) * part_cols] for j in range(tps)]
     mixed = total([parts[0]] + [send(parts[j], "tp", j) for j in range(1, tps)])
-    hidden_part = resid_in.astype(jnp.float32) + attended.astype(jnp.float32)
     return (hidden_part + mixed).astype(jnp.bfloat16)
 
 

time: 80.6 us -> 80.6 us (level)
  no operation moved by 1% of the time
where the time goes in v6:
time: 80.6 us; the launch traced here: 80.4 us
  Pallas kernels  37.3 us (46%)
  starting transfers between devices  21.8 us (27%)
  waiting for transfers between devices  19.8 us (25%)
  other arithmetic  1.23 us (2%)
    ppermute x22, starting transfers between devices, swap(): return lax.ppermute(array, axis, [(i, i ^ offset) for i in range(size)])  21.8 us
    ppermute x22, waiting for transfers between devices, swap(): return lax.ppermute(array, axis, [(i, i ^ offset) for i in range(size)])  19.8 us
    pallas_call x3, Pallas kernels, fetch(): pl.pallas_call(functools.partial(fetch_kernel, jobs=[([span[:2] for span...  13.2 us
    pallas_call x1, Pallas kernels, gate_up(): pl.pallas_call(functools.partial(gate_up_kernel, layout=tuple((len(parts)...  12.2 us
    pallas_call x2, Pallas kernels, down(): pl.pallas_call(functools.partial(down_kernel, count=len(weights), nb=part...  5.82 us
    pallas_call x1, Pallas kernels, attend(): pl.pallas_call(functools.partial(attend_kernel, extras=len(extra), kv_loc...  5.56 us
  transfers between devices with their start and end apart: 22, of which 12 were waited for; matrix products, arithmetic and copies ran while one was open for 0% of the time, Pallas kernels for 18%

profile of v6, /device:TPU:0, one launch (start us, length us, event | category | flops | bytes accessed | tf_op | source)
XLA Modules:
  0.0 80.4 jit_solution(963512719581085189)
XLA Ops:
  0.0 5.6 %attend.1 = (f32[24,1536]{1,0:T(8,128)S(1)}, bf16[24,1536]{1,0:T(8,128)(2,1)S(1)}, f32[1,6144]{1,0:T(1,128)S(1)}, f32[8,6144]{1,0:T(8,128)S(1)}, s32[2,24]{1,0:T(2,128)S(1)}) custom-call(s32[24]{0:T(128)} %lengths_hbm.1, bf16[3,8,1536]{2,1,0:T(8,128)(2,1)} %bitcast.6, bf16[24,2,256]{2,1,0:T(2,128)(2,1)} %new_hbm.1, bf16[3,8,1536]{2,1,0:T(8,128)(2,1)} %bitcast.7, ...), custom_call_target="tpu_custom_call" | custom-call | bytes 6291456 | tf_op jit(solution)/shard_map/attend/pallas_call | solution.py:148
  5.6 5.1 %collective-permute-start.2 = (bf16[24,1536]{1,0:T(8,128)(2,1)S(1)}, bf16[24,1536]{1,0:T(8,128)(2,1)S(1)}, u32[]{:S(2)}, u32[]{:S(2)}) collective-permute-start(bf16[24,1536]{1,0:T(8,128)(2,1)S(1)} %get-tuple-element.48.after_ref.earlier_ref.rest_0_), channel_id=1, source_target_pairs={{0,3},{1,2},{2,1},{3,0},{4,7},{5,6},{6,5},{7,4},{8,11},{9,10},{10,... | collective-permute-start | bytes 221192 | tf_op jit(solution)/shard_map/ppermute | solution.py:503
  10.7 0.0 collective-permute-start.1
  10.7 0.6 collective-permute-start
  11.3 4.7 %fetch.3 = (bf16[6144,1024]{1,0:T(8,128)(2,1)S(1)}, f32[8,128]{1,0:T(8,128)S(1)}) custom-call(bf16[24,1536]{1,0:T(8,128)(2,1)S(1)} %get-tuple-element.48.after_ref.earlier_ref.rest_0_, bf16[24,1536]{1,0:T(8,128)(2,1)S(1)} %get-tuple-element.48.after_ref.earlier_ref.rest_0_, bf16[2,6144,1024]{2,1,0:T(8,128)(2,1)} %gate_hbm.1), custom_call_target="tpu_custom_call" | custom-call | bytes 12582912 | tf_op jit(solution)/shard_map/fetch/pallas_call | solution.py:214
  16.0 0.0 collective-permute-done.2.rest_3_
  16.0 0.9 %collective-permute-done.1.rest_2_ = bf16[24,1536]{1,0:T(8,128)(2,1)S(1)} collective-permute-done((bf16[24,1536]{1,0:T(8,128)(2,1)S(1)}, bf16[24,1536]{1,0:T(8,128)(2,1)S(1)}, u32[]{:S(2)}, u32[]{:S(2)}) %collective-permute-start.1) | collective-permute-done | bytes 73760 | tf_op jit(solution)/shard_map/ppermute | solution.py:503
  16.9 0.0 collective-permute-done.rest_1_
  16.9 0.6 norm.1.after_ref.rest_0_
  17.5 1.6 %collective-permute-start.4 = (bf16[24,6272]{1,0:T(8,128)(2,1)S(1)}, bf16[24,6272]{1,0:T(8,128)(2,1)S(1)}, u32[]{:S(2)}, u32[]{:S(2)}) collective-permute-start(bf16[24,6272]{1,0:T(8,128)(2,1)S(1)} %norm.1.after_ref.rest_0_), channel_id=1, source_target_pairs={{0,8},{4,12},{8,0},{12,4},{1,9},{5,13},{9,1},{13,5},{2,10},{6,14},... | collective-permute-start | bytes 903176 | tf_op jit(solution)/shard_map/ppermute | solution.py:503
  19.1 1.5 %collective-permute-start.3 = (bf16[24,6272]{1,0:T(8,128)(2,1)S(1)}, bf16[24,6272]{1,0:T(8,128)(2,1)S(1)}, u32[]{:S(2)}, u32[]{:S(2)}) collective-permute-start(bf16[24,6272]{1,0:T(8,128)(2,1)S(1)} %norm.1.after_ref.rest_0_), channel_id=1, source_target_pairs={{0,4},{4,0},{8,12},{12,8},{1,5},{5,1},{9,13},{13,9},{2,6},{6,2},{1... | collective-permute-start | bytes 903176 | tf_op jit(solution)/shard_map/ppermute | solution.py:503
  20.6 5.4 %fetch.4 = (bf16[1024,4608]{1,0:T(8,128)(2,1)S(1)}, bf16[256,4608]{1,0:T(8,128)(2,1)S(1)}, bf16[1536,1024]{1,0:T(8,128)(2,1)S(1)}, f32[8,128]{1,0:T(8,128)S(1)}) custom-call(bf16[24,6272]{1,0:T(8,128)(2,1)S(1)} %norm.1.after_ref.rest_0_, f32[8,128]{1,0:T(8,128)S(1)} %get-tuple-element.52.earlier_ref, bf16[2,1024,6144]{2,1,0:T(8,128)(2,1)} %rest_3_.1, ...), custom_call_target="tpu_custom_call" | custom-call | bytes 14942208 | tf_op jit(solution)/shard_map/fetch/pallas_call | solution.py:214
  25.9 0.1 collective-permute-done.4.first_ref.rest_2_
  26.0 1.4 %collective-permute-done.3.second_ref.rest_1_ = bf16[24,6272]{1,0:T(8,128)(2,1)S(1)} collective-permute-done((bf16[24,6272]{1,0:T(8,128)(2,1)S(1)}, bf16[24,6272]{1,0:T(8,128)(2,1)S(1)}, u32[]{:S(2)}, u32[]{:S(2)}) %collective-permute-start.3) | collective-permute-done | bytes 301088 | tf_op jit(solution)/shard_map/ppermute | solution.py:503
  27.5 0.4 collective-permute-start.6
  27.9 1.6 %collective-permute-start.5 = (bf16[24,3072]{1,0:T(8,128)(2,1)S(1)}, bf16[24,3072]{1,0:T(8,128)(2,1)S(1)}, u32[]{:S(2)}, u32[]{:S(2)}) collective-permute-start(bf16[24,3072]{1,0:T(8,128)(2,1)S(1)} %get-tuple-element.56.after_ref), channel_id=1, source_target_pairs={{0,4},{4,0},{8,12},{12,8},{1,5},{5,1},{9,13},{13,9},{2,6},{6,2},{1... | collective-permute-start | bytes 442376 | tf_op jit(solution)/shard_map/ppermute | solution.py:503
  29.6 0.0 collective-permute-start.7
  29.6 0.5 collective-permute-start.9
  30.1 0.0 collective-permute-start.8
  30.1 3.1 %fetch.5 = (bf16[768,4608]{1,0:T(8,128)(2,1)S(1)}, f32[8,128]{1,0:T(8,128)S(1)}) custom-call(bf16[24,3072]{1,0:T(8,128)(2,1)S(1)} %get-tuple-element.56.after_ref, f32[8,128]{1,0:T(8,128)S(1)} %get-tuple-element.58.earlier_ref, bf16[2,1024,6144]{2,1,0:T(8,128)(2,1)} %rest_3_.1), custom_call_target="tpu_custom_call" | custom-call | bytes 7077888 | tf_op jit(solution)/shard_map/fetch/pallas_call | solution.py:214
  33.2 0.0 collective-permute-done.5.rest_3_
  33.2 0.0 collective-permute-done.6.rest_4_
  33.3 0.6 collective-permute-start.11
  33.8 0.1 collective-permute-start.10
  33.9 0.0 collective-permute-done.7.rest_5_
  33.9 0.0 collective-permute-done.9.rest_7_
  33.9 0.0 collective-permute-done.8.rest_6_
  33.9 1.3 %collective-permute-done.10.rest_8_ = bf16[24,3072]{1,0:T(8,128)(2,1)S(1)} collective-permute-done((bf16[24,3072]{1,0:T(8,128)(2,1)S(1)}, bf16[24,3072]{1,0:T(8,128)(2,1)S(1)}, u32[]{:S(2)}, u32[]{:S(2)}) %collective-permute-start.10) | collective-permute-done | bytes 147488 | tf_op jit(solution)/shard_map/ppermute | solution.py:503
  35.2 0.0 collective-permute-done.11.rest_9_
  35.2 12.2 %gate_up.1.act_ref = bf16[192,2048]{1,0:T(8,128)(2,1)S(1)} custom-call(bf16[2,6144,1024]{2,1,0:T(8,128)(2,1)} %gate_hbm.1, bf16[2,6144,1024]{2,1,0:T(8,128)(2,1)} %up_hbm.1, f32[8,128]{1,0:T(8,128)S(1)} %get-tuple-element.60.token_ref, bf16[6144,1024]{1,0:T(8,128)(2,1)S(1)} %get-tuple-element.61.gate_ref, bf16[1536,1024]{1,0:T(8,128)(2,1)S(1)} %get-tuple-element.62.up_ref, ...), custom_call_target="tpu_custom_call" | custom-call | flops 9663676416 | bytes 50331648 | tf_op jit(solution)/shard_map/gate_up/pallas_call | solution.py:414
  47.4 4.4 %down.2 = (bf16[96,4608]{1,0:T(8,128)(2,1)S(1)}, bf16[96,4608]{1,0:T(8,128)(2,1)S(1)}, bf16[1024,1536]{1,0:T(8,128)(2,1)S(1)}, bf16[1024,1536]{1,0:T(8,128)(2,1)S(1)}) custom-call(bf16[192,2048]{1,0:T(8,128)(2,1)S(1)} %gate_up.1.act_ref, bf16[1024,4608]{1,0:T(8,128)(2,1)S(1)} %get-tuple-element.66.rest_0_, bf16[256,4608]{1,0:T(8,128)(2,1)S(1)} %get-tuple-element.67.rest_1_, ...), custom_call_target="tpu_custom_call" | custom-call | flops 3623878656 | tf_op jit(solution)/shard_map/down/pallas_call | solution.py:478
  51.8 0.3 collective-permute-start.12
  52.1 1.4 %down.3 = (bf16[96,1536]{1,0:T(8,128)(2,1)S(1)}, bf16[96,1536]{1,0:T(8,128)(2,1)S(1)}) custom-call(bf16[192,2048]{1,0:T(8,128)(2,1)S(1)} %gate_up.1.act_ref, bf16[1024,1536]{1,0:T(8,128)(2,1)S(1)} %get-tuple-element.72.rest_0_, bf16[1024,1536]{1,0:T(8,128)(2,1)S(1)} %get-tuple-element.73.rest_1_), custom_call_target="tpu_custom_call" | custom-call | flops 1207959552 | tf_op jit(solution)/shard_map/down/pallas_call | solution.py:478
  53.5 0.4 collective-permute-start.13
  53.8 0.4 collective-permute-done.12
  54.3 0.2 convert_add_fusion.2
  54.5 1.2 %collective-permute-start.14 = (bf16[24,3072]{1,0:T(8,128)(2,1)S(1)}, bf16[24,3072]{1,0:T(8,128)(2,1)S(1)}, u32[]{:S(2)}, u32[]{:S(2)}) collective-permute-start(bf16[24,3072]{1,0:T(8,128)(2,1)S(1)} %slice.117), channel_id=1, source_target_pairs={{0,4},{4,0},{8,12},{12,8},{1,5},{5,1},{9,13},{13,9},{2,6},{6,2},{1... | collective-permute-start | bytes 442376 | tf_op jit(solution)/shard_map/ppermute | solution.py:503
  55.7 0.0 collective-permute-done.13
  55.7 1.6 %collective-permute-start.16 = (bf16[24,1536]{1,0:T(8,128)(2,1)S(1)}, bf16[24,1536]{1,0:T(8,128)(2,1)S(1)}, u32[]{:S(2)}, u32[]{:S(2)}) collective-permute-start(bf16[24,1536]{1,0:T(8,128)(2,1)S(1)} %add_convert_fusion.3), channel_id=1, source_target_pairs={{0,8},{4,12},{8,0},{12,4},{1,9},{5,13},{9,1},{13,5},{2,10},{6,14},... | collective-permute-start | bytes 221192 | tf_op jit(solution)/shard_map/ppermute | solution.py:503
  57.3 0.5 collective-permute-start.15
  57.8 2.8 %collective-permute-done.16 = bf16[24,1536]{1,0:T(8,128)(2,1)S(1)} collective-permute-done((bf16[24,1536]{1,0:T(8,128)(2,1)S(1)}, bf16[24,1536]{1,0:T(8,128)(2,1)S(1)}, u32[]{:S(2)}, u32[]{:S(2)}) %collective-permute-start.16) | collective-permute-done | bytes 73760 | tf_op jit(solution)/shard_map/ppermute | solution.py:503
  60.7 1.0 %collective-permute-done.15 = bf16[24,1536]{1,0:T(8,128)(2,1)S(1)} collective-permute-done((bf16[24,1536]{1,0:T(8,128)(2,1)S(1)}, bf16[24,1536]{1,0:T(8,128)(2,1)S(1)}, u32[]{:S(2)}, u32[]{:S(2)}) %collective-permute-start.15) | collective-permute-done | bytes 73760 | tf_op jit(solution)/shard_map/ppermute | solution.py:503
  61.7 0.0 collective-permute-done.14
  61.8 0.1 convert_add_fusion.3
  61.9 1.0 %collective-permute-start.17 = (bf16[24,6144]{1,0:T(8,128)(2,1)S(1)}, bf16[24,6144]{1,0:T(8,128)(2,1)S(1)}, u32[]{:S(2)}, u32[]{:S(2)}) collective-permute-start(bf16[24,6144]{1,0:T(8,128)(2,1)S(1)} %pad_maximum_fusion), channel_id=1, source_target_pairs={{0,4},{4,0},{8,12},{12,8},{1,5},{5,1},{9,13},{13,9},{2,6},{6,2},{1... | collective-permute-start | bytes 884744 | tf_op jit(solution)/shard_map/ppermute | solution.py:503
  62.9 1.3 %collective-permute-start.18 = (bf16[24,6144]{1,0:T(8,128)(2,1)S(1)}, bf16[24,6144]{1,0:T(8,128)(2,1)S(1)}, u32[]{:S(2)}, u32[]{:S(2)}) collective-permute-start(bf16[24,6144]{1,0:T(8,128)(2,1)S(1)} %pad_maximum_fusion.1), channel_id=1, source_target_pairs={{0,8},{4,12},{8,0},{12,4},{1,9},{5,13},{9,1},{13,5},{2,10},{6,14},... | collective-permute-start | bytes 884744 | tf_op jit(solution)/shard_map/ppermute | solution.py:503
  64.3 6.0 %collective-permute-done.17 = bf16[24,6144]{1,0:T(8,128)(2,1)S(1)} collective-permute-done((bf16[24,6144]{1,0:T(8,128)(2,1)S(1)}, bf16[24,6144]{1,0:T(8,128)(2,1)S(1)}, u32[]{:S(2)}, u32[]{:S(2)}) %collective-permute-start.17) | collective-permute-done | bytes 294944 | tf_op jit(solution)/shard_map/ppermute | solution.py:503
  70.3 0.7 collective-permute-done.18
  71.0 0.1 fusion.7
  71.1 0.2 collective-permute-start.19
  71.3 2.4 %collective-permute-start.21 = (bf16[24,1536]{1,0:T(8,128)(2,1)S(1)}, bf16[24,1536]{1,0:T(8,128)(2,1)S(1)}, u32[]{:S(2)}, u32[]{:S(2)}) collective-permute-start(bf16[24,1536]{1,0:T(8,128)(2,1)S(1)} %get-tuple-element.89), channel_id=1, source_target_pairs={{0,3},{1,2},{2,1},{3,0},{4,7},{5,6},{6,5},{7,4},{8,11},{9,10},{10,... | collective-permute-start | bytes 221192 | tf_op jit(solution)/shard_map/ppermute | solution.py:503
  73.7 1.0 %collective-permute-start.20 = (bf16[24,1536]{1,0:T(8,128)(2,1)S(1)}, bf16[24,1536]{1,0:T(8,128)(2,1)S(1)}, u32[]{:S(2)}, u32[]{:S(2)}) collective-permute-start(bf16[24,1536]{1,0:T(8,128)(2,1)S(1)} %get-tuple-element.90), channel_id=1, source_target_pairs={{0,2},{1,3},{2,0},{3,1},{4,6},{5,7},{6,4},{7,5},{8,10},{9,11},{10,... | collective-permute-start | bytes 221192 | tf_op jit(solution)/shard_map/ppermute | solution.py:503
  74.7 1.6 %collective-permute-done.19 = bf16[24,1536]{1,0:T(8,128)(2,1)S(1)} collective-permute-done((bf16[24,1536]{1,0:T(8,128)(2,1)S(1)}, bf16[24,1536]{1,0:T(8,128)(2,1)S(1)}, u32[]{:S(2)}, u32[]{:S(2)}) %collective-permute-start.19) | collective-permute-done | bytes 73760 | tf_op jit(solution)/shard_map/ppermute | solution.py:503
  76.2 1.3 %collective-permute-done.21 = bf16[24,1536]{1,0:T(8,128)(2,1)S(1)} collective-permute-done((bf16[24,1536]{1,0:T(8,128)(2,1)S(1)}, bf16[24,1536]{1,0:T(8,128)(2,1)S(1)}, u32[]{:S(2)}, u32[]{:S(2)}) %collective-permute-start.21) | collective-permute-done | bytes 73760 | tf_op jit(solution)/shard_map/ppermute | solution.py:503
  77.5 2.2 %collective-permute-done.20 = bf16[24,1536]{1,0:T(8,128)(2,1)S(1)} collective-permute-done((bf16[24,1536]{1,0:T(8,128)(2,1)S(1)}, bf16[24,1536]{1,0:T(8,128)(2,1)S(1)}, u32[]{:S(2)}, u32[]{:S(2)}) %collective-permute-start.20) | collective-permute-done | bytes 73760 | tf_op jit(solution)/shard_map/ppermute | solution.py:503
  79.7 0.7 fusion.5
  (14 shorter events, 0.2 us)
Async XLA Ops:
  5.6 10.5 %collective-permute-start.2 = (bf16[24,1536]{1,0:T(8,128)(2,1)S(1)}, bf16[24,1536]{1,0:T(8,128)(2,1)S(1)}, u32[]{:S(2)}, u32[]{:S(2)}) collective-permute-start(bf16[24,1536]{1,0:T(8,128)(2,1)S(1)} %get-tuple-element.48.after_ref.earlier_ref.rest_0_), channel_id=1, source_target_pairs={{0,3},{1,2},{2,1},{3,0},{4,7},{5,6},{6,5},{7,4},{8,11},{9,10},{10,... | collective-permute-start | bytes 221192 | tf_op jit(solution)/shard_map/ppermute | solution.py:503
  10.7 6.2 %collective-permute-start.1 = (bf16[24,1536]{1,0:T(8,128)(2,1)S(1)}, bf16[24,1536]{1,0:T(8,128)(2,1)S(1)}, u32[]{:S(2)}, u32[]{:S(2)}) collective-permute-start(bf16[24,1536]{1,0:T(8,128)(2,1)S(1)} %get-tuple-element.48.after_ref.earlier_ref.rest_0_), channel_id=1, source_target_pairs={{0,2},{1,3},{2,0},{3,1},{4,6},{5,7},{6,4},{7,5},{8,10},{9,11},{10,... | collective-permute-start | bytes 221192 | tf_op jit(solution)/shard_map/ppermute | solution.py:503
  10.7 6.2 %collective-permute-start = (bf16[24,1536]{1,0:T(8,128)(2,1)S(1)}, bf16[24,1536]{1,0:T(8,128)(2,1)S(1)}, u32[]{:S(2)}, u32[]{:S(2)}) collective-permute-start(bf16[24,1536]{1,0:T(8,128)(2,1)S(1)} %get-tuple-element.48.after_ref.earlier_ref.rest_0_), channel_id=1, source_target_pairs={{0,1},{1,0},{2,3},{3,2},{4,5},{5,4},{6,7},{7,6},{8,9},{9,8},{10,11... | collective-permute-start | bytes 221192 | tf_op jit(solution)/shard_map/ppermute | solution.py:503
  17.5 8.6 %collective-permute-start.4 = (bf16[24,6272]{1,0:T(8,128)(2,1)S(1)}, bf16[24,6272]{1,0:T(8,128)(2,1)S(1)}, u32[]{:S(2)}, u32[]{:S(2)}) collective-permute-start(bf16[24,6272]{1,0:T(8,128)(2,1)S(1)} %norm.1.after_ref.rest_0_), channel_id=1, source_target_pairs={{0,8},{4,12},{8,0},{12,4},{1,9},{5,13},{9,1},{13,5},{2,10},{6,14},... | collective-permute-start | bytes 903176 | tf_op jit(solution)/shard_map/ppermute | solution.py:503
  19.1 8.4 %collective-permute-start.3 = (bf16[24,6272]{1,0:T(8,128)(2,1)S(1)}, bf16[24,6272]{1,0:T(8,128)(2,1)S(1)}, u32[]{:S(2)}, u32[]{:S(2)}) collective-permute-start(bf16[24,6272]{1,0:T(8,128)(2,1)S(1)} %norm.1.after_ref.rest_0_), channel_id=1, source_target_pairs={{0,4},{4,0},{8,12},{12,8},{1,5},{5,1},{9,13},{13,9},{2,6},{6,2},{1... | collective-permute-start | bytes 903176 | tf_op jit(solution)/shard_map/ppermute | solution.py:503
  27.5 5.7 %collective-permute-start.6 = (bf16[24,3200]{1,0:T(8,128)(2,1)S(1)}, bf16[24,3200]{1,0:T(8,128)(2,1)S(1)}, u32[]{:S(2)}, u32[]{:S(2)}) collective-permute-start(bf16[24,3200]{1,0:T(8,128)(2,1)S(1)} %get-tuple-element.57), channel_id=1, source_target_pairs={{0,8},{4,12},{8,0},{12,4},{1,9},{5,13},{9,1},{13,5},{2,10},{6,14},... | collective-permute-start | bytes 460808 | tf_op jit(solution)/shard_map/ppermute | solution.py:503
  27.9 5.3 %collective-permute-start.5 = (bf16[24,3072]{1,0:T(8,128)(2,1)S(1)}, bf16[24,3072]{1,0:T(8,128)(2,1)S(1)}, u32[]{:S(2)}, u32[]{:S(2)}) collective-permute-start(bf16[24,3072]{1,0:T(8,128)(2,1)S(1)} %get-tuple-element.56.after_ref), channel_id=1, source_target_pairs={{0,4},{4,0},{8,12},{12,8},{1,5},{5,1},{9,13},{13,9},{2,6},{6,2},{1... | collective-permute-start | bytes 442376 | tf_op jit(solution)/shard_map/ppermute | solution.py:503
  29.6 4.3 %collective-permute-start.7 = (bf16[24,6272]{1,0:T(8,128)(2,1)S(1)}, bf16[24,6272]{1,0:T(8,128)(2,1)S(1)}, u32[]{:S(2)}, u32[]{:S(2)}) collective-permute-start(bf16[24,6272]{1,0:T(8,128)(2,1)S(1)} %norm.1.after_ref.rest_0_), channel_id=1, source_target_pairs={{0,16},{16,0},{1,17},{17,1},{2,18},{18,2},{3,19},{19,3},{4,20},{20... | collective-permute-start | bytes 903176 | tf_op jit(solution)/shard_map/ppermute | solution.py:503
  29.6 4.3 %collective-permute-start.9 = (bf16[24,6272]{1,0:T(8,128)(2,1)S(1)}, bf16[24,6272]{1,0:T(8,128)(2,1)S(1)}, u32[]{:S(2)}, u32[]{:S(2)}) collective-permute-start(bf16[24,6272]{1,0:T(8,128)(2,1)S(1)} %collective-permute-done.4.first_ref.rest_2_), channel_id=1, source_target_pairs={{0,16},{16,0},{1,17},{17,1},{2,18},{18,2},{3,19},{19,3},{4,20},{20... | collective-permute-start | bytes 903176 | tf_op jit(solution)/shard_map/ppermute | solution.py:503
  30.1 3.8 %collective-permute-start.8 = (bf16[24,6272]{1,0:T(8,128)(2,1)S(1)}, bf16[24,6272]{1,0:T(8,128)(2,1)S(1)}, u32[]{:S(2)}, u32[]{:S(2)}) collective-permute-start(bf16[24,6272]{1,0:T(8,128)(2,1)S(1)} %collective-permute-done.3.second_ref.rest_1_), channel_id=1, source_target_pairs={{0,16},{16,0},{1,17},{17,1},{2,18},{18,2},{3,19},{19,3},{4,20},{20... | collective-permute-start | bytes 903176 | tf_op jit(solution)/shard_map/ppermute | solution.py:503
  33.3 1.9 %collective-permute-start.11 = (bf16[24,3200]{1,0:T(8,128)(2,1)S(1)}, bf16[24,3200]{1,0:T(8,128)(2,1)S(1)}, u32[]{:S(2)}, u32[]{:S(2)}) collective-permute-start(bf16[24,3200]{1,0:T(8,128)(2,1)S(1)} %collective-permute-done.6.rest_4_), channel_id=1, source_target_pairs={{0,16},{16,0},{1,17},{17,1},{2,18},{18,2},{3,19},{19,3},{4,20},{20... | collective-permute-start | bytes 460808 | tf_op jit(solution)/shard_map/ppermute | solution.py:503
  33.8 1.4 %collective-permute-start.10 = (bf16[24,3072]{1,0:T(8,128)(2,1)S(1)}, bf16[24,3072]{1,0:T(8,128)(2,1)S(1)}, u32[]{:S(2)}, u32[]{:S(2)}) collective-permute-start(bf16[24,3072]{1,0:T(8,128)(2,1)S(1)} %collective-permute-done.5.rest_3_), channel_id=1, source_target_pairs={{0,16},{16,0},{1,17},{17,1},{2,18},{18,2},{3,19},{19,3},{4,20},{20... | collective-permute-start | bytes 442376 | tf_op jit(solution)/shard_map/ppermute | solution.py:503
  51.8 2.5 %collective-permute-start.12 = (bf16[96,4608]{1,0:T(8,128)(2,1)S(1)}, bf16[96,4608]{1,0:T(8,128)(2,1)S(1)}, u32[]{:S(2)}, u32[]{:S(2)}) collective-permute-start(bf16[96,4608]{1,0:T(8,128)(2,1)S(1)} %get-tuple-element.70), channel_id=1, source_target_pairs={{0,16},{16,0},{1,17},{17,1},{2,18},{18,2},{3,19},{19,3},{4,20},{20... | collective-permute-start | bytes 2654216 | tf_op jit(solution)/shard_map/ppermute | solution.py:503
  53.5 2.2 %collective-permute-start.13 = (bf16[96,1536]{1,0:T(8,128)(2,1)S(1)}, bf16[96,1536]{1,0:T(8,128)(2,1)S(1)}, u32[]{:S(2)}, u32[]{:S(2)}) collective-permute-start(bf16[96,1536]{1,0:T(8,128)(2,1)S(1)} %get-tuple-element.75), channel_id=1, source_target_pairs={{0,16},{16,0},{1,17},{17,1},{2,18},{18,2},{3,19},{19,3},{4,20},{20... | collective-permute-start | bytes 884744 | tf_op jit(solution)/shard_map/ppermute | solution.py:503
  54.5 7.2 %collective-permute-start.14 = (bf16[24,3072]{1,0:T(8,128)(2,1)S(1)}, bf16[24,3072]{1,0:T(8,128)(2,1)S(1)}, u32[]{:S(2)}, u32[]{:S(2)}) collective-permute-start(bf16[24,3072]{1,0:T(8,128)(2,1)S(1)} %slice.117), channel_id=1, source_target_pairs={{0,4},{4,0},{8,12},{12,8},{1,5},{5,1},{9,13},{13,9},{2,6},{6,2},{1... | collective-permute-start | bytes 442376 | tf_op jit(solution)/shard_map/ppermute | solution.py:503
  55.7 4.9 %collective-permute-start.16 = (bf16[24,1536]{1,0:T(8,128)(2,1)S(1)}, bf16[24,1536]{1,0:T(8,128)(2,1)S(1)}, u32[]{:S(2)}, u32[]{:S(2)}) collective-permute-start(bf16[24,1536]{1,0:T(8,128)(2,1)S(1)} %add_convert_fusion.3), channel_id=1, source_target_pairs={{0,8},{4,12},{8,0},{12,4},{1,9},{5,13},{9,1},{13,5},{2,10},{6,14},... | collective-permute-start | bytes 221192 | tf_op jit(solution)/shard_map/ppermute | solution.py:503
  57.3 4.4 %collective-permute-start.15 = (bf16[24,1536]{1,0:T(8,128)(2,1)S(1)}, bf16[24,1536]{1,0:T(8,128)(2,1)S(1)}, u32[]{:S(2)}, u32[]{:S(2)}) collective-permute-start(bf16[24,1536]{1,0:T(8,128)(2,1)S(1)} %slice.118), channel_id=1, source_target_pairs={{0,8},{4,12},{8,0},{12,4},{1,9},{5,13},{9,1},{13,5},{2,10},{6,14},... | collective-permute-start | bytes 221192 | tf_op jit(solution)/shard_map/ppermute | solution.py:503
  61.9 8.3 %collective-permute-start.17 = (bf16[24,6144]{1,0:T(8,128)(2,1)S(1)}, bf16[24,6144]{1,0:T(8,128)(2,1)S(1)}, u32[]{:S(2)}, u32[]{:S(2)}) collective-permute-start(bf16[24,6144]{1,0:T(8,128)(2,1)S(1)} %pad_maximum_fusion), channel_id=1, source_target_pairs={{0,4},{4,0},{8,12},{12,8},{1,5},{5,1},{9,13},{13,9},{2,6},{6,2},{1... | collective-permute-start | bytes 884744 | tf_op jit(solution)/shard_map/ppermute | solution.py:503
  62.9 8.0 %collective-permute-start.18 = (bf16[24,6144]{1,0:T(8,128)(2,1)S(1)}, bf16[24,6144]{1,0:T(8,128)(2,1)S(1)}, u32[]{:S(2)}, u32[]{:S(2)}) collective-permute-start(bf16[24,6144]{1,0:T(8,128)(2,1)S(1)} %pad_maximum_fusion.1), channel_id=1, source_target_pairs={{0,8},{4,12},{8,0},{12,4},{1,9},{5,13},{9,1},{13,5},{2,10},{6,14},... | collective-permute-start | bytes 884744 | tf_op jit(solution)/shard_map/ppermute | solution.py:503
  71.1 5.1 %collective-permute-start.19 = (bf16[24,1536]{1,0:T(8,128)(2,1)S(1)}, bf16[24,1536]{1,0:T(8,128)(2,1)S(1)}, u32[]{:S(2)}, u32[]{:S(2)}) collective-permute-start(bf16[24,1536]{1,0:T(8,128)(2,1)S(1)} %get-tuple-element.88), channel_id=1, source_target_pairs={{0,1},{1,0},{2,3},{3,2},{4,5},{5,4},{6,7},{7,6},{8,9},{9,8},{10,11... | collective-permute-start | bytes 221192 | tf_op jit(solution)/shard_map/ppermute | solution.py:503
  71.3 6.2 %collective-permute-start.21 = (bf16[24,1536]{1,0:T(8,128)(2,1)S(1)}, bf16[24,1536]{1,0:T(8,128)(2,1)S(1)}, u32[]{:S(2)}, u32[]{:S(2)}) collective-permute-start(bf16[24,1536]{1,0:T(8,128)(2,1)S(1)} %get-tuple-element.89), channel_id=1, source_target_pairs={{0,3},{1,2},{2,1},{3,0},{4,7},{5,6},{6,5},{7,4},{8,11},{9,10},{10,... | collective-permute-start | bytes 221192 | tf_op jit(solution)/shard_map/ppermute | solution.py:503
  73.7 6.0 %collective-permute-start.20 = (bf16[24,1536]{1,0:T(8,128)(2,1)S(1)}, bf16[24,1536]{1,0:T(8,128)(2,1)S(1)}, u32[]{:S(2)}, u32[]{:S(2)}) collective-permute-start(bf16[24,1536]{1,0:T(8,128)(2,1)S(1)} %get-tuple-element.90), channel_id=1, source_target_pairs={{0,2},{1,3},{2,0},{3,1},{4,6},{5,7},{6,4},{7,5},{8,10},{9,11},{10,... | collective-permute-start | bytes 221192 | tf_op jit(solution)/shard_map/ppermute | solution.py:503
